TPU v7x, 32 devices: a whole 2x2x4 slice. The times are simulated.
32 devices in a mesh: dp: 4 (over y, x), seq: 8 (over z, core).
Axes of the slice: x: 2, y: 2, z: 4, core: 2. Of those that a mesh axis runs over, the one named last changes fastest.
Arguments:
- tokens: bfloat16 [64, 1024, 768], P(('dp', 'seq')), may hold values from -6 to 6
- lengths: int32 [64], P(('dp', 'seq')), may hold values from 64 to 1024, as said below
- mixer: bfloat16 [12, 1024, 1024], P('dp', 'seq'), may hold values from -8 to 8
- gain_one: bfloat16 [768], P(('dp', 'seq')), may hold values from 0.099609375 to 1.8984375
- gain_two: bfloat16 [768], P(('dp', 'seq')), may hold values from 0.099609375 to 1.8984375
- w_value: bfloat16 [768, 768], P(('dp', 'seq')), may hold values from -0.21875 to 0.21875
- w_out: bfloat16 [768, 768], P(('dp', 'seq')), may hold values from -1.75 to 1.75
- w_up: bfloat16 [768, 3072], P(('dp', 'seq')), may hold values from -0.21875 to 0.21875
- w_down: bfloat16 [3072, 768], P(('dp', 'seq')), may hold values from -0.15625 to 0.15625
- cotangent: bfloat16 [64, 1024, 768], P(('dp', 'seq')), may hold values from -6 to 6
Outputs:
- output: bfloat16 [64, 1024, 768], P(('dp', 'seq'))
- grad_tokens: bfloat16 [64, 1024, 768], P(('dp', 'seq'))
- grad_mixer: float32 [12, 1024, 1024], P('dp', 'seq')
- grad_gain_one: float32 [768], P(('dp', 'seq'))
- grad_gain_two: float32 [768], P(('dp', 'seq'))
- grad_w_value: float32 [768, 768], P(('dp', 'seq'))
- grad_w_out: float32 [768, 768], P(('dp', 'seq'))
- grad_w_up: float32 [768, 3072], P(('dp', 'seq'))
- grad_w_down: float32 [3072, 768], P(('dp', 'seq'))
Inputs may be any that keep to these rules, and one draw needn't show every extreme that they name: `lengths`: valid prefix of each item; in every draw some item has length 1024 and some item 64.
All inputs are finite; a program needn't handle non-finite values.
Results may differ from a plain program's by a relative error of at most 0.017.
Values may be sent and summed in bfloat16 or wider, within the bound.
No kernel may reach another device: no remote copies, remote signals or barrier semaphores. Data moves between devices by JAX's collectives and lax.ppermute only.
A program may use at most 448 MiB of HBM per device.

v0:
```python
import jax
import jax.numpy as jnp
from jax import lax
from jax.sharding import PartitionSpec as P

epsilon = 1e-06


def rms_scale(inputs, gain):
    factor = lax.rsqrt(jnp.mean(inputs * inputs, axis=-1, keepdims=True) + epsilon)
    return (inputs * factor * gain, factor)


def rms_back(inputs, factor, gain, grad_normed):
    weighted = gain * grad_normed
    grad_gain = jnp.sum((grad_normed * inputs * factor).reshape(-1, inputs.shape[-1]), axis=0)
    grad_inputs = factor * weighted - inputs * factor**3 * jnp.mean(
        weighted * inputs, axis=-1, keepdims=True
    )
    return (grad_inputs, grad_gain)


def softmax_rows(mixer_all, length):
    rows = lax.broadcasted_iota(jnp.int32, mixer_all.shape, 1)
    columns = lax.broadcasted_iota(jnp.int32, mixer_all.shape, 2)
    keep_keys = columns < length
    masked = jnp.where(keep_keys, mixer_all.astype(jnp.float32), -1e30)
    top = jnp.max(masked, axis=2, keepdims=True)
    expos = jnp.where(keep_keys, jnp.exp(masked - top), 0.0)
    probs = expos / jnp.sum(expos, axis=2, keepdims=True)
    return jnp.where(rows < length, probs, 0.0)


def mix_items(values, group_lengths, mixer_all):
    heads_here = mixer_all.shape[0]
    length_all = values.shape[1]
    head_width = values.shape[2] // heads_here

    def single(entry):
        vectors, length = entry
        probs = softmax_rows(mixer_all, length).astype(jnp.bfloat16)
        split = vectors.reshape(length_all, heads_here, head_width)
        mixed = jnp.einsum("hij,jhd->ihd", probs, split, preferred_element_type=jnp.float32)
        return mixed.reshape(length_all, heads_here * head_width).astype(jnp.bfloat16)

    return lax.map(single, (values, group_lengths))


def mix_back(values, grad_mixed, group_lengths, mixer_all):
    heads_here = mixer_all.shape[0]
    length_all = values.shape[1]
    head_width = values.shape[2] // heads_here

    def single(total, entry):
        vectors, gradient, length = entry
        probs = softmax_rows(mixer_all, length)
        split = vectors.reshape(length_all, heads_here, head_width)
        grad_split = gradient.reshape(length_all, heads_here, head_width)
        grad_probs = jnp.einsum(
            "ihd,jhd->hij", grad_split, split, preferred_element_type=jnp.float32
        )
        grad_vectors = jnp.einsum(
            "hij,ihd->jhd",
            probs.astype(jnp.bfloat16),
            grad_split,
            preferred_element_type=jnp.float32,
        )
        grad_scores = probs * (grad_probs - jnp.sum(probs * grad_probs, axis=2, keepdims=True))
        return (
            total + grad_scores,
            grad_vectors.reshape(length_all, heads_here * head_width).astype(jnp.bfloat16),
        )

    start = jnp.zeros(mixer_all.shape, jnp.float32)
    return lax.scan(single, start, (values, grad_mixed, group_lengths))


def body(tokens, lengths, mixer, gain_one, gain_two, w_value, w_out, w_up, w_down, cotangent):
    gain_one_all, gain_two_all, value_all, out_all, up_all, down_all = (
        lax.all_gather(gain_one, ("dp", "seq"), axis=0, tiled=True),
        lax.all_gather(gain_two, ("dp", "seq"), axis=0, tiled=True),
        lax.all_gather(w_value, ("dp", "seq"), axis=0, tiled=True),
        lax.all_gather(w_out, ("dp", "seq"), axis=0, tiled=True),
        lax.all_gather(w_up, ("dp", "seq"), axis=0, tiled=True),
        lax.all_gather(w_down, ("dp", "seq"), axis=0, tiled=True),
    )
    mixer_rows = lax.all_gather(mixer, "seq", axis=1, tiled=True)
    gain_first = gain_one_all.astype(jnp.float32)
    gain_second = gain_two_all.astype(jnp.float32)
    inputs = tokens.astype(jnp.float32)
    normed, factor_one = rms_scale(inputs, gain_first)
    normed_low = normed.astype(jnp.bfloat16)
    values = jnp.dot(normed_low, value_all, preferred_element_type=jnp.float32).astype(jnp.bfloat16)
    mixer_all = lax.all_gather(mixer_rows, "dp", axis=0, tiled=True)
    mixed = mix_items(values, lengths, mixer_all)
    hidden = inputs + jnp.dot(mixed, out_all, preferred_element_type=jnp.float32)
    normed_two, factor_two = rms_scale(hidden, gain_second)
    normed_two_low = normed_two.astype(jnp.bfloat16)
    pre_active = jnp.dot(normed_two_low, up_all, preferred_element_type=jnp.float32)
    active, gelu_pull = jax.vjp(lambda inner: jax.nn.gelu(inner, approximate=True), pre_active)
    active_low = active.astype(jnp.bfloat16)
    result = hidden + jnp.dot(active_low, down_all, preferred_element_type=jnp.float32)
    grad_w_down = jnp.einsum(
        "ilf,ild->fd", active_low, cotangent, preferred_element_type=jnp.float32
    )
    grad_active = jnp.einsum("ild,fd->ilf", cotangent, down_all, preferred_element_type=jnp.float32)
    grad_pre = gelu_pull(grad_active)[0].astype(jnp.bfloat16)
    grad_w_up = jnp.einsum(
        "ild,ilf->df", normed_two_low, grad_pre, preferred_element_type=jnp.float32
    )
    grad_normed_two = jnp.einsum(
        "ilf,df->ild", grad_pre, up_all, preferred_element_type=jnp.float32
    )
    grad_hidden, grad_gain_two = rms_back(hidden, factor_two, gain_second, grad_normed_two)
    grad_hidden = grad_hidden + cotangent.astype(jnp.float32)
    grad_attended = grad_hidden.astype(jnp.bfloat16)
    grad_w_out = jnp.einsum("ilc,ild->cd", mixed, grad_attended, preferred_element_type=jnp.float32)
    grad_mixed = jnp.einsum(
        "ild,cd->ilc", grad_attended, out_all, preferred_element_type=jnp.float32
    ).astype(jnp.bfloat16)
    grad_mixer_all, grad_values = mix_back(values, grad_mixed, lengths, mixer_all)
    grad_rows = lax.psum_scatter(
        grad_mixer_all.astype(jnp.bfloat16), "dp", scatter_dimension=0, tiled=True
    )
    grad_mixer = lax.psum_scatter(grad_rows, "seq", scatter_dimension=1, tiled=True).astype(
        jnp.float32
    )
    grad_w_value = jnp.einsum(
        "ild,ile->de", normed_low, grad_values, preferred_element_type=jnp.float32
    )
    grad_normed = jnp.einsum(
        "ile,de->ild", grad_values, value_all, preferred_element_type=jnp.float32
    )
    grad_inputs, grad_gain_one = rms_back(inputs, factor_one, gain_first, grad_normed)
    grad_inputs = grad_inputs + grad_hidden
    summed = (
        lax.psum_scatter(grad_gain_one, ("dp", "seq"), scatter_dimension=0, tiled=True),
        lax.psum_scatter(grad_gain_two, ("dp", "seq"), scatter_dimension=0, tiled=True),
        lax.psum_scatter(grad_w_value, ("dp", "seq"), scatter_dimension=0, tiled=True),
        lax.psum_scatter(grad_w_out, ("dp", "seq"), scatter_dimension=0, tiled=True),
        lax.psum_scatter(grad_w_up, ("dp", "seq"), scatter_dimension=0, tiled=True),
        lax.psum_scatter(grad_w_down, ("dp", "seq"), scatter_dimension=0, tiled=True),
    )
    return (
        result.astype(jnp.bfloat16),
        grad_inputs.astype(jnp.bfloat16),
        grad_mixer,
        summed[0],
        summed[1],
        summed[2],
        summed[3],
        summed[4],
        summed[5],
    )


def solution(mesh):
    placed = (
        P(("dp", "seq"), None, None),
        P(("dp", "seq")),
        P("dp", "seq", None),
        P(("dp", "seq")),
        P(("dp", "seq")),
        P(("dp", "seq"), None),
        P(("dp", "seq"), None),
        P(("dp", "seq"), None),
        P(("dp", "seq"), None),
        P(("dp", "seq"), None, None),
    )
    return jax.shard_map(
        body,
        mesh=mesh,
        in_specs=placed,
        out_specs=(
            P(("dp", "seq"), None, None),
            P(("dp", "seq"), None, None),
            P("dp", "seq", None),
            P(("dp", "seq")),
            P(("dp", "seq")),
            P(("dp", "seq"), None),
            P(("dp", "seq"), None),
            P(("dp", "seq"), None),
            P(("dp", "seq"), None),
        ),
        check_vma=False,
    )
```

profile of v0, /device:TPU:0, one launch (start us, length us, event | category | flops | bytes accessed | tf_op | source)
XLA Modules:
  0.0 1731.8 jit_solution(5488560692535288322)
XLA Ops:
  8.7 68.4 %all-gather.9.cloned.1.call-done = bf16[3,1024,1024]{2,1,0:T(8,128)(2,1)} async-done(((bf16[3,128,1024]{2,1,0:T(8,128)(2,1)}), bf16[3,1024,1024]{2,1,0:T(8,128)(2,1)}) %all-gather.9.cloned.1.call-update) | async-done | bytes 6291472 | tf_op jit(solution)/shard_map/all_gather | solution.py:87
  79.4 39.0 %all-reduce.6 = (bf16[768]{0:T(1024)(128)(2,1)S(1)}, bf16[768]{0:T(1024)(128)(2,1)S(1)}) all-reduce(bf16[768]{0:T(1024)(128)(2,1)S(1)} %dynamic-update-slice, bf16[768]{0:T(1024)(128)(2,1)S(1)} %dynamic-update-slice.1), channel_id=1, replica_groups=mesh['dp'=4,'seq'=8] {'dp','seq'}, use_global_device_ids=true, to_apply=%add | all-reduce | flops 1536 | bytes 6144
  119.0 3.2 copy.44
  123.9 4.6 copy.51
  128.5 4.5 all-gather.7.cloned.1.call-done
  133.0 5.5 convolution_convert_fusion.1
  138.6 3.5 copy.46
  142.1 219.5 %all-gather.11.cloned.1.call-done = bf16[12,1024,1024]{2,1,0:T(8,128)(2,1)} async-done(((bf16[3,1024,1024]{2,1,0:T(8,128)(2,1)}), bf16[12,1024,1024]{2,1,0:T(8,128)(2,1)}) %all-gather.11.cloned.1.call-update) | async-done | bytes 25165840 | tf_op jit(solution)/shard_map/all_gather | solution.py:94
  361.6 2.1 broadcast.83.clone
  363.6 121.9 %while.23 = (s32[]{:T(128)}, bf16[2,1024,768]{1,2,0:T(8,128)(2,1)}, bf16[2,1024,768]{1,2,0:T(8,128)(2,1)S(1)}, s32[2]{0:T(128)S(1)}, bf16[12,1024,1024]{2,1,0:T(8,128)(2,1)}, /*index=5*/s32[]{:T(128)}) while((s32[]{:T(128)}, bf16[2,1024,768]{1,2,0:T(8,128)(2,1)}, bf16[2,1024,768]{1,2,0:T(8,128)(2,1)S(1)}, s32[2]{0:T(128)S(1)}, ...), condition=%wide.region_4.5_spmd, body=%wide.region_1.4_spmd.sunk | while | flops 1737230336 | bytes 160533664 | solution.py:46
  365.0 38.7 %fusion.89 = (f32[12,1024]{1,0:T(8,128)S(1)}, f32[12,1024,1024]{2,1,0:T(8,128)}) fusion(bf16[12,1024,1024]{2,1,0:T(8,128)(2,1)} %get-tuple-element.291, pred[1024]{0:T(1024)(128)(4,1)S(1)} %iota_compare_fusion.4), kind=kOutput, calls=%fused_computation.92.clone.1 | output fusion | flops 88081408 | bytes 75547648 | tf_op jit(solution)/shard_map/while/body/eval_jaxpr/sub | solution.py:29
  403.7 18.9 %fusion.90 = bf16[12,64,1024]{2,1,0:T(8,128)(2,1)S(1)} fusion(bf16[1024,12,64]{0,2,1:T(8,128)(2,1)S(1)} %bitcast.92, f32[12,1024,1024]{2,1,0:T(8,128)} %get-tuple-element.262, f32[12,1024]{1,0:T(8,128)S(1)} %get-tuple-element.263, pred[1024]{0:T(1024)(128)(4,1)S(1)} %iota_compare_fusion.4), kind=kOutput, calls=%fused_computation.8.clone.1 | convolution fusion | flops 1649147904 | bytes 53527552 | tf_op jit(solution)/shard_map/while/body/eval_jaxpr/hij,jhd->ihd/dot_general | solution.py:43
  425.9 38.7 %fusion.89 = (f32[12,1024]{1,0:T(8,128)S(1)}, f32[12,1024,1024]{2,1,0:T(8,128)}) fusion(bf16[12,1024,1024]{2,1,0:T(8,128)(2,1)} %get-tuple-element.291, pred[1024]{0:T(1024)(128)(4,1)S(1)} %iota_compare_fusion.4), kind=kOutput, calls=%fused_computation.92.clone.1 | output fusion | flops 88081408 | bytes 75547648 | tf_op jit(solution)/shard_map/while/body/eval_jaxpr/sub | solution.py:29
  464.7 18.9 %fusion.90 = bf16[12,64,1024]{2,1,0:T(8,128)(2,1)S(1)} fusion(bf16[1024,12,64]{0,2,1:T(8,128)(2,1)S(1)} %bitcast.92, f32[12,1024,1024]{2,1,0:T(8,128)} %get-tuple-element.262, f32[12,1024]{1,0:T(8,128)S(1)} %get-tuple-element.263, pred[1024]{0:T(1024)(128)(4,1)S(1)} %iota_compare_fusion.4), kind=kOutput, calls=%fused_computation.8.clone.1 | convolution fusion | flops 1649147904 | bytes 53527552 | tf_op jit(solution)/shard_map/while/body/eval_jaxpr/hij,jhd->ihd/dot_general | solution.py:43
  485.6 8.9 multiply_reduce_fusion.3
  494.6 18.4 %fusion.46 = f32[2,1024,3072]{2,1,0:T(8,128)} fusion(bf16[768,3072]{1,0:T(8,128)(2,1)} %all-gather.15.cloned.1.call-done, f32[2,1024,768]{1,2,0:T(8,128)} %get-tuple-element.186, f32[768]{0:T(1024)S(1)} %copy-done.16, f32[2,1024]{1,0:T(2,128)S(1)} %get-tuple-element.184), kind=kOutput, calls=%fused_computation.73 | convolution fusion | flops 9668395008 | bytes 36187136 | tf_op jit(solution)/shard_map/dot_general | solution.py:99
  513.0 36.7 %all-gather.17.cloned.1.call-done = bf16[3072,768]{1,0:T(8,128)(2,1)} async-done(((bf16[96,768]{1,0:T(8,128)(2,1)}), bf16[3072,768]{1,0:T(8,128)(2,1)}) %all-gather.17.cloned.1.call-update) | async-done | bytes 4718608 | tf_op jit(solution)/shard_map/all_gather | solution.py:85
  549.6 31.5 %fusion.30 = bf16[2,1024,3072]{2,1,0:T(8,128)(2,1)} fusion(f32[2,1024,3072]{2,1,0:T(8,128)} %fusion.46, bf16[2,1024,768]{2,1,0:T(8,128)(2,1)} %param.23, bf16[3072,768]{1,0:T(8,128)(2,1)} %all-gather.17.cloned.1.call-done), kind=kOutput, calls=%fused_computation.42 | convolution fusion | flops 9789505536 | bytes 45613056 | tf_op jit(solution)/shard_map/ild,fd->ilf/dot_general | solution.py:106
  581.1 15.8 multiply_reduce_fusion.1
  597.0 4.0 convert_add_fusion.1
  601.0 32.7 %copy.53 = bf16[12,1024,1024]{1,2,0:T(8,128)(2,1)} copy(bf16[12,1024,1024]{2,1,0:T(8,128)(2,1)} %get-tuple-element.336) | data formatting | bytes 50331648
  633.7 7.4 convolution_convert_fusion
  641.1 2.1 broadcast.83
  643.2 259.8 %while.24 = (s32[]{:T(128)}, f32[12,1024,1024]{1,2,0:T(8,128)}, bf16[2,1024,768]{1,2,0:T(8,128)(2,1)}, s32[2]{0:T(128)S(1)}, bf16[12,1024,1024]{1,2,0:T(8,128)(2...) while((s32[]{:T(128)}, f32[12,1024,1024]{1,2,0:T(8,128)}, ...), condition=%wide.region_11.12_spmd.clone, body=%wide.region_7.11_spmd.clone.sunk | while | flops 5071715328 | bytes 352473472 | solution.py:75
  649.2 41.3 %fusion.99 = (f32[12,1024]{1,0:T(8,128)S(1)}, f32[12,1024,1024]{1,2,0:T(8,128)}) fusion(bf16[12,1024,1024]{1,2,0:T(8,128)(2,1)} %get-tuple-element.315, pred[1024]{0:T(1024)(128)(4,1)S(1)} %iota_compare_fusion.5), kind=kOutput, calls=%fused_computation.93.clone.1 | output fusion | flops 88081408 | bytes 75547648 | tf_op jit(solution)/shard_map/while/body/eval_jaxpr/sub | solution.py:29
  690.5 18.3 %fusion.100 = bf16[12,64,1024]{2,1,0:T(8,128)(2,1)S(1)} fusion(bf16[1024,12,64]{0,2,1:T(8,128)(2,1)S(1)} %bitcast.89, f32[12,1024,1024]{1,2,0:T(8,128)} %get-tuple-element.271, f32[12,1024]{1,0:T(8,128)S(1)} %get-tuple-element.272, pred[1024]{0:T(1024)(128)(4,1)S(1)} %iota_compare_fusion.5), kind=kOutput, calls=%fused_computation.28.clone.1 | convolution fusion | flops 1649147904 | bytes 53527552 | tf_op jit(solution)/shard_map/while/body/eval_jaxpr/hij,ihd->jhd/dot_general | solution.py:62
  710.4 1.7 copy-done.8
  712.1 53.7 %select_add_fusion.2 = f32[12,1024,1024]{1,2,0:T(8,128)} fusion(f32[12,1024,1024]{1,2,0:T(8,128)} %get-tuple-element.303, pred[]{:T(512)S(6)} %compare.3, bf16[1024,12,64]{0,2,1:T(8,128)(2,1)} %bitcast.88, bf16[1024,12,64]{0,2,1:T(8,128)(2,1)} %bitcast.90, f32[12,1024,1024]{1,2,0:T(8,128)} %get-tuple-element.271, ...), kind=kOutput, calls=%fused_computation.16.clone.1 | convolution fusion | flops 3334484992 | bytes 154190848 | tf_op jit(solution)/shard_map/while/body/eval_jaxpr/sub | solution.py:68
  771.2 41.3 %fusion.99 = (f32[12,1024]{1,0:T(8,128)S(1)}, f32[12,1024,1024]{1,2,0:T(8,128)}) fusion(bf16[12,1024,1024]{1,2,0:T(8,128)(2,1)} %get-tuple-element.315, pred[1024]{0:T(1024)(128)(4,1)S(1)} %iota_compare_fusion.5), kind=kOutput, calls=%fused_computation.93.clone.1 | output fusion | flops 88081408 | bytes 75547648 | tf_op jit(solution)/shard_map/while/body/eval_jaxpr/sub | solution.py:29
  812.6 18.3 %fusion.100 = bf16[12,64,1024]{2,1,0:T(8,128)(2,1)S(1)} fusion(bf16[1024,12,64]{0,2,1:T(8,128)(2,1)S(1)} %bitcast.89, f32[12,1024,1024]{1,2,0:T(8,128)} %get-tuple-element.271, f32[12,1024]{1,0:T(8,128)S(1)} %get-tuple-element.272, pred[1024]{0:T(1024)(128)(4,1)S(1)} %iota_compare_fusion.5), kind=kOutput, calls=%fused_computation.28.clone.1 | convolution fusion | flops 1649147904 | bytes 53527552 | tf_op jit(solution)/shard_map/while/body/eval_jaxpr/hij,ihd->jhd/dot_general | solution.py:62
  834.1 68.9 %select_add_fusion.2 = f32[12,1024,1024]{1,2,0:T(8,128)} fusion(f32[12,1024,1024]{1,2,0:T(8,128)} %get-tuple-element.303, pred[]{:T(512)S(6)} %compare.3, bf16[1024,12,64]{0,2,1:T(8,128)(2,1)} %bitcast.88, bf16[1024,12,64]{0,2,1:T(8,128)(2,1)} %bitcast.90, f32[12,1024,1024]{1,2,0:T(8,128)} %get-tuple-element.271, ...), kind=kOutput, calls=%fused_computation.16.clone.1 | convolution fusion | flops 3334484992 | bytes 154190848 | tf_op jit(solution)/shard_map/while/body/eval_jaxpr/sub | solution.py:68
  903.0 37.7 %copy.58 = bf16[12,1024,1024]{2,1,0:T(8,128)(2,1)} copy(f32[12,1024,1024]{1,2,0:T(8,128)} %get-tuple-element.76) | data formatting | bytes 75497472 | tf_op jit(solution)/shard_map/while | solution.py:75
  940.8 220.8 %reduce-scatter.19.cloned.1.call-done = bf16[3,1024,1024]{2,1,0:T(8,128)(2,1)} async-done(((bf16[12,1024,1024]{2,1,0:T(8,128)(2,1)}), bf16[3,1024,1024]{2,1,0:T(8,128)(2,1)}) %reduce-scatter.19.cloned.1.call-update) | async-done | bytes 6291472
  1161.8 7.9 convolution_bitcast_fusion.2
  1169.9 6.1 convolution_bitcast_fusion.3
  1176.1 21.6 %convolution_bitcast_fusion = f32[3072,768]{1,0:T(8,128)} fusion(bf16[2,1024,768]{2,1,0:T(8,128)(2,1)} %param.23, f32[2,1024,3072]{2,1,0:T(8,128)} %fusion.46), kind=kOutput, calls=%fused_computation.66 | convolution fusion | flops 9720299520 | bytes 37748736 | tf_op jit(solution)/shard_map/ilf,ild->fd/dot_general | solution.py:103
  1198.4 17.2 convolution_bitcast_fusion.1
  1215.6 18.6 %add_convert_fusion = bf16[2,1024,768]{1,2,0:T(8,128)(2,1)} fusion(f32[2,1024,768]{1,2,0:T(8,128)} %get-tuple-element.186, bf16[3072,768]{1,0:T(8,128)(2,1)} %all-gather.17.cloned.1.call-done, f32[2,1024,3072]{2,1,0:T(8,128)} %fusion.46), kind=kOutput, calls=%fused_computation.63 | convolution fusion | flops 9723445248 | bytes 39321600 | tf_op jit(solution)/shard_map/dot_general | solution.py:102
  1234.2 4.6 copy.64
  1238.8 8.0 fusion.40
  1246.8 39.6 %all-reduce.5 = (f32[768]{0:T(1024)S(1)}, f32[768]{0:T(1024)S(1)}) all-reduce(f32[768]{0:T(1024)S(1)} %get-tuple-element.145, f32[768]{0:T(1024)S(1)} %copy-done.20), channel_id=4, replica_groups=mesh['dp'=4,'seq'=8] {'dp','seq'}, use_global_device_ids=true, to_apply=%region_16.17.clone | all-reduce | flops 1536 | bytes 12288
  1287.6 7.0 fusion.37
  1294.6 4.6 copy.65
  1299.3 2.5 convert_element_type.103
  1301.7 36.2 %reduce-scatter.13.cloned.1.call-done = f32[24,768]{1,0:T(8,128)} async-done(((f32[768,768]{1,0:T(8,128)}), f32[24,768]{1,0:T(8,128)}) %reduce-scatter.13.cloned.1.call-update) | async-done | bytes 73744 | tf_op jit(solution)/shard_map/reduce_scatter | solution.py:140
  1337.9 103.8 %reduce-scatter.11.cloned.1.call-done = f32[24,768]{1,0:T(8,128)} async-done(((f32[768,768]{1,0:T(8,128)}), f32[24,768]{1,0:T(8,128)}) %reduce-scatter.11.cloned.1.call-update) | async-done | bytes 73744 | tf_op jit(solution)/shard_map/reduce_scatter | solution.py:139
  1441.7 142.0 %reduce-scatter.17.cloned.1.call-done = f32[96,768]{1,0:T(8,128)} async-done(((f32[3072,768]{1,0:T(8,128)}), f32[96,768]{1,0:T(8,128)}) %reduce-scatter.17.cloned.1.call-update) | async-done | bytes 294928 | tf_op jit(solution)/shard_map/reduce_scatter | solution.py:142
  1583.7 140.9 %reduce-scatter.15.cloned.1.call-done = f32[24,3072]{1,0:T(8,128)} async-done(((f32[768,3072]{1,0:T(8,128)}), f32[24,3072]{1,0:T(8,128)}) %reduce-scatter.15.cloned.1.call-update) | async-done | bytes 294928 | tf_op jit(solution)/shard_map/reduce_scatter | solution.py:141
  (128 shorter events, 30.6 us)
Async XLA Ops:
  7.2 71.8 %copy-start.21 = (bf16[24]{0:T(256)(128)(2,1)S(1)}, bf16[24]{0:T(256)(128)(2,1)}, u32[]{:S(2)}) copy-start(bf16[24]{0:T(256)(128)(2,1)} %param.17) | copy-start | bytes 148
  7.2 72.0 %copy-start.22 = (bf16[24]{0:T(256)(128)(2,1)S(1)}, bf16[24]{0:T(256)(128)(2,1)}, u32[]{:S(2)}) copy-start(bf16[24]{0:T(256)(128)(2,1)} %param.18) | copy-start | bytes 148
  7.2 69.9 %all-gather.9.cloned.1.call-start = ((), (), s32[]{:S(2)}) async-start(), calls=%async_computation.7 | async-start | bytes 7077888 | tf_op jit(solution)/shard_map/all_gather | solution.py:87
  7.9 125.1 %all-gather.7.cloned.1.call-start = ((), (), s32[]{:S(2)}) async-start(), calls=%async_computation.6 | async-start | bytes 1216512 | tf_op jit(solution)/shard_map/all_gather | solution.py:82
  8.7 352.9 %all-gather.11.cloned.1.call-start = ((), (), s32[]{:S(2)}) async-start(), calls=%async_computation.8 | async-start | bytes 31457280 | tf_op jit(solution)/shard_map/all_gather | solution.py:94
  77.1 408.5 %all-gather.13.cloned.1.call-start = ((), (), s32[]{:S(2)}) async-start(), calls=%async_computation.9 | async-start | bytes 1216512 | tf_op jit(solution)/shard_map/all_gather | solution.py:83
  77.7 416.9 %all-gather.15.cloned.1.call-start = ((), (), s32[]{:S(2)}) async-start(), calls=%async_computation.10 | async-start | bytes 4866048 | tf_op jit(solution)/shard_map/all_gather | solution.py:84
  78.3 471.3 %all-gather.17.cloned.1.call-start = ((), (), s32[]{:S(2)}) async-start(), calls=%async_computation.11 | async-start | bytes 4866048 | tf_op jit(solution)/shard_map/all_gather | solution.py:85
  78.8 1082.7 %reduce-scatter.19.cloned.1.call-start = ((), (), s32[]{:S(2)}) async-start(), calls=%async_computation.17 | async-start | bytes 31457280
  118.4 14.6 copy-start.18
  122.2 10.8 copy-start.3
  123.9 14.7 copy-start.14
  138.6 225.1 %copy-start.23 = (s32[2]{0:T(128)S(1)}, s32[2]{0:T(128)}, u32[]{:S(2)}) copy-start(s32[2]{0:T(128)} %param.15) | copy-start | bytes 28
  403.7 18.9 %copy-start.9 = (bf16[2,1024,768]{1,2,0:T(8,128)(2,1)S(1)}, bf16[2,1024,768]{1,2,0:T(8,128)(2,1)}, u32[]{:S(2)}) copy-start(bf16[2,1024,768]{1,2,0:T(8,128)(2,1)} %get-tuple-element.282) | copy-start | bytes 9437188 | tf_op jit(solution)/shard_map/while
  422.9 1.7 copy-start.10
  464.7 18.9 %copy-start.9 = (bf16[2,1024,768]{1,2,0:T(8,128)(2,1)S(1)}, bf16[2,1024,768]{1,2,0:T(8,128)(2,1)}, u32[]{:S(2)}) copy-start(bf16[2,1024,768]{1,2,0:T(8,128)(2,1)} %get-tuple-element.282) | copy-start | bytes 9437188 | tf_op jit(solution)/shard_map/while
  483.8 1.7 copy-start.10
  485.6 8.9 copy-start.16
  494.5 102.4 %copy-start.11 = (f32[2,1024]{1,0:T(2,128)}, f32[2,1024]{1,0:T(2,128)S(1)}, u32[]{:S(2)}) copy-start(f32[2,1024]{1,0:T(2,128)S(1)} %get-tuple-element.184) | copy-start | bytes 24580
  549.6 31.5 %copy-start.6 = (f32[2,1024,768]{1,2,0:T(8,128)S(1)}, f32[2,1024,768]{1,2,0:T(8,128)}, u32[]{:S(2)}) copy-start(f32[2,1024,768]{1,2,0:T(8,128)} %get-tuple-element.186) | copy-start | bytes 18874372
  581.1 15.9 copy-start.5
  643.7 1.7 copy-start
  643.7 46.8 %copy-start.24 = (s32[2]{0:T(128)}, s32[2]{0:T(128)S(1)}, u32[]{:S(2)}) copy-start(s32[2]{0:T(128)S(1)} %get-tuple-element.314) | copy-start | bytes 28 | tf_op jit(solution)/shard_map/while
  649.2 41.3 %copy-start.2 = (bf16[1,1024,768]{1,2,0:T(8,128)(2,1)S(1)}, bf16[1,1024,768]{1,2,0:T(8,128)(2,1)}, u32[]{:S(2)}) copy-start(bf16[1,1024,768]{1,2,0:T(8,128)(2,1)} %copy.80) | copy-start | bytes 4718596 | tf_op jit(solution)/shard_map/while
  690.5 18.3 %copy-start.1 = (bf16[2,1024,768]{1,2,0:T(8,128)(2,1)S(1)}, bf16[2,1024,768]{1,2,0:T(8,128)(2,1)}, u32[]{:S(2)}) copy-start(bf16[2,1024,768]{1,2,0:T(8,128)(2,1)} %copy-done) | copy-start | bytes 9437188 | tf_op jit(solution)/shard_map/while
  690.5 18.3 %copy-start.7 = (bf16[2,1024,768]{1,2,0:T(8,128)(2,1)S(1)}, bf16[2,1024,768]{1,2,0:T(8,128)(2,1)}, u32[]{:S(2)}) copy-start(bf16[2,1024,768]{1,2,0:T(8,128)(2,1)} %get-tuple-element.304) | copy-start | bytes 9437188 | tf_op jit(solution)/shard_map/while
  710.4 1.7 copy-start.8
  712.1 53.7 %copy-start.25 = (s32[2]{0:T(128)S(1)}, s32[2]{0:T(128)}, u32[]{:S(2)}) copy-start(s32[2]{0:T(128)} %copy-done.24) | copy-start | bytes 28 | tf_op jit(solution)/shard_map/while
  765.7 1.7 copy-start
  765.7 46.8 %copy-start.24 = (s32[2]{0:T(128)}, s32[2]{0:T(128)S(1)}, u32[]{:S(2)}) copy-start(s32[2]{0:T(128)S(1)} %get-tuple-element.314) | copy-start | bytes 28 | tf_op jit(solution)/shard_map/while
  771.2 41.3 %copy-start.2 = (bf16[1,1024,768]{1,2,0:T(8,128)(2,1)S(1)}, bf16[1,1024,768]{1,2,0:T(8,128)(2,1)}, u32[]{:S(2)}) copy-start(bf16[1,1024,768]{1,2,0:T(8,128)(2,1)} %copy.80) | copy-start | bytes 4718596 | tf_op jit(solution)/shard_map/while
  812.5 18.3 %copy-start.1 = (bf16[2,1024,768]{1,2,0:T(8,128)(2,1)S(1)}, bf16[2,1024,768]{1,2,0:T(8,128)(2,1)}, u32[]{:S(2)}) copy-start(bf16[2,1024,768]{1,2,0:T(8,128)(2,1)} %copy-done) | copy-start | bytes 9437188 | tf_op jit(solution)/shard_map/while
  812.6 18.3 %copy-start.7 = (bf16[2,1024,768]{1,2,0:T(8,128)(2,1)S(1)}, bf16[2,1024,768]{1,2,0:T(8,128)(2,1)}, u32[]{:S(2)}) copy-start(bf16[2,1024,768]{1,2,0:T(8,128)(2,1)} %get-tuple-element.304) | copy-start | bytes 9437188 | tf_op jit(solution)/shard_map/while
  832.4 1.7 copy-start.8
  834.1 68.9 %copy-start.25 = (s32[2]{0:T(128)S(1)}, s32[2]{0:T(128)}, u32[]{:S(2)}) copy-start(s32[2]{0:T(128)} %copy-done.24) | copy-start | bytes 28 | tf_op jit(solution)/shard_map/while
  940.7 358.5 %reduce-scatter.9.cloned.1.call-start = ((), (), s32[]{:S(2)}) async-start(), calls=%async_computation.12 | async-start | bytes 7077888 | tf_op jit(solution)/shard_map/reduce_scatter | solution.py:125
  1161.6 8.2 copy-start.4
  1161.6 8.2 copy-start.15
  1161.6 8.2 copy-start.19
  1161.6 176.3 %reduce-scatter.13.cloned.1.call-start = ((), (), s32[]{:S(2)}) async-start(), calls=%async_computation.14 | async-start | bytes 2433024 | tf_op jit(solution)/shard_map/reduce_scatter | solution.py:140
  1169.8 272.0 %reduce-scatter.11.cloned.1.call-start = ((), (), s32[]{:S(2)}) async-start(), calls=%async_computation.13 | async-start | bytes 2433024 | tf_op jit(solution)/shard_map/reduce_scatter | solution.py:139
  1176.0 407.7 %reduce-scatter.17.cloned.1.call-start = ((), (), s32[]{:S(2)}) async-start(), calls=%async_computation.16 | async-start | bytes 9732096 | tf_op jit(solution)/shard_map/reduce_scatter | solution.py:142
  1197.7 0.7 copy-start.12
  1197.7 0.7 copy-start.17
  1197.7 526.9 %reduce-scatter.15.cloned.1.call-start = ((), (), s32[]{:S(2)}) async-start(), calls=%async_computation.15 | async-start | bytes 9732096 | tf_op jit(solution)/shard_map/reduce_scatter | solution.py:141
  1238.8 8.0 copy-start.20
  1238.8 48.8 %copy-start.13 = (f32[2,1024]{1,0:T(2,128)S(1)}, f32[2,1024]{1,0:T(2,128)}, u32[]{:S(2)}) copy-start(f32[2,1024]{1,0:T(2,128)} %get-tuple-element.181) | copy-start | bytes 24580
Sparse Core Ops, SparseCore 0:
  9.6 67.4 all-gather.8
  80.1 52.8 all-gather.6
  134.9 226.6 all-gather.10
  364.5 54.1 all-gather.12
  421.5 62.6 all-gather.14
  487.1 62.4 all-gather.16
  940.9 220.6 reduce-scatter.18
  1164.0 69.7 reduce-scatter.8
  1240.5 97.3 reduce-scatter.12
  1343.6 98.0 reduce-scatter.10
  1449.2 134.4 reduce-scatter.16
  1590.1 134.5 reduce-scatter.14
where the time goes:
time: 1740 us; the launch traced here: 1730 us
  waiting for transfers between devices  976 us (56%)
  matrix products  364 us (21%)
  other arithmetic  178 us (10%)
  local copies, waits for them, and re-layouts  119 us (7%)
  blocking collectives  78.7 us (5%)
    unnamed x13, waiting for transfers between devices  224 us
    all_gather x1, waiting for transfers between devices, body(): mixer_all = lax.all_gather(mixer_rows, 'dp', axis=0, tiled=True)  219 us
    sub x4, other arithmetic, softmax_rows(): expos = jnp.where(keep_keys, jnp.exp(masked - top), 0.0)  160 us
    reduce_scatter x1, waiting for transfers between devices, body(): lax.psum_scatter(grad_w_down, ('dp', 'seq'), scatter_dimension=0, tiled=T...  142 us
    reduce_scatter x1, waiting for transfers between devices, body(): lax.psum_scatter(grad_w_up, ('dp', 'seq'), scatter_dimension=0, tiled=True)  141 us
    sub x2, matrix products, single(): grad_probs - jnp.sum(probs * grad_probs, axis=2, keepdims=True)  123 us
    reduce_scatter x1, waiting for transfers between devices, body(): lax.psum_scatter(grad_w_value, ('dp', 'seq'), scatter_dimension=0, tiled=...  104 us
    unnamed x2, blocking collectives  78.7 us
  transfers between devices with their start and end apart: 12, of which 9 were waited for; matrix products, arithmetic and copies ran while one was open for 15% of the time, Pallas kernels for 0%

commit v1 on v0

v1 whole, which is shorter than its diff:
```python
import functools

import jax
import jax.numpy as jnp
from jax import lax
from jax.experimental import pallas as pl
from jax.experimental.pallas import tpu as pltpu
from jax.sharding import PartitionSpec as P

epsilon = 1e-06
bf16 = jnp.bfloat16
f32 = jnp.float32
WIDTH = 768
LENGTH = 1024
HIDDEN = 3072
HEADS = 12
HEAD_DIM = 64
CHUNKS = 4
VMEM = 58 * 1024 * 1024


def rows_by_rows(left, right):
    return lax.dot_general(left, right, (((1,), (1,)), ((), ())), preferred_element_type=f32)


def times(left, right):
    return jnp.dot(left, right, preferred_element_type=f32)


def rms(values):
    return lax.rsqrt(jnp.mean(values * values, axis=-1, keepdims=True) + epsilon)


def params(**more):
    return pltpu.CompilerParams(vmem_limit_bytes=VMEM, **more)


def cost(flops, moved):
    return pl.CostEstimate(flops=int(flops), bytes_accessed=int(moved), transcendentals=0)


def spread(scratch, refs, place, group):
    for at, ref in enumerate(refs):
        start = pl.multiple_of((place ^ at) * group, 64)
        scratch[pl.ds(start, group), :] = ref[0]


def pick(scratch, refs, place, group):
    for at, ref in enumerate(refs):
        start = pl.multiple_of((place ^ at) * group, 64)
        ref[0] = scratch[pl.ds(start, group), :]


def values_kernel(where, x_ref, w_ref, *rest):
    outs, (turned, scratch) = rest[:-2], rest[-2:]

    @pl.when((pl.program_id(0) == 0) & (pl.program_id(1) == 0))
    def _():
        turned[...] = w_ref[...].T

    x = x_ref[0].astype(f32)
    scaled = (x * rms(x)).astype(bf16)
    scratch[...] = rows_by_rows(turned[...], scaled).astype(bf16)
    pick(scratch, outs, where[0], outs[0].shape[1])


def project_values(where, tokens, weight, groups):
    items = tokens.shape[0]
    rows = 512
    group = WIDTH // groups
    return pl.pallas_call(
        values_kernel,
        grid_spec=pltpu.PrefetchScalarGridSpec(
            num_scalar_prefetch=1,
            grid=(items, LENGTH // rows),
            in_specs=[
                pl.BlockSpec((1, rows, WIDTH), lambda i, j, s: (i, j, 0)),
                pl.BlockSpec((WIDTH, WIDTH), lambda i, j, s: (0, 0)),
            ],
            out_specs=[pl.BlockSpec((1, group, rows), lambda i, j, s: (i, 0, j))] * groups,
            scratch_shapes=[pltpu.VMEM((WIDTH, WIDTH), bf16), pltpu.VMEM((WIDTH, rows), bf16)],
        ),
        out_shape=[jax.ShapeDtypeStruct((items, group, LENGTH), bf16)] * groups,
        compiler_params=params(),
        cost_estimate=cost(2 * items * LENGTH * WIDTH * WIDTH, 4 * items * LENGTH * WIDTH),
        name="project_values",
    )(where, tokens, weight)


def load_logits(offsets, pieces, held, sems, first):
    def copy(head, at):
        rows = pieces[at].shape[1]
        start = pl.multiple_of(offsets[at], rows)
        return pltpu.make_async_copy(
            pieces[at].at[head], held.at[head, pl.ds(start, rows)], sems.at[head, at]
        )

    head = pl.program_id(0)

    @pl.when(first)
    def _():
        for h in range(held.shape[0]):
            for at in range(len(pieces)):
                copy(h, at).start()

    for at in range(len(pieces)):
        copy(head, at).wait()


def mix_kernel(lengths, offsets, *rest, groups, pieces):
    values, parts = rest[:groups], rest[groups : groups + pieces]
    outs = rest[groups + pieces : 2 * groups + pieces]
    sums_ref, held, left, sems = rest[2 * groups + pieces :]
    load_logits(offsets, parts, held, sems, pl.program_id(0) == 0)
    items = values[0].shape[0]
    total = groups * items
    places = lax.broadcasted_iota(jnp.int32, (1, LENGTH), 1)
    for k in range(total):
        block = values[k // items][k % items]
        keep = places < lengths[k]
        left[pl.ds(k * HEAD_DIM, HEAD_DIM), :] = jnp.where(keep, block, jnp.zeros_like(block))
    which = lax.broadcasted_iota(jnp.int32, (16, LENGTH), 0)
    reach = jnp.zeros((16, LENGTH), jnp.int32)
    for k in range(total):
        reach = jnp.where(which == k, lengths[k], reach)
    columns = lax.broadcasted_iota(jnp.int32, (16, LENGTH), 1)
    left[pl.ds(total * HEAD_DIM, 16), :] = jnp.where(columns < reach, 1.0, 0.0).astype(bf16)
    product = rows_by_rows(left[...], held[pl.program_id(0)])
    sums = product[total * HEAD_DIM : total * HEAD_DIM + total]
    sums_ref[0] = sums
    for k in range(total):
        mixed = product[k * HEAD_DIM : (k + 1) * HEAD_DIM] / sums[k : k + 1]
        keep = places < lengths[k]
        outs[k // items][k % items] = jnp.where(keep, mixed, 0.0).astype(bf16)


def mix_items(lengths, offsets, values, parts):
    groups, pieces = len(values), len(parts)
    items, group, _ = values[0].shape
    heads = group // HEAD_DIM
    total = groups * items
    block = pl.BlockSpec((items, HEAD_DIM, LENGTH), lambda h, s, o: (0, h, 0))
    outs = pl.pallas_call(
        functools.partial(mix_kernel, groups=groups, pieces=pieces),
        grid_spec=pltpu.PrefetchScalarGridSpec(
            num_scalar_prefetch=2,
            grid=(heads,),
            in_specs=[block] * groups + [pl.BlockSpec(memory_space=pl.ANY)] * pieces,
            out_specs=[block] * groups
            + [pl.BlockSpec((1, total, LENGTH), lambda h, s, o: (h, 0, 0))],
            scratch_shapes=[
                pltpu.VMEM((heads, LENGTH, LENGTH), bf16),
                pltpu.VMEM((total * HEAD_DIM + 16, LENGTH), bf16),
                pltpu.SemaphoreType.DMA((heads, pieces)),
            ],
        ),
        out_shape=[jax.ShapeDtypeStruct((items, group, LENGTH), bf16)] * groups
        + [jax.ShapeDtypeStruct((heads, total, LENGTH), f32)],
        compiler_params=params(),
        cost_estimate=cost(2 * heads * total * 66 * LENGTH * LENGTH, 12 << 20),
        name="mix_items",
    )(lengths, offsets, *values, *parts)
    return outs[:groups], outs[groups]


def mix_back_kernel(lengths, offsets, *rest, groups, pieces, shares):
    grads, values, mixed = (rest[k * groups : (k + 1) * groups] for k in range(3))
    rest = rest[3 * groups :]
    sums_ref, parts = rest[0], rest[1 : 1 + pieces]
    outs = rest[1 + pieces : 1 + pieces + groups]
    rest = rest[1 + pieces + groups :]
    shares_refs = rest[: len(shares)]
    held, left, right, whole, sems = rest[len(shares) :]
    load_logits(offsets, parts, held, sems, pl.program_id(0) == 0)
    items = values[0].shape[0]
    total = groups * items
    places = lax.broadcasted_iota(jnp.int32, (1, LENGTH), 1)
    which = lax.broadcasted_iota(jnp.int32, (16, LENGTH), 0)
    base = total * HEAD_DIM
    extra_left = jnp.zeros((16, LENGTH), f32)
    extra_right = jnp.zeros((16, LENGTH), f32)
    for k in range(total):
        keep = places < lengths[k]
        inverse = jnp.where(keep, 1.0 / sums_ref[0, k : k + 1], 0.0)
        grad = grads[k // items][k % items].astype(f32)
        delta = jnp.sum(grad * mixed[k // items][k % items].astype(f32), axis=0, keepdims=True)
        left[pl.ds(k * HEAD_DIM, HEAD_DIM), :] = (grad * inverse).astype(bf16)
        extra_left = jnp.where(which == k, -(delta * inverse), extra_left)
        extra_right = jnp.where((which == k) & keep, 1.0, extra_right)
        block = values[k // items][k % items]
        right[pl.ds(k * HEAD_DIM, HEAD_DIM), :] = jnp.where(keep, block, jnp.zeros_like(block))
    left[pl.ds(base, 16), :] = extra_left.astype(bf16)
    right[pl.ds(base, 16), :] = extra_right.astype(bf16)
    grad_values = times(left[pl.ds(0, base), :], held[pl.program_id(0)])
    for k in range(total):
        keep = places < lengths[k]
        part = grad_values[k * HEAD_DIM : (k + 1) * HEAD_DIM]
        outs[k // items][k % items] = jnp.where(keep, part, 0.0).astype(bf16)
    whole[...] = times(left[...].T, right[...]).astype(bf16)
    at = pieces
    for ref, (count, rows) in zip(shares_refs, shares):
        for k in range(count):
            ref[k, 0] = whole[pl.ds(pl.multiple_of(offsets[at], rows), rows), :]
            at += 1


def mix_back(lengths, offsets, grads, values, mixed, sums, parts, shares):
    groups, pieces = len(values), len(parts)
    items, group, _ = values[0].shape
    heads = group // HEAD_DIM
    total = groups * items
    block = pl.BlockSpec((items, HEAD_DIM, LENGTH), lambda h, s, o: (0, h, 0))
    outs = pl.pallas_call(
        functools.partial(mix_back_kernel, groups=groups, pieces=pieces, shares=shares),
        grid_spec=pltpu.PrefetchScalarGridSpec(
            num_scalar_prefetch=2,
            grid=(heads,),
            in_specs=[block] * (3 * groups)
            + [pl.BlockSpec((1, total, LENGTH), lambda h, s, o: (h, 0, 0))]
            + [pl.BlockSpec(memory_space=pl.ANY)] * pieces,
            out_specs=[block] * groups
            + [
                pl.BlockSpec((count, 1, rows, LENGTH), lambda h, s, o: (0, h, 0, 0))
                for count, rows in shares
            ],
            scratch_shapes=[
                pltpu.VMEM((heads, LENGTH, LENGTH), bf16),
                pltpu.VMEM((total * HEAD_DIM + 16, LENGTH), bf16),
                pltpu.VMEM((total * HEAD_DIM + 16, LENGTH), bf16),
                pltpu.VMEM((LENGTH, LENGTH), bf16),
                pltpu.SemaphoreType.DMA((heads, pieces)),
            ],
        ),
        out_shape=[jax.ShapeDtypeStruct((items, group, LENGTH), bf16)] * groups
        + [jax.ShapeDtypeStruct((count, heads, rows, LENGTH), bf16) for count, rows in shares],
        compiler_params=params(),
        cost_estimate=cost(4 * heads * total * 66 * LENGTH * LENGTH, 24 << 20),
        name="mix_back",
    )(lengths, offsets, *grads, *values, *mixed, sums, *parts)
    return outs[:groups], outs[groups:]


def attend_kernel(where, *rest, groups):
    mixed, (x_ref, w_ref, hidden_ref, scaled_ref, scratch) = rest[:groups], rest[groups:]
    spread(scratch, mixed, where[0], mixed[0].shape[1])
    hidden = x_ref[0].astype(f32) + times(scratch[...].T, w_ref[...])
    hidden_ref[0] = hidden
    scaled_ref[0] = (hidden * rms(hidden)).astype(bf16)


def attend(where, mixed, tokens, weight):
    groups = len(mixed)
    items, group, _ = mixed[0].shape
    rows = 512
    tall = pl.BlockSpec((1, rows, WIDTH), lambda i, j, s: (i, j, 0))
    return pl.pallas_call(
        functools.partial(attend_kernel, groups=groups),
        grid_spec=pltpu.PrefetchScalarGridSpec(
            num_scalar_prefetch=1,
            grid=(items, LENGTH // rows),
            in_specs=[pl.BlockSpec((1, group, rows), lambda i, j, s: (i, 0, j))] * groups
            + [tall, pl.BlockSpec((WIDTH, WIDTH), lambda i, j, s: (0, 0))],
            out_specs=[tall, tall],
            scratch_shapes=[pltpu.VMEM((WIDTH, rows), bf16)],
        ),
        out_shape=[
            jax.ShapeDtypeStruct(tokens.shape, f32),
            jax.ShapeDtypeStruct(tokens.shape, bf16),
        ],
        compiler_params=params(),
        cost_estimate=cost(2 * items * LENGTH * WIDTH * WIDTH, 16 << 20),
        name="attend",
    )(where, *mixed, tokens, weight)


FIRST = 0.7978845608028654
SECOND = FIRST * 0.044715


def feed_kernel(scaled_ref, grad_ref, up_ref, down_ref, *rest, carried):
    before, rest = rest[: 2 * carried], rest[2 * carried :]
    out_ref, back_ref, grad_up_ref, grad_down_ref = rest[:4]
    up_turned, down_turned, active, grad_pre, sum_up, sum_down = rest[4:]
    step = pl.program_id(0)
    units = down_ref.shape[0]

    @pl.when(step == 0)
    def _():
        up_turned[...] = up_ref[...].T
        down_turned[...] = down_ref[...].T

    scaled, grad = scaled_ref[...], grad_ref[...]
    slab = 256
    for k in range(units // slab):
        at = pl.ds(k * slab, slab)
        pre = rows_by_rows(up_turned[at, :], scaled)
        grad_active = rows_by_rows(down_ref[at, :], grad)
        square = pre * pre
        half = 0.5 + 0.5 * jnp.tanh(pre * (FIRST + SECOND * square))
        act = pre * half
        active[at, :] = act.astype(bf16)
        slope = half + act * (1.0 - half) * (2.0 * FIRST + 6.0 * SECOND * square)
        grad_pre[at, :] = (grad_active * slope).astype(bf16)
    out = times(down_turned[...], active[...])
    back = times(up_ref[...], grad_pre[...])
    if carried:
        out, back = out + before[0][...], back + before[1][...]
    out_ref[...] = out
    back_ref[...] = back
    down = times(active[...], grad)
    up = times(grad_pre[...], scaled)

    @pl.when(step == 0)
    def _():
        sum_down[...] = down
        sum_up[...] = up

    @pl.when(step > 0)
    def _():
        sum_down[...] += down
        sum_up[...] += up

    @pl.when(step == pl.num_programs(0) - 1)
    def _():
        grad_down_ref[...] = sum_down[...].astype(bf16)
        grad_up_ref[...] = sum_up[...].T.astype(bf16)


def feed(scaled, grad, up, down, before):
    rows = 512
    total = scaled.shape[0]
    units = down.shape[0]
    tall = pl.BlockSpec((rows, WIDTH), lambda j: (j, 0))
    wide = pl.BlockSpec((WIDTH, rows), lambda j: (0, j))
    up_block = pl.BlockSpec((WIDTH, units), lambda j: (0, 0))
    down_block = pl.BlockSpec((units, WIDTH), lambda j: (0, 0))
    return pl.pallas_call(
        functools.partial(feed_kernel, carried=bool(before)),
        grid=(total // rows,),
        in_specs=[tall, tall, up_block, down_block] + [wide] * len(before),
        out_specs=[wide, wide, up_block, down_block],
        scratch_shapes=[
            pltpu.VMEM((units, WIDTH), bf16),
            pltpu.VMEM((WIDTH, units), bf16),
            pltpu.VMEM((units, rows), bf16),
            pltpu.VMEM((units, rows), bf16),
            pltpu.VMEM((units, WIDTH), f32),
            pltpu.VMEM((units, WIDTH), f32),
        ],
        out_shape=[
            jax.ShapeDtypeStruct((WIDTH, total), f32),
            jax.ShapeDtypeStruct((WIDTH, total), f32),
            jax.ShapeDtypeStruct((WIDTH, units), bf16),
            jax.ShapeDtypeStruct((units, WIDTH), bf16),
        ],
        input_output_aliases={4: 0, 5: 1} if before else {},
        compiler_params=params(),
        cost_estimate=cost(12 * total * WIDTH * units, 30 << 20),
        name="feed",
    )(scaled, grad, up, down, *before)


def finish_kernel(where, out_ref, back_ref, hidden_ref, grad_ref, w_ref, *rest, groups):
    mixed, rest = rest[:groups], rest[groups:]
    result_ref, grad_hidden_ref = rest[:2]
    grads, rest = rest[2 : 2 + groups], rest[2 + groups :]
    grad_w_ref, gain_ref, scratch, turned, sum_w, sum_gain = rest
    first = (pl.program_id(0) == 0) & (pl.program_id(1) == 0)
    last = (pl.program_id(0) == pl.num_programs(0) - 1) & (
        pl.program_id(1) == pl.num_programs(1) - 1
    )
    hidden = hidden_ref[0]
    result_ref[0] = (hidden + out_ref[...].T).astype(bf16)
    weighted = back_ref[...].T
    scale = rms(hidden)
    both = weighted * hidden
    mean = jnp.mean(both, axis=-1, keepdims=True)
    grad_hidden = grad_ref[0].astype(f32) + scale * weighted - hidden * (scale**3 * mean)
    attended = grad_hidden.astype(bf16)
    grad_hidden_ref[0] = attended
    gain = jnp.sum(both * scale, axis=0, keepdims=True)
    group = mixed[0].shape[1]
    scratch[...] = rows_by_rows(w_ref[...], attended).astype(bf16)
    pick(scratch, grads, where[0], group)
    spread(turned, mixed, where[0], group)
    part = times(turned[...], attended)

    @pl.when(first)
    def _():
        sum_w[...] = part
        sum_gain[...] = gain

    @pl.when(jnp.logical_not(first))
    def _():
        sum_w[...] += part
        sum_gain[...] += gain

    @pl.when(last)
    def _():
        grad_w_ref[...] = sum_w[...].astype(bf16)
        gain_ref[...] = sum_gain[...]


def finish(where, out, back, hidden, grad, weight, mixed):
    groups = len(mixed)
    items, group, _ = mixed[0].shape
    rows = 512
    steps = LENGTH // rows
    tall = pl.BlockSpec((1, rows, WIDTH), lambda i, j, s: (i, j, 0))
    wide = pl.BlockSpec((WIDTH, rows), lambda i, j, s: (0, i * steps + j))
    square = pl.BlockSpec((WIDTH, WIDTH), lambda i, j, s: (0, 0))
    split = pl.BlockSpec((1, group, rows), lambda i, j, s: (i, 0, j))
    outs = pl.pallas_call(
        functools.partial(finish_kernel, groups=groups),
        grid_spec=pltpu.PrefetchScalarGridSpec(
            num_scalar_prefetch=1,
            grid=(items, steps),
            in_specs=[wide, wide, tall, tall, square] + [split] * groups,
            out_specs=[tall, tall]
            + [split] * groups
            + [square, pl.BlockSpec((1, WIDTH), lambda i, j, s: (0, 0))],
            scratch_shapes=[
                pltpu.VMEM((WIDTH, rows), bf16),
                pltpu.VMEM((WIDTH, rows), bf16),
                pltpu.VMEM((WIDTH, WIDTH), f32),
                pltpu.VMEM((1, WIDTH), f32),
            ],
        ),
        out_shape=[
            jax.ShapeDtypeStruct(grad.shape, bf16),
            jax.ShapeDtypeStruct(grad.shape, bf16),
        ]
        + [jax.ShapeDtypeStruct((items, group, LENGTH), bf16)] * groups
        + [
            jax.ShapeDtypeStruct((WIDTH, WIDTH), bf16),
            jax.ShapeDtypeStruct((1, WIDTH), f32),
        ],
        compiler_params=params(),
        cost_estimate=cost(4 * items * LENGTH * WIDTH * WIDTH, 34 << 20),
        name="finish",
    )(where, out, back, hidden, grad, weight, *mixed)
    return outs[0], outs[1], outs[2 : 2 + groups], outs[2 + groups], outs[3 + groups]


def tokens_kernel(where, x_ref, grad_ref, w_ref, *rest, groups):
    grads, rest = rest[:groups], rest[groups:]
    result_ref, grad_w_ref, gain_ref, turned, sum_w, sum_gain = rest
    first = (pl.program_id(0) == 0) & (pl.program_id(1) == 0)
    last = (pl.program_id(0) == pl.num_programs(0) - 1) & (
        pl.program_id(1) == pl.num_programs(1) - 1
    )
    spread(turned, grads, where[0], grads[0].shape[1])
    x = x_ref[0].astype(f32)
    scale = rms(x)
    scaled = (x * scale).astype(bf16)
    weighted = rows_by_rows(turned[...].T, w_ref[...])
    both = weighted * x
    mean = jnp.mean(both, axis=-1, keepdims=True)
    total = grad_ref[0].astype(f32) + scale * weighted - x * (scale**3 * mean)
    result_ref[0] = total.astype(bf16)
    gain = jnp.sum(both * scale, axis=0, keepdims=True)
    part = times(turned[...], scaled)

    @pl.when(first)
    def _():
        sum_w[...] = part
        sum_gain[...] = gain

    @pl.when(jnp.logical_not(first))
    def _():
        sum_w[...] += part
        sum_gain[...] += gain

    @pl.when(last)
    def _():
        grad_w_ref[...] = sum_w[...].T.astype(bf16)
        gain_ref[...] = sum_gain[...]


def grad_tokens_of(where, tokens, grad_hidden, weight, grads):
    groups = len(grads)
    items, group, _ = grads[0].shape
    rows = 512
    tall = pl.BlockSpec((1, rows, WIDTH), lambda i, j, s: (i, j, 0))
    square = pl.BlockSpec((WIDTH, WIDTH), lambda i, j, s: (0, 0))
    return pl.pallas_call(
        functools.partial(tokens_kernel, groups=groups),
        grid_spec=pltpu.PrefetchScalarGridSpec(
            num_scalar_prefetch=1,
            grid=(items, LENGTH // rows),
            in_specs=[tall, tall, square]
            + [pl.BlockSpec((1, group, rows), lambda i, j, s: (i, 0, j))] * groups,
            out_specs=[tall, square, pl.BlockSpec((1, WIDTH), lambda i, j, s: (0, 0))],
            scratch_shapes=[
                pltpu.VMEM((WIDTH, rows), bf16),
                pltpu.VMEM((WIDTH, WIDTH), f32),
                pltpu.VMEM((1, WIDTH), f32),
            ],
        ),
        out_shape=[
            jax.ShapeDtypeStruct(tokens.shape, bf16),
            jax.ShapeDtypeStruct((WIDTH, WIDTH), bf16),
            jax.ShapeDtypeStruct((1, WIDTH), f32),
        ],
        compiler_params=params(),
        cost_estimate=cost(4 * items * LENGTH * WIDTH * WIDTH, 14 << 20),
        name="grad_tokens",
    )(where, tokens, grad_hidden, weight, *grads)


ALL = ("dp", "seq")


def exchange(parts):
    got = [parts[0]]
    for r in range(1, len(parts)):
        got.append(lax.ppermute(parts[r], "dp", [(i, i ^ r) for i in range(len(parts))]))
    return got


def body(tokens, lengths, mixer, gain_one, gain_two, w_value, w_out, w_up, w_down, cotangent, groups, seqs):
    ranks = groups * seqs
    here, row = lax.axis_index("dp"), lax.axis_index("seq")
    where = jnp.stack([here, row]).astype(jnp.int32)
    items = tokens.shape[0]
    shard = w_value.shape[0]
    slices = HIDDEN // WIDTH

    first_gain = gain_one.astype(f32)[:, None]
    second_gain = gain_two.astype(f32)[:, None]
    value_mine = (w_value.astype(f32) * first_gain).astype(bf16)
    up_mine = (w_up.astype(f32) * second_gain).astype(bf16)

    value_all = lax.all_gather(value_mine, ALL, axis=0, tiled=True)
    packed = jnp.concatenate([w_out, up_mine.reshape(shard * slices, WIDTH), w_down], axis=0)
    gathered = lax.all_gather(packed, ALL, axis=0, tiled=False)
    out_all = gathered[:, :shard].reshape(WIDTH, WIDTH)
    up_all = jnp.moveaxis(
        gathered[:, shard : shard * (1 + slices)].reshape(WIDTH, slices, WIDTH), 1, 0
    )
    down_all = gathered[:, shard * (1 + slices) :].reshape(slices, WIDTH, WIDTH)

    logits = jnp.exp(mixer.astype(f32))
    logits_low = logits.astype(bf16)
    logits_parts = [lax.all_gather(logits_low, "seq", axis=1, tiled=True)]
    shares = ((1, LENGTH),)
    offsets = jnp.zeros((2,), jnp.int32)

    lengths_here = jnp.concatenate(exchange([lengths] * groups))
    values = exchange(project_values(where, tokens, value_all, groups))
    mixed_out, sums = mix_items(lengths_here, offsets, values, logits_parts)
    mixed = exchange(mixed_out)
    hidden, scaled = attend(where, mixed, tokens, out_all)

    scaled_flat = scaled.reshape(items * LENGTH, WIDTH)
    grad_flat = cotangent.reshape(items * LENGTH, WIDTH)
    before = ()
    ups, downs = [], []
    for k in range(slices):
        out, back, grad_up, grad_down = feed(scaled_flat, grad_flat, up_all[k], down_all[k], before)
        before = (out, back)
        ups.append(grad_up)
        downs.append(grad_down)
    result, grad_hidden, grads_out, grad_out_w, gain_two_sum = finish(
        where, before[0], before[1], hidden, cotangent, out_all, mixed
    )
    grads = exchange(grads_out)
    back_values, grad_logits = mix_back(
        lengths_here, offsets, grads, values, mixed_out, sums, logits_parts, shares
    )
    grad_mixer = lax.psum_scatter(grad_logits[0][0], "seq", scatter_dimension=1, tiled=True)
    grad_mixer = grad_mixer.astype(f32) * logits
    grad_values = exchange(back_values)
    grad_tokens, grad_value_w, gain_one_sum = grad_tokens_of(
        where, tokens, grad_hidden, value_all, grad_values
    )

    gains = jnp.concatenate(
        [gain_one_sum.reshape(ranks, 1, shard), gain_two_sum.reshape(ranks, 1, shard)], axis=2
    )
    gains = jnp.pad(gains, ((0, 0), (0, 7), (0, WIDTH - 2 * shard))).astype(bf16)
    payload = jnp.concatenate(
        [
            grad_out_w.reshape(ranks, shard, WIDTH),
            jnp.stack([u.reshape(ranks, shard, WIDTH) for u in ups], axis=2).reshape(
                ranks, shard * slices, WIDTH
            ),
            jnp.stack(downs).reshape(ranks, shard * slices, WIDTH),
            grad_value_w.reshape(ranks, shard, WIDTH),
            gains,
        ],
        axis=1,
    )
    payload = lax.psum_scatter(payload, ALL, scatter_dimension=0, tiled=False).astype(f32)
    at = shard
    sum_out = payload[:at]
    sum_up = payload[at : at + shard * slices].reshape(shard, HIDDEN) * second_gain
    at += shard * slices
    sum_down = payload[at : at + shard * slices]
    at += shard * slices
    sum_value = payload[at : at + shard] * first_gain
    at += shard
    sum_gain_one = payload[at, :shard] / first_gain[:, 0]
    sum_gain_two = payload[at, shard : 2 * shard] / second_gain[:, 0]
    return (
        result,
        grad_tokens,
        grad_mixer,
        sum_gain_one,
        sum_gain_two,
        sum_value,
        sum_out,
        sum_up,
        sum_down,
    )


def solution(mesh):
    rows = P(ALL, None)
    line = P(ALL)
    cube = P(ALL, None, None)
    logits = P("dp", "seq", None)
    return jax.shard_map(
        functools.partial(body, groups=mesh.shape["dp"], seqs=mesh.shape["seq"]),
        mesh=mesh,
        in_specs=(cube, line, logits, line, line, rows, rows, rows, rows, cube),
        out_specs=(cube, cube, logits, line, line, rows, rows, rows, rows),
        check_vma=False,
    )
```

time: 1740 us -> 704 us (0.40)
  waiting for transfers between devices: 976 us -> 394 us
  matrix products: 364 us -> 0 us
  Pallas kernels: 0 us -> 175 us
  other arithmetic: 178 us -> 30.6 us
  blocking collectives: 78.7 us -> 0 us
  local copies, waits for them, and re-layouts: 119 us -> 61.9 us
    reduce_scatter x5 -> x2, waiting for transfers between devices: 423 us -> 147 us  [the longest x1 147 us: body(): lax.psum_scatter(payload, ALL, scatter_dimension=0, tiled=False).astype(f32)]
    dot_general x16 -> x0, matrix products: 241 us -> none  [the longest x2 37.8 us: single(): jnp.einsum('hij,jhd->ihd', probs, split, preferred_element_type=jnp.float32)]
    unnamed x13 -> x5, waiting for transfers between devices: 224 us -> 0.08 us
    all_gather x6 -> x3, waiting for transfers between devices: 329 us -> 153 us  [the longest x1 87.3 us: body(): gathered = lax.all_gather(packed, ALL, axis=0, tiled=False)]
    pallas_call x0 -> x10, Pallas kernels: none -> 175 us  [the longest x4 100 us: feed(): pl.pallas_call(functools.partial(feed_kernel, carried=bool(before)), grid...]
    sub x4 -> x0, other arithmetic: 160 us -> none  [softmax_rows(): expos = jnp.where(keep_keys, jnp.exp(masked - top), 0.0)]
    sub x2 -> x0, matrix products: 123 us -> none  [single(): grad_probs - jnp.sum(probs * grad_probs, axis=2, keepdims=True)]
    ppermute x0 -> x15, waiting for transfers between devices: none -> 93.8 us  [exchange(): lax.ppermute(parts[r], 'dp', [(i, i ^ r) for i in range(len(parts))])]
  transfers between devices with their start and end apart: 12 -> 20, of which waited for: 9 -> 10; matrix products, arithmetic and copies ran while one was open for 15% -> 11% of each run, Pallas kernels for 0% -> 4%
where the time goes in v1:
time: 704 us; the launch traced here: 694 us
  waiting for transfers between devices  394 us (56%)
  Pallas kernels  175 us (25%)
  local copies, waits for them, and re-layouts  61.9 us (9%)
  other arithmetic  30.6 us (4%)
  starting transfers between devices  18.1 us (3%)
  between operations  14.7 us (2%)
    reduce_scatter x1, waiting for transfers between devices, body(): lax.psum_scatter(payload, ALL, scatter_dimension=0, tiled=False).astype(f32)  147 us
    pallas_call x4, Pallas kernels, feed(): pl.pallas_call(functools.partial(feed_kernel, carried=bool(before)), grid...  100 us
    ppermute x15, waiting for transfers between devices, exchange(): lax.ppermute(parts[r], 'dp', [(i, i ^ r) for i in range(len(parts))])  93.8 us
    all_gather x1, waiting for transfers between devices, body(): gathered = lax.all_gather(packed, ALL, axis=0, tiled=False)  87.3 us
    all_gather x1, waiting for transfers between devices, body(): value_all = lax.all_gather(value_mine, ALL, axis=0, tiled=True)  51.6 us
    pallas_call x1, Pallas kernels, finish(): pl.pallas_call(functools.partial(finish_kernel, groups=groups), grid_spec...  18.9 us
    ppermute x15, starting transfers between devices, exchange(): lax.ppermute(parts[r], 'dp', [(i, i ^ r) for i in range(len(parts))])  17.7 us
    unnamed x72, local copies, waits for them, and re-layouts  16.1 us
  transfers between devices with their start and end apart: 20, of which 10 were waited for; matrix products, arithmetic and copies ran while one was open for 11% of the time, Pallas kernels for 4%

profile of v1, /device:TPU:0, one launch (start us, length us, event | category | flops | bytes accessed | tf_op | source)
XLA Modules:
  0.0 694.0 jit_solution(1555541840945444776)
XLA Ops:
  8.4 1.5 multiply_convert_fusion.1
  9.9 2.3 fusion
  14.6 1.7 pad_maximum_fusion.2
  16.9 51.6 %all-gather.5.cloned.1.call-done.w_ref = bf16[768,768]{1,0:T(8,128)(2,1)} async-done(((bf16[24,768]{1,0:T(8,128)(2,1)}), bf16[768,768]{1,0:T(8,128)(2,1)}) %all-gather.5.cloned.1.call-update) | async-done | bytes 1179664 | tf_op jit(solution)/shard_map/all_gather | solution.py:534
  68.5 8.0 %project_values.1 = (bf16[2,192,1024]{2,1,0:T(8,128)(2,1)}, bf16[2,192,1024]{2,1,0:T(8,128)(2,1)}, bf16[2,192,1024]{2,1,0:T(8,128)(2,1)}, bf16[2,192,1024]{2,1,0:T(8,128)(2,1)}) custom-call(s32[2]{0:T(128)} %pad_add_fusion.where, bf16[2,1024,768]{2,1,0:T(8,128)(2,1)} %x_ref.3, bf16[768,768]{1,0:T(8,128)(2,1)} %all-gather.5.cloned.1.call-done.w_ref), custom_call_target="tpu_custom_call" | custom-call | flops 2415919104 | bytes 6291456 | tf_op jit(solution)/shard_map/project_values/pallas_call | solution.py:71
  78.5 1.5 collective-permute-start.5
  80.0 1.5 collective-permute-start.1
  82.0 32.5 %collective-permute-done.1 = s32[2]{0:T(128)S(1)} collective-permute-done((s32[2]{0:T(128)S(1)}, s32[2]{0:T(128)S(1)}, u32[]{:S(2)}, u32[]{:S(2)}) %collective-permute-start.1) | collective-permute-done | bytes 40 | tf_op jit(solution)/shard_map/ppermute | solution.py:517
  114.5 1.5 collective-permute-start.2
  116.0 2.9 collective-permute-done.2
  119.6 14.2 %all-gather.7.cloned.1.call-done.rest_4_.rest_13_ = bf16[3,1024,1024]{2,1,0:T(8,128)(2,1)} async-done(((bf16[3,128,1024]{2,1,0:T(8,128)(2,1)}), bf16[3,1024,1024]{2,1,0:T(8,128)(2,1)}) %all-gather.7.cloned.1.call-update) | async-done | bytes 6291472 | tf_op jit(solution)/shard_map/all_gather | solution.py:545
  134.3 9.4 %mix_items.1 = (bf16[2,192,1024]{2,1,0:T(8,128)(2,1)}, bf16[2,192,1024]{2,1,0:T(8,128)(2,1)}, bf16[2,192,1024]{2,1,0:T(8,128)(2,1)}, bf16[2,192,1024]{2,1,0:T(8,128)(2,1)}, f32[3,8,1024]{2,1,0:T(8,128)}) custom-call(s32[8]{0:T(128)} %pad_add_fusion.1.lengths, s32[2]{0:T(128)} %broadcast_1_offsets.2.offsets, ...), custom_call_target="tpu_custom_call" | custom-call | flops 3321888768 | bytes 12582912 | tf_op jit(solution)/shard_map/mix_items/pallas_call | solution.py:143
  143.7 1.5 collective-permute-start.6
  145.3 1.5 collective-permute-start.7
  147.3 87.3 %all-gather.9.cloned.1.call-done = bf16[6912,768]{1,0:T(8,128)(2,1)} async-done(((bf16[216,768]{1,0:T(8,128)(2,1)}), bf16[6912,768]{1,0:T(8,128)(2,1)}) %all-gather.9.cloned.1.call-update) | async-done | bytes 10616848 | tf_op jit(solution)/shard_map/all_gather | solution.py:536
  234.6 2.4 slice.86
  236.9 4.8 slice.87
  241.7 8.9 %reshape.77 = bf16[768,4,768]{2,1,0:T(4,128)(2,1)} reshape(bf16[32,96,768]{2,1,0:T(8,128)(2,1)} %slice.87) | data formatting | bytes 9437184 | tf_op jit(solution)/shard_map/reshape | solution.py:539
  250.6 2.9 copy.37
  253.6 4.6 fusion.11
  258.2 2.3 slice_bitcast_fusion
  261.9 10.1 %attend.1 = (f32[2,1024,768]{2,1,0:T(8,128)}, bf16[2,1024,768]{2,1,0:T(8,128)(2,1)}) custom-call(s32[2]{0:T(128)} %pad_add_fusion.where, bf16[2,192,1024]{2,1,0:T(8,128)(2,1)} %get-tuple-element.56.rest_0_.rest_8_, bf16[2,192,1024]{2,1,0:T(8,128)(2,1)} %copy-done.11, bf16[2,192,1024]{2,1,0:T(8,128)(2,1)} %copy-done.12, bf16[2,192,1024]{2,1,0:T(8,128)(2,1)} %copy-done.13, ...), custom_call_target="tpu_custom_call" | custom-call | flops 2415919104 | bytes 16777216 | tf_op jit(solution)/shard_map/attend/pallas_call | solution.py:256
  272.0 23.8 %feed.4 = (f32[768,2048]{1,0:T(8,128)}, f32[768,2048]{1,0:T(8,128)}, bf16[768,768]{1,0:T(8,128)(2,1)}, bf16[768,768]{1,0:T(8,128)(2,1)}) custom-call(bf16[2048,768]{1,0:T(8,128)(2,1)} %bitcast.77, bf16[2048,768]{1,0:T(8,128)(2,1)} %bitcast.59, bf16[768,768]{1,0:T(8,128)(2,1)} %get-tuple-element.99.up_ref, bf16[768,768]{1,0:T(8,128)(2,1)} %bitcast.70), custom_call_target="tpu_custom_call" | custom-call | flops 14495514624 | bytes 31457280 | tf_op jit(solution)/shard_map/feed/pallas_call | solution.py:337
  295.8 25.8 %feed.5 = (f32[768,2048]{1,0:T(8,128)}, f32[768,2048]{1,0:T(8,128)}, bf16[768,768]{1,0:T(8,128)(2,1)}, bf16[768,768]{1,0:T(8,128)(2,1)}) custom-call(bf16[2048,768]{1,0:T(8,128)(2,1)} %bitcast.78, bf16[2048,768]{1,0:T(8,128)(2,1)} %bitcast.60, bf16[768,768]{1,0:T(8,128)(2,1)} %get-tuple-element.100.up_ref, ...), custom_call_target="tpu_custom_call", output_to_operand_aliasing={{0}: (4, {}), {1}: (5, {})} | custom-call | flops 14495514624 | bytes 31457280 | tf_op jit(solution)/shard_map/feed/pallas_call | solution.py:337
  321.6 25.2 %feed.6 = (f32[768,2048]{1,0:T(8,128)}, f32[768,2048]{1,0:T(8,128)}, bf16[768,768]{1,0:T(8,128)(2,1)}, bf16[768,768]{1,0:T(8,128)(2,1)}) custom-call(bf16[2048,768]{1,0:T(8,128)(2,1)} %bitcast.79, bf16[2048,768]{1,0:T(8,128)(2,1)} %bitcast.61, bf16[768,768]{1,0:T(8,128)(2,1)} %get-tuple-element.101.up_ref, ...), custom_call_target="tpu_custom_call", output_to_operand_aliasing={{0}: (4, {}), {1}: (5, {})} | custom-call | flops 14495514624 | bytes 31457280 | tf_op jit(solution)/shard_map/feed/pallas_call | solution.py:337
  346.8 25.5 %feed.7 = (f32[768,2048]{1,0:T(8,128)}, f32[768,2048]{1,0:T(8,128)}, bf16[768,768]{1,0:T(8,128)(2,1)}, bf16[768,768]{1,0:T(8,128)(2,1)}) custom-call(bf16[2048,768]{1,0:T(8,128)(2,1)} %bitcast.80, bf16[2048,768]{1,0:T(8,128)(2,1)} %bitcast.62, bf16[768,768]{1,0:T(8,128)(2,1)} %get-tuple-element.102.up_ref, ...), custom_call_target="tpu_custom_call", output_to_operand_aliasing={{0}: (4, {}), {1}: (5, {})} | custom-call | flops 14495514624 | bytes 31457280 | tf_op jit(solution)/shard_map/feed/pallas_call | solution.py:337
  372.3 18.9 %finish.1 = (bf16[2,1024,768]{2,1,0:T(8,128)(2,1)}, bf16[2,1024,768]{2,1,0:T(8,128)(2,1)}, bf16[2,192,1024]{2,1,0:T(8,128)(2,1)}, bf16[2,192,1024]{2,1,0:T(8,128...) custom-call(s32[2]{0:T(128)} %pad_add_fusion.where, ...), custom_call_target="tpu_custom_call" | custom-call | flops 4831838208 | bytes 35651584 | tf_op jit(solution)/shard_map/finish/pallas_call | solution.py:413
  391.2 1.5 collective-permute-start.9
  393.3 1.4 collective-permute-start.11
  394.8 17.1 %collective-permute-done.9.rest_1_ = bf16[2,192,1024]{2,1,0:T(8,128)(2,1)S(1)} collective-permute-done((bf16[2,192,1024]{2,1,0:T(8,128)(2,1)}, bf16[2,192,1024]{2,1,0:T(8,128)(2,1)S(1)}, u32[]{:S(2)}, u32[]{:S(2)}) %collective-permute-start.9) | collective-permute-done | bytes 786464 | tf_op jit(solution)/shard_map/ppermute | solution.py:517
  411.9 17.3 %collective-permute-done.10.rest_2_ = bf16[2,192,1024]{2,1,0:T(8,128)(2,1)S(1)} collective-permute-done((bf16[2,192,1024]{2,1,0:T(8,128)(2,1)}, bf16[2,192,1024]{2,1,0:T(8,128)(2,1)S(1)}, u32[]{:S(2)}, u32[]{:S(2)}) %collective-permute-start.10) | collective-permute-done | bytes 786464 | tf_op jit(solution)/shard_map/ppermute | solution.py:517
  430.4 15.5 %mix_back.1 = (bf16[2,192,1024]{2,1,0:T(8,128)(2,1)}, bf16[2,192,1024]{2,1,0:T(8,128)(2,1)}, bf16[2,192,1024]{2,1,0:T(8,128)(2,1)}, bf16[2,192,1024]{2,1,0:T(8,128)(2,1)}, bf16[1,3,1024,1024]{3,2,1,0:T(8,128)(2,1)}) custom-call(s32[8]{0:T(128)} %pad_add_fusion.1.lengths, s32[2]{0:T(128)} %broadcast_1_offsets.2.offsets, ...), custom_call_target="tpu_custom_call" | custom-call | flops 6643777536 | bytes 25165824 | tf_op jit(solution)/shard_map/mix_back/pallas_call | solution.py:213
  448.0 1.8 copy.33
  449.8 1.8 copy.32
  451.6 1.8 copy.31
  453.5 1.8 copy.30
  455.3 13.2 %pad_maximum_fusion = bf16[32,24,4,768]{3,2,1,0:T(4,128)(2,1)} fusion(bf16[32,24,1,768]{3,2,1,0:T(2,128)(2,1)S(1)} %copy.33, bf16[32,24,1,768]{3,2,1,0:T(2,128)(2,1)S(1)} %copy.32, bf16[32,24,1,768]{3,2,1,0:T(2,128)(2,1)S(1)} %copy.31, bf16[32,24,1,768]{3,2,1,0:T(2,128)(2,1)S(1)} %copy.30), kind=kLoop, calls=%fused_computation | loop fusion | flops 18874368 | bytes 9437184 | tf_op jit(solution)/shard_map/stack | solution.py:585
  468.5 8.8 %reshape.79 = bf16[32,96,768]{2,1,0:T(8,128)(2,1)} reshape(bf16[32,24,4,768]{3,2,1,0:T(4,128)(2,1)} %pad_maximum_fusion) | data formatting | bytes 9437184 | tf_op jit(solution)/shard_map/reshape | solution.py:585
  478.0 1.5 collective-permute-start.13
  479.5 1.5 collective-permute-start.14
  481.0 2.7 constant_dynamic-update-slice_fusion.2
  484.7 4.4 copy-done
  489.1 8.8 %collective-permute-done.12.rest_1_ = bf16[2,192,1024]{2,1,0:T(8,128)(2,1)S(1)} collective-permute-done((bf16[2,192,1024]{2,1,0:T(8,128)(2,1)S(1)}, bf16[2,192,1024]{2,1,0:T(8,128)(2,1)S(1)}, u32[]{:S(2)}, u32[]{:S(2)}) %collective-permute-start.12) | collective-permute-done | bytes 786464 | tf_op jit(solution)/shard_map/ppermute | solution.py:517
  497.9 15.1 %collective-permute-done.13.rest_2_ = bf16[2,192,1024]{2,1,0:T(8,128)(2,1)S(1)} collective-permute-done((bf16[2,192,1024]{2,1,0:T(8,128)(2,1)S(1)}, bf16[2,192,1024]{2,1,0:T(8,128)(2,1)S(1)}, u32[]{:S(2)}, u32[]{:S(2)}) %collective-permute-start.13) | collective-permute-done | bytes 786464 | tf_op jit(solution)/shard_map/ppermute | solution.py:517
  514.2 12.4 %grad_tokens.1 = (bf16[2,1024,768]{2,1,0:T(8,128)(2,1)}, bf16[768,768]{1,0:T(8,128)(2,1)}, f32[1,768]{1,0:T(1,128)}) custom-call(s32[2]{0:T(128)} %pad_add_fusion.where, bf16[2,1024,768]{2,1,0:T(8,128)(2,1)} %x_ref.3, bf16[2,1024,768]{2,1,0:T(8,128)(2,1)} %get-tuple-element.71.grad_ref, bf16[768,768]{1,0:T(8,128)(2,1)} %all-gather.5.cloned.1.call-done.w_ref, ...), custom_call_target="tpu_custom_call" | custom-call | flops 4831838208 | bytes 14680064 | tf_op jit(solution)/shard_map/grad_tokens/pallas_call | solution.py:486
  527.4 2.4 constant_dynamic-update-slice_fusion
  531.8 2.6 convert_multiply_fusion
  534.3 147.1 %reduce-scatter.5.cloned.1.call-done = bf16[1,248,768]{2,1,0:T(8,128)(2,1)} async-done(((bf16[32,248,768]{2,1,0:T(8,128)(2,1)}), bf16[1,248,768]{2,1,0:T(8,128)(2,1)}) %reduce-scatter.5.cloned.1.call-update) | async-done | bytes 380944 | tf_op jit(solution)/shard_map/reduce_scatter | solution.py:594
  (116 shorter events, 24.9 us)
Async XLA Ops:
  7.2 61.3 %all-gather.5.cloned.1.call-start = ((), (), s32[]{:S(2)}) async-start(), calls=%async_computation.2 | async-start | bytes 1216512 | tf_op jit(solution)/shard_map/all_gather | solution.py:534
  9.9 123.9 %all-gather.7.cloned.1.call-start = ((), (), s32[]{:S(2)}) async-start(), calls=%async_computation.3 | async-start | bytes 7077888 | tf_op jit(solution)/shard_map/all_gather | solution.py:545
  12.2 222.4 %all-gather.9.cloned.1.call-start = ((), (), s32[]{:S(2)}) async-start(), calls=%async_computation.6 | async-start | bytes 10948608 | tf_op jit(solution)/shard_map/all_gather | solution.py:536
  16.2 63.8 %copy-start.19 = (s32[2]{0:T(128)S(1)}, s32[2]{0:T(128)}, u32[]{:S(2)}) copy-start(s32[2]{0:T(128)} %param.11) | copy-start | bytes 28
  16.3 514.5 %reduce-scatter.3.cloned.1.call-start = ((), (), s32[]{:S(2)}) async-start(), calls=%async_computation.4 | async-start | bytes 7077888 | tf_op jit(solution)/shard_map/reduce_scatter | solution.py:571
  76.5 43.0 %collective-permute-start.3 = (bf16[2,192,1024]{2,1,0:T(8,128)(2,1)}, bf16[2,192,1024]{2,1,0:T(8,128)(2,1)S(1)}, u32[]{:S(2)}, u32[]{:S(2)}) collective-permute-start(bf16[2,192,1024]{2,1,0:T(8,128)(2,1)} %get-tuple-element.53), channel_id=1, source_target_pairs={{0,8},{8,0},{16,24},{24,16},{1,9},{9,1},{17,25},{25,17},{2,10},{10... | collective-permute-start | bytes 2359304 | tf_op jit(solution)/shard_map/ppermute | solution.py:517
  77.9 41.6 %collective-permute-start.4 = (bf16[2,192,1024]{2,1,0:T(8,128)(2,1)}, bf16[2,192,1024]{2,1,0:T(8,128)(2,1)S(1)}, u32[]{:S(2)}, u32[]{:S(2)}) collective-permute-start(bf16[2,192,1024]{2,1,0:T(8,128)(2,1)} %get-tuple-element.54), channel_id=1, source_target_pairs={{0,16},{8,24},{16,0},{24,8},{1,17},{9,25},{17,1},{25,9},{2,18},{10... | collective-permute-start | bytes 2359304 | tf_op jit(solution)/shard_map/ppermute | solution.py:517
  78.5 41.1 %collective-permute-start.5 = (bf16[2,192,1024]{2,1,0:T(8,128)(2,1)}, bf16[2,192,1024]{2,1,0:T(8,128)(2,1)S(1)}, u32[]{:S(2)}, u32[]{:S(2)}) collective-permute-start(bf16[2,192,1024]{2,1,0:T(8,128)(2,1)} %get-tuple-element.55), channel_id=1, source_target_pairs={{0,24},{8,16},{16,8},{24,0},{1,25},{9,17},{17,9},{25,1},{2,26},{10... | collective-permute-start | bytes 2359304 | tf_op jit(solution)/shard_map/ppermute | solution.py:517
  80.0 34.5 %collective-permute-start.1 = (s32[2]{0:T(128)S(1)}, s32[2]{0:T(128)S(1)}, u32[]{:S(2)}, u32[]{:S(2)}) collective-permute-start(s32[2]{0:T(128)S(1)} %copy-done.19), channel_id=1, source_target_pairs={{0,16},{8,24},{16,0},{24,8},{1,17},{9,25},{17,1},{25,9},{2,18},{10... | collective-permute-start | bytes 32 | tf_op jit(solution)/shard_map/ppermute | solution.py:517
  81.5 34.5 %collective-permute-start = (s32[2]{0:T(128)S(1)}, s32[2]{0:T(128)S(1)}, u32[]{:S(2)}, u32[]{:S(2)}) collective-permute-start(s32[2]{0:T(128)S(1)} %copy-done.19), channel_id=1, source_target_pairs={{0,8},{8,0},{16,24},{24,16},{1,9},{9,1},{17,25},{25,17},{2,10},{10... | collective-permute-start | bytes 32 | tf_op jit(solution)/shard_map/ppermute | solution.py:517
  114.5 4.4 collective-permute-start.2
  119.6 14.8 %copy-start.22 = (bf16[2,192,1024]{2,1,0:T(8,128)(2,1)}, bf16[2,192,1024]{2,1,0:T(8,128)(2,1)S(1)}, u32[]{:S(2)}) copy-start(bf16[2,192,1024]{2,1,0:T(8,128)(2,1)S(1)} %collective-permute-done.3.rest_1_.rest_5_) | copy-start | bytes 2359300
  119.6 14.8 %copy-start.23 = (bf16[2,192,1024]{2,1,0:T(8,128)(2,1)}, bf16[2,192,1024]{2,1,0:T(8,128)(2,1)S(1)}, u32[]{:S(2)}) copy-start(bf16[2,192,1024]{2,1,0:T(8,128)(2,1)S(1)} %collective-permute-done.4.rest_2_.rest_6_) | copy-start | bytes 2359300
  119.6 14.7 %copy-start.24 = (bf16[2,192,1024]{2,1,0:T(8,128)(2,1)}, bf16[2,192,1024]{2,1,0:T(8,128)(2,1)S(1)}, u32[]{:S(2)}) copy-start(bf16[2,192,1024]{2,1,0:T(8,128)(2,1)S(1)} %collective-permute-done.5.rest_3_.rest_7_) | copy-start | bytes 2359300
  143.7 116.7 %collective-permute-start.6 = (bf16[2,192,1024]{2,1,0:T(8,128)(2,1)}, bf16[2,192,1024]{2,1,0:T(8,128)(2,1)S(1)}, u32[]{:S(2)}, u32[]{:S(2)}) collective-permute-start(bf16[2,192,1024]{2,1,0:T(8,128)(2,1)} %get-tuple-element.57.rest_9_), channel_id=1, source_target_pairs={{0,8},{8,0},{16,24},{24,16},{1,9},{9,1},{17,25},{25,17},{2,10},{10... | collective-permute-start | bytes 2359304 | tf_op jit(solution)/shard_map/ppermute | solution.py:517
  145.3 115.2 %collective-permute-start.7 = (bf16[2,192,1024]{2,1,0:T(8,128)(2,1)}, bf16[2,192,1024]{2,1,0:T(8,128)(2,1)S(1)}, u32[]{:S(2)}, u32[]{:S(2)}) collective-permute-start(bf16[2,192,1024]{2,1,0:T(8,128)(2,1)} %get-tuple-element.58.rest_10_), channel_id=1, source_target_pairs={{0,16},{8,24},{16,0},{24,8},{1,17},{9,25},{17,1},{25,9},{2,18},{10... | collective-permute-start | bytes 2359304 | tf_op jit(solution)/shard_map/ppermute | solution.py:517
  146.8 113.7 %collective-permute-start.8 = (bf16[2,192,1024]{2,1,0:T(8,128)(2,1)}, bf16[2,192,1024]{2,1,0:T(8,128)(2,1)S(1)}, u32[]{:S(2)}, u32[]{:S(2)}) collective-permute-start(bf16[2,192,1024]{2,1,0:T(8,128)(2,1)} %get-tuple-element.59.rest_11_), channel_id=1, source_target_pairs={{0,24},{8,16},{16,8},{24,0},{1,25},{9,17},{17,9},{25,1},{2,26},{10... | collective-permute-start | bytes 2359304 | tf_op jit(solution)/shard_map/ppermute | solution.py:517
  260.5 1.1 copy-start.12
  260.5 1.4 copy-start.13
  391.2 20.6 %collective-permute-start.9 = (bf16[2,192,1024]{2,1,0:T(8,128)(2,1)}, bf16[2,192,1024]{2,1,0:T(8,128)(2,1)S(1)}, u32[]{:S(2)}, u32[]{:S(2)}) collective-permute-start(bf16[2,192,1024]{2,1,0:T(8,128)(2,1)} %get-tuple-element.73), channel_id=1, source_target_pairs={{0,8},{8,0},{16,24},{24,16},{1,9},{9,1},{17,25},{25,17},{2,10},{10... | collective-permute-start | bytes 2359304 | tf_op jit(solution)/shard_map/ppermute | solution.py:517
  392.7 36.5 %collective-permute-start.10 = (bf16[2,192,1024]{2,1,0:T(8,128)(2,1)}, bf16[2,192,1024]{2,1,0:T(8,128)(2,1)S(1)}, u32[]{:S(2)}, u32[]{:S(2)}) collective-permute-start(bf16[2,192,1024]{2,1,0:T(8,128)(2,1)} %get-tuple-element.74), channel_id=1, source_target_pairs={{0,16},{8,24},{16,0},{24,8},{1,17},{9,25},{17,1},{25,9},{2,18},{10... | collective-permute-start | bytes 2359304 | tf_op jit(solution)/shard_map/ppermute | solution.py:517
  393.3 35.9 %collective-permute-start.11 = (bf16[2,192,1024]{2,1,0:T(8,128)(2,1)}, bf16[2,192,1024]{2,1,0:T(8,128)(2,1)S(1)}, u32[]{:S(2)}, u32[]{:S(2)}) collective-permute-start(bf16[2,192,1024]{2,1,0:T(8,128)(2,1)} %get-tuple-element.75), channel_id=1, source_target_pairs={{0,24},{8,16},{16,8},{24,0},{1,25},{9,17},{17,9},{25,1},{2,26},{10... | collective-permute-start | bytes 2359304 | tf_op jit(solution)/shard_map/ppermute | solution.py:517
  411.9 17.3 %copy-start.30 = (bf16[2,192,1024]{2,1,0:T(8,128)(2,1)}, bf16[2,192,1024]{2,1,0:T(8,128)(2,1)S(1)}, u32[]{:S(2)}) copy-start(bf16[2,192,1024]{2,1,0:T(8,128)(2,1)S(1)} %collective-permute-done.9.rest_1_) | copy-start | bytes 2359300
  429.2 1.2 copy-start.33
  445.9 2.1 copy-start.9
  445.9 3.9 copy-start.8
  445.9 5.7 copy-start.7
  445.9 235.5 %reduce-scatter.5.cloned.1.call-start = ((), (), s32[]{:S(2)}) async-start(), calls=%async_computation.5 | async-start | bytes 12570624 | tf_op jit(solution)/shard_map/reduce_scatter | solution.py:594
  447.9 5.5 copy-start.6
  468.5 8.8 %copy-start.10 = (bf16[768,768]{1,0:T(8,128)(2,1)S(1)}, bf16[768,768]{1,0:T(8,128)(2,1)}, u32[]{:S(2)}) copy-start(bf16[768,768]{1,0:T(8,128)(2,1)} %get-tuple-element.83) | copy-start | bytes 3538948
  468.5 8.8 %copy-start.27 = (bf16[2,192,1024]{2,1,0:T(8,128)(2,1)S(1)}, bf16[2,192,1024]{2,1,0:T(8,128)(2,1)}, u32[]{:S(2)}) copy-start(bf16[2,192,1024]{2,1,0:T(8,128)(2,1)} %get-tuple-element.78) | copy-start | bytes 2359300
  468.5 9.5 %copy-start.26 = (bf16[2,192,1024]{2,1,0:T(8,128)(2,1)S(1)}, bf16[2,192,1024]{2,1,0:T(8,128)(2,1)}, u32[]{:S(2)}) copy-start(bf16[2,192,1024]{2,1,0:T(8,128)(2,1)} %get-tuple-element.79) | copy-start | bytes 2359300
  468.5 11.0 %copy-start.25 = (bf16[2,192,1024]{2,1,0:T(8,128)(2,1)S(1)}, bf16[2,192,1024]{2,1,0:T(8,128)(2,1)}, u32[]{:S(2)}) copy-start(bf16[2,192,1024]{2,1,0:T(8,128)(2,1)} %get-tuple-element.80) | copy-start | bytes 2359300
  477.3 20.5 %collective-permute-start.12 = (bf16[2,192,1024]{2,1,0:T(8,128)(2,1)S(1)}, bf16[2,192,1024]{2,1,0:T(8,128)(2,1)S(1)}, u32[]{:S(2)}, u32[]{:S(2)}) collective-permute-start(bf16[2,192,1024]{2,1,0:T(8,128)(2,1)S(1)} %copy-done.27), channel_id=1, source_target_pairs={{0,8},{8,0},{16,24},{24,16},{1,9},{9,1},{17,25},{25,17},{2,10},{10... | collective-permute-start | bytes 2359304 | tf_op jit(solution)/shard_map/ppermute | solution.py:517
  478.0 35.0 %collective-permute-start.13 = (bf16[2,192,1024]{2,1,0:T(8,128)(2,1)S(1)}, bf16[2,192,1024]{2,1,0:T(8,128)(2,1)S(1)}, u32[]{:S(2)}, u32[]{:S(2)}) collective-permute-start(bf16[2,192,1024]{2,1,0:T(8,128)(2,1)S(1)} %copy-done.26), channel_id=1, source_target_pairs={{0,16},{8,24},{16,0},{24,8},{1,17},{9,25},{17,1},{25,9},{2,18},{10... | collective-permute-start | bytes 2359304 | tf_op jit(solution)/shard_map/ppermute | solution.py:517
  479.5 4.2 copy-start.2
  479.5 4.2 copy-start.3
  479.5 4.2 copy-start.4
  479.5 4.2 copy-start.5
  479.5 33.5 %collective-permute-start.14 = (bf16[2,192,1024]{2,1,0:T(8,128)(2,1)S(1)}, bf16[2,192,1024]{2,1,0:T(8,128)(2,1)S(1)}, u32[]{:S(2)}, u32[]{:S(2)}) collective-permute-start(bf16[2,192,1024]{2,1,0:T(8,128)(2,1)S(1)} %copy-done.25), channel_id=1, source_target_pairs={{0,24},{8,16},{16,8},{24,0},{1,25},{9,17},{17,9},{25,1},{2,26},{10... | collective-permute-start | bytes 2359304 | tf_op jit(solution)/shard_map/ppermute | solution.py:517
  484.7 4.4 copy-start
  497.9 15.1 %copy-start.28 = (bf16[2,192,1024]{2,1,0:T(8,128)(2,1)}, bf16[2,192,1024]{2,1,0:T(8,128)(2,1)S(1)}, u32[]{:S(2)}) copy-start(bf16[2,192,1024]{2,1,0:T(8,128)(2,1)S(1)} %collective-permute-done.12.rest_1_) | copy-start | bytes 2359300
  513.0 1.2 copy-start.31
  530.6 1.1 copy-start.1
  530.7 151.9 %copy-start.16 = (f32[24]{0:T(128)S(1)}, f32[24]{0:T(128)}, u32[]{:S(2)}) copy-start(f32[24]{0:T(128)} %copy-done.15) | copy-start | bytes 292
  530.7 155.0 %copy-start.18 = (f32[24]{0:T(128)S(1)}, f32[24]{0:T(128)}, u32[]{:S(2)}) copy-start(f32[24]{0:T(128)} %copy-done.17) | copy-start | bytes 292
  530.7 155.8 %copy-start.20 = (bf16[24]{0:T(256)(128)(2,1)S(1)}, bf16[24]{0:T(256)(128)(2,1)}, u32[]{:S(2)}) copy-start(bf16[24]{0:T(256)(128)(2,1)} %param.13) | copy-start | bytes 148
  530.7 155.8 %copy-start.21 = (bf16[24]{0:T(256)(128)(2,1)S(1)}, bf16[24]{0:T(256)(128)(2,1)}, u32[]{:S(2)}) copy-start(bf16[24]{0:T(256)(128)(2,1)} %param.14) | copy-start | bytes 148
  (6 other events, 4.4 us)
Sparse Core Ops, SparseCore 0:
  11.6 56.8 all-gather.4
  70.1 63.6 all-gather.6
  136.8 97.6 all-gather.8
  446.0 68.3 reduce-scatter.2
  530.8 150.6 reduce-scatter.4

commit v2 on v0

v2 whole, which is shorter than its diff:
```python
import functools

import jax
import jax.numpy as jnp
from jax import lax
from jax.experimental import pallas as pl
from jax.experimental.pallas import tpu as pltpu
from jax.sharding import PartitionSpec as P

epsilon = 1e-06
bf16 = jnp.bfloat16
f32 = jnp.float32
WIDTH = 768
LENGTH = 1024
HIDDEN = 3072
HEADS = 12
HEAD_DIM = 64
CHUNKS = 2


def rows_by_rows(left, right):
    return lax.dot_general(left, right, (((1,), (1,)), ((), ())), preferred_element_type=f32)


def times(left, right):
    return jnp.dot(left, right, preferred_element_type=f32)


def rms(values):
    return lax.rsqrt(jnp.mean(values * values, axis=-1, keepdims=True) + epsilon)


def share(offsets, at, refs, source):
    for ref in refs:
        count, rows, _ = ref.shape
        for k in range(count):
            ref[k] = source[pl.ds(pl.multiple_of(offsets[at], 16), rows), :]
            at += 1
    return at


def share_two(core, offsets, at, keeps, sends, first, second):
    @pl.when(core == 0)
    def _():
        share(offsets, at, keeps, first)
        share(offsets, at, sends, second)

    @pl.when(core != 0)
    def _():
        share(offsets, at, keeps, second)
        share(offsets, at, sends, first)


VMEM = 59 * 1024 * 1024
SCALE = 0.001
ANY = pl.BlockSpec(memory_space=pl.ANY)
ALL = ("dp", "seq")
FIRST = 0.7978845608028654
SECOND = FIRST * 0.044715


def call(kernel, name, grid, scalars, operands, outputs, scratch, flops, moved, after=(), aliases=None):
    count = len(scalars) + len(operands)

    def run(*refs):
        kernel(*refs[:count], *refs[count + len(after) :])

    return pl.pallas_call(
        run,
        grid_spec=pltpu.PrefetchScalarGridSpec(
            num_scalar_prefetch=len(scalars),
            grid=grid,
            in_specs=[block for _, block in operands] + [ANY] * len(after),
            out_specs=[block for _, block in outputs],
            scratch_shapes=scratch,
        ),
        out_shape=[shape for shape, _ in outputs],
        input_output_aliases=aliases or {},
        compiler_params=pltpu.CompilerParams(vmem_limit_bytes=VMEM),
        cost_estimate=pl.CostEstimate(
            flops=int(flops * SCALE), bytes_accessed=int(moved * SCALE), transcendentals=0
        ),
        name=name,
    )(*scalars, *[array for array, _ in operands], *after)


def shape(*sizes, kind=bf16):
    return jax.ShapeDtypeStruct(sizes, kind)


def spread(scratch, refs, place):
    for at, ref in enumerate(refs):
        group = ref.shape[0]
        scratch[pl.ds(pl.multiple_of((place ^ at) * group, 64), group), :] = ref[...]


def pick(scratch, refs, place):
    for at, ref in enumerate(refs):
        group = ref.shape[0]
        ref[...] = scratch[pl.ds(pl.multiple_of((place ^ at) * group, 64), group), :]


def values_kernel(where, offsets, x_ref, *rest, pieces, groups):
    parts, rest = rest[:pieces], rest[pieces:]
    outs, (w_ref, turned, scratch, sem) = rest[:groups], rest[groups:]
    step = pl.program_id(0)

    @pl.when(step == 0)
    def _():
        load_weight(offsets, parts, w_ref, sem)
        turned[...] = w_ref[...].T

    for half in range(2):
        at = pl.ds(half * LENGTH // 2, LENGTH // 2)
        x = x_ref[0, at, :].astype(f32)
        scaled = (x * rms(x)).astype(bf16)
        scratch[:, at] = rows_by_rows(turned[...], scaled).astype(bf16)
    pick(scratch, [out.at[0] for out in outs], where[0])


def project_values(where, offsets, tokens, parts, groups, after):
    items = tokens.shape[0]
    group = WIDTH // groups
    units = sum(p.shape[0] for p in parts)
    whole = lambda *_: (0, 0)
    outs = call(
        functools.partial(values_kernel, pieces=len(parts), groups=groups),
        "project_values",
        (items,),
        [where, offsets],
        [(tokens, pl.BlockSpec((1, LENGTH, WIDTH), lambda i, *_: (i, 0, 0)))]
        + [(p, ANY) for p in parts],
        [(shape(items, group, LENGTH), pl.BlockSpec((1, group, LENGTH), lambda i, *_: (i, 0, 0)))] * groups
        + [(shape(WIDTH, WIDTH), pl.BlockSpec((WIDTH, WIDTH), whole))],
        [
            pltpu.VMEM((WIDTH, WIDTH), bf16),
            pltpu.VMEM((WIDTH, LENGTH), bf16),
            pltpu.SemaphoreType.DMA((units,)),
        ],
        2 * items * LENGTH * WIDTH * WIDTH,
        4 * items * LENGTH * WIDTH,
        after,
    )
    return outs[:groups], outs[groups]


def load_logits(offsets, pieces, held, sems):
    def copy(head, at):
        rows = pieces[at].shape[1]
        start = pl.multiple_of(offsets[at], rows)
        return pltpu.make_async_copy(
            pieces[at].at[head], held.at[head, pl.ds(start, rows)], sems.at[head, at]
        )

    head = pl.program_id(0)

    @pl.when(head == 0)
    def _():
        for h in range(held.shape[0]):
            for at in range(len(pieces)):
                copy(h, at).start()

    for at in range(len(pieces)):
        copy(head, at).wait()


def reach(lengths, base, count):
    which = lax.broadcasted_iota(jnp.int32, (16, LENGTH), 0)
    ends = jnp.zeros((16, LENGTH), jnp.int32)
    for k in range(count):
        ends = jnp.where(which == k, lengths[base + k], ends)
    return jnp.where(lax.broadcasted_iota(jnp.int32, (16, LENGTH), 1) < ends, 1.0, 0.0)


def keep_of(lengths, k):
    return lax.broadcasted_iota(jnp.int32, (1, LENGTH), 1) < lengths[k]


def mix_kernel(lengths, offsets, *rest, groups, pieces, base):
    values, parts = rest[:groups], rest[groups : groups + pieces]
    outs = rest[groups + pieces : 2 * groups + pieces]
    sums_ref, held, left, sems = rest[2 * groups + pieces :]
    load_logits(offsets, parts, held, sems)
    for k in range(groups):
        block = values[k][0]
        left[pl.ds(k * HEAD_DIM, HEAD_DIM), :] = jnp.where(
            keep_of(lengths, base + k), block, jnp.zeros_like(block)
        )
    left[pl.ds(groups * HEAD_DIM, 16), :] = reach(lengths, base, groups).astype(bf16)
    product = rows_by_rows(left[...], held[pl.program_id(0)])
    sums = product[groups * HEAD_DIM : groups * HEAD_DIM + 8]
    sums_ref[0] = sums
    for k in range(groups):
        mixed = product[k * HEAD_DIM : (k + 1) * HEAD_DIM] / sums[k : k + 1]
        outs[k][...] = jnp.where(keep_of(lengths, base + k), mixed, 0.0).astype(bf16)


def mix_items(lengths, offsets, values, parts, item, after=()):
    groups, pieces = len(values), len(parts)
    group = values[0].shape[1]
    base = item * groups
    heads = group // HEAD_DIM
    block = pl.BlockSpec((HEAD_DIM, LENGTH), lambda h, *_: (h, 0))
    outs = call(
        functools.partial(mix_kernel, groups=groups, pieces=pieces, base=base),
        "mix_items",
        (heads,),
        [lengths, offsets],
        [(v, pl.BlockSpec((1, HEAD_DIM, LENGTH), lambda h, *_: (item, h, 0))) for v in values] + [(p, ANY) for p in parts],
        [(shape(group, LENGTH), block)] * groups
        + [(shape(heads, 8, LENGTH, kind=f32), pl.BlockSpec((1, 8, LENGTH), lambda h, *_: (h, 0, 0)))],
        [
            pltpu.VMEM((heads, LENGTH, LENGTH), bf16),
            pltpu.VMEM((groups * HEAD_DIM + 16, LENGTH), bf16),
            pltpu.SemaphoreType.DMA((heads, pieces)),
        ],
        2 * heads * (groups * HEAD_DIM + 16) * LENGTH * LENGTH,
        12 << 20,
        after,
    )
    return outs[:groups], outs[groups]


def values_back_kernel(lengths, offsets, *rest, groups, pieces, base):
    grads, mixed, rest = rest[:groups], rest[groups : 2 * groups], rest[2 * groups :]
    sums_ref, parts = rest[0], rest[1 : 1 + pieces]
    outs = rest[1 + pieces : 1 + pieces + groups]
    left_ref, held, sems = rest[1 + pieces + groups :]
    load_logits(offsets, parts, held, sems)
    which = lax.broadcasted_iota(jnp.int32, (16, LENGTH), 0)
    extra = jnp.zeros((16, LENGTH), f32)
    for k in range(groups):
        keep = keep_of(lengths, base + k)
        inverse = jnp.where(keep, 1.0 / sums_ref[0, k : k + 1], 0.0)
        grad = grads[k][...].astype(f32)
        delta = jnp.sum(grad * mixed[k][...].astype(f32), axis=0, keepdims=True)
        left_ref[0, pl.ds(k * HEAD_DIM, HEAD_DIM), :] = (grad * inverse).astype(bf16)
        extra = jnp.where(which == k, -(delta * inverse), extra)
    left_ref[0, pl.ds(groups * HEAD_DIM, 16), :] = extra.astype(bf16)
    product = times(left_ref[0, pl.ds(0, groups * HEAD_DIM), :], held[pl.program_id(0)])
    for k in range(groups):
        part = product[k * HEAD_DIM : (k + 1) * HEAD_DIM]
        outs[k][...] = jnp.where(keep_of(lengths, base + k), part, 0.0).astype(bf16)


def values_back(lengths, offsets, grads, mixed, sums, parts, base, after=()):
    groups, pieces = len(grads), len(parts)
    group = grads[0].shape[0]
    heads = group // HEAD_DIM
    tall = groups * HEAD_DIM + 16
    block = pl.BlockSpec((HEAD_DIM, LENGTH), lambda h, *_: (h, 0))
    outs = call(
        functools.partial(values_back_kernel, groups=groups, pieces=pieces, base=base),
        "values_back",
        (heads,),
        [lengths, offsets],
        [(g, block) for g in grads]
        + [(m, block) for m in mixed]
        + [(sums, pl.BlockSpec((1, 8, LENGTH), lambda h, *_: (h, 0, 0)))]
        + [(p, ANY) for p in parts],
        [(shape(group, LENGTH), block)] * groups
        + [(shape(heads, tall, LENGTH), pl.BlockSpec((1, tall, LENGTH), lambda h, *_: (h, 0, 0)))],
        [
            pltpu.VMEM((heads, LENGTH, LENGTH), bf16),
            pltpu.SemaphoreType.DMA((heads, pieces)),
        ],
        2 * heads * tall * LENGTH * LENGTH,
        14 << 20,
        after,
    )
    return outs[:groups], outs[groups]


def logits_back_kernel(lengths, offsets, *rest, count, groups, shares):
    lefts, values, rest = rest[:count], rest[count : count + groups], rest[count + groups :]
    refs, (left, right, whole) = rest[: len(shares)], rest[len(shares) :]
    tall = groups * HEAD_DIM + 16
    for item in range(count):
        left[pl.ds(item * tall, tall), :] = lefts[item][0]
        for k in range(groups):
            block = values[k][item]
            right[pl.ds(item * tall + k * HEAD_DIM, HEAD_DIM), :] = jnp.where(
                keep_of(lengths, item * groups + k), block, jnp.zeros_like(block)
            )
        right[pl.ds(item * tall + groups * HEAD_DIM, 16), :] = reach(
            lengths, item * groups, groups
        ).astype(bf16)
    whole[...] = times(left[...].T, right[...]).astype(bf16)
    at = 0
    for ref, (number, rows) in zip(refs, shares):
        for k in range(number):
            ref[k, 0] = whole[pl.ds(pl.multiple_of(offsets[at], rows), rows), :]
            at += 1


def logits_back(lengths, offsets, lefts, values, shares, after=()):
    count, groups = len(lefts), len(values)
    heads, tall, _ = lefts[0].shape
    block = pl.BlockSpec((count, HEAD_DIM, LENGTH), lambda h, *_: (0, h, 0))
    return call(
        functools.partial(logits_back_kernel, count=count, groups=groups, shares=shares),
        "logits_back",
        (heads,),
        [lengths, offsets],
        [(v, pl.BlockSpec((1, tall, LENGTH), lambda h, *_: (h, 0, 0))) for v in lefts]
        + [(v, block) for v in values],
        [
            (
                shape(number, heads, rows, LENGTH),
                pl.BlockSpec((number, 1, rows, LENGTH), lambda h, *_: (0, h, 0, 0)),
            )
            for number, rows in shares
        ],
        [
            pltpu.VMEM((count * tall, LENGTH), bf16),
            pltpu.VMEM((count * tall, LENGTH), bf16),
            pltpu.VMEM((LENGTH, LENGTH), bf16),
        ],
        2 * heads * count * tall * LENGTH * LENGTH,
        14 << 20,
        after,
    )


def load_weight(offsets, pieces, held, sem):
    copies = []
    at = 0
    for piece in pieces:
        count, rows, columns = piece.shape
        for k in range(count):
            start = pl.multiple_of(offsets[2 * at], 16)
            side = pl.multiple_of(offsets[2 * at + 1], 128)
            copies.append(
                pltpu.make_async_copy(
                    piece.at[k], held.at[pl.ds(start, rows), pl.ds(side, columns)], sem.at[at]
                )
            )
            at += 1
    for copy in copies:
        copy.start()
    for copy in copies:
        copy.wait()


def halves(total, gain, low, high):
    half = WIDTH // 2
    column = jnp.broadcast_to(gain, (128, WIDTH)).T
    leading = column.astype(bf16)
    low[:, pl.ds(0, half)] = total[:, :half].astype(bf16)
    high[:, pl.ds(0, half)] = total[:, half:].astype(bf16)
    low[:, pl.ds(half, 128)] = leading
    high[:, pl.ds(half, 128)] = (column - leading.astype(f32)).astype(bf16)


class Refs:
    def __init__(self, refs):
        self.refs, self.at = refs, 0

    def take(self, count=None):
        if count is None:
            self.at += 1
            return self.refs[self.at - 1]
        self.at += count
        return self.refs[self.at - count : self.at]


def feed_kernel(where, units_at, pieces_at, *refs, first, last, carried, settled, plain, slices, groups, parts, pieces):
    refs = Refs(refs)
    grad_ref, weights = refs.take(), refs.take(pieces)
    mixed = refs.take(groups) if first or last else None
    w_ref = refs.take() if last and not first else None
    if first:
        x_ref = refs.take()
    else:
        hidden_ref, scaled_ref, out_ref, back_ref = refs.take(4)
    if carried:
        carry = refs.take(2 + 2 * last)
    if last and carried:
        refs.take()
    if first:
        hidden_out, scaled_out, w_out = refs.take(3)
    if last:
        result_ref, grad_hidden_ref, grads = refs.take(), refs.take(), refs.take(groups)
    else:
        out_next, back_next = refs.take(2)
    if settled and plain:
        joint = refs.take(1 + last)
    elif settled:
        keeps, sends = refs.take(parts[0]), refs.take(parts[1])
        if last:
            w_keeps, w_sends = refs.take(parts[0]), refs.take(parts[1])
    else:
        handed = refs.take(2 + 2 * last)
    held, up_turned, down_turned, active, grad_pre, sum_up, sum_down, sems, loaded = refs.take(9)
    if first or last:
        turned = refs.take()
    if last:
        scratch, sum_w, sum_gain, low, high = refs.take(5)
    step = pl.program_id(0)
    final = step == pl.num_programs(0) - 1
    units = slices * WIDTH
    up_ref = held.at[:, pl.ds(0, units)]
    down_ref = held.at[:, pl.ds(units, units)]
    downs = [held.at[:, pl.ds(units + q * WIDTH, WIDTH)] for q in range(slices)]
    if first:
        w_ref = held.at[:, pl.ds(2 * units, WIDTH)]
    sums = [sum_up, sum_down] + ([sum_w, sum_gain] if last else [])

    def bring():
        return [pltpu.make_async_copy(carry[k], sums[k], sems.at[k]) for k in range(len(sums))]

    @pl.when(step == 0)
    def _():
        if carried:
            for copy in bring():
                copy.start()
        else:
            for total in sums:
                total[...] = jnp.zeros_like(total)
        load_weight(pieces_at, weights, held, loaded)
        if first:
            w_out[...] = w_ref[...]
        up_turned[...] = up_ref[...].T
        for q in range(slices):
            down_turned[:, pl.ds(q * WIDTH, WIDTH)] = downs[q][...].T

    if first or last:
        spread(turned, mixed, where[0])
    if first:
        hidden = x_ref[0].astype(f32) + times(turned[...].T, w_ref[...])
        hidden_out[...] = hidden
        scaled = (hidden * rms(hidden)).astype(bf16)
        scaled_out[...] = scaled
    else:
        scaled = scaled_ref[...]
    grad = grad_ref[0]
    slab = 256
    for k in range(units // slab):
        at = pl.ds(k * slab, slab)
        inner = pl.ds(k * slab % WIDTH, slab)
        pre = rows_by_rows(up_turned[at, :], scaled)
        grad_active = rows_by_rows(downs[k * slab // WIDTH][inner, :], grad)
        square = pre * pre
        half = 0.5 + 0.5 * jnp.tanh(pre * (FIRST + SECOND * square))
        act = pre * half
        active[at, :] = act.astype(bf16)
        slope = half + act * (1.0 - half) * (2.0 * FIRST + 6.0 * SECOND * square)
        grad_pre[at, :] = (grad_active * slope).astype(bf16)
    out = times(down_turned[...], active[...])
    back = times(up_ref[...], grad_pre[...])
    if not first:
        out, back = out + out_ref[...], back + back_ref[...]
    if carried:

        @pl.when(step == 0)
        def _():
            for copy in bring():
                copy.wait()

    for q in range(slices):
        at = pl.ds(q * WIDTH, WIDTH)
        sum_down[at, :] += times(active[at, :], grad)
        sum_up[at, :] += times(grad_pre[at, :], scaled)
    if last:
        hidden = hidden if first else hidden_ref[...]
        result_ref[0] = (hidden + out.T).astype(bf16)
        weighted = back.T
        scale = rms(hidden)
        both = weighted * hidden
        mean = jnp.mean(both, axis=-1, keepdims=True)
        attended = (grad.astype(f32) + scale * weighted - hidden * (scale**3 * mean)).astype(bf16)
        grad_hidden_ref[...] = attended
        scratch[...] = rows_by_rows(w_ref[...], attended).astype(bf16)
        pick(scratch, grads, where[0])
        sum_w[...] += times(turned[...], attended)
        sum_gain[...] += jnp.sum(both * scale, axis=0, keepdims=True)
    else:
        out_next[...] = out
        back_next[...] = back

    @pl.when(final)
    def _():
        if settled:
            for q in range(slices):
                at = pl.ds(q * WIDTH, WIDTH)
                up_ref[:, at] = sum_up[at, :].T.astype(bf16)
                down_ref[:, at] = sum_down[at, :].astype(bf16)
            if last:
                halves(sum_w[...], sum_gain[...], low, high)
            if plain:
                joint[0][...] = held[:, pl.ds(0, 2 * units)]
                if last:
                    joint[1][:, pl.ds(0, low.shape[1])] = low[...]
                    joint[1][:, pl.ds(low.shape[1], low.shape[1])] = high[...]
            else:
                share_two(where[2], units_at, 0, keeps, sends, up_ref, down_ref)
                if last:
                    share_two(where[2], units_at, 0, w_keeps, w_sends, low, high)
        else:
            copies = [
                pltpu.make_async_copy(sums[k], handed[k], sems.at[k]) for k in range(len(sums))
            ]
            for copy in copies:
                copy.start()
            for copy in copies:
                copy.wait()


def feed(where, units_at, item, chunk, grad, packed, w_out, tokens, mixed, state, carry, earlier, shapes, settled, after=()):
    rows = 256
    groups, parts, plain = len(mixed), [len(kind) for kind in shapes or ()], shapes is None
    group = mixed[0].shape[0]
    first, last = chunk == 0, chunk == CHUNKS - 1
    slices = HIDDEN // CHUNKS // WIDTH
    units = slices * WIDTH
    once = pl.Buffered(1)
    tall = pl.BlockSpec((1, rows, WIDTH), lambda j, *_: (item, j, 0))
    flat = pl.BlockSpec((rows, WIDTH), lambda j, *_: (j, 0))
    wide = pl.BlockSpec((WIDTH, rows), lambda j, *_: (0, j))
    split = pl.BlockSpec((group, rows), lambda j, *_: (0, j))
    square = pl.BlockSpec((WIDTH, WIDTH), lambda j, *_: (0, 0), pipeline_mode=once)
    weights, weights_at = packed
    operands = [(grad, tall)] + [(w, ANY) for w in weights]
    if first or last:
        operands += [(m, split) for m in mixed]
    if last and not first:
        operands += [(w_out, square)]
    if first:
        operands += [(tokens, tall)]
    else:
        operands += list(zip(state, (flat, flat, wide, wide)))
    aliases = {}
    if carry:
        operands += [(c, ANY) for c in carry]
    outputs = []
    if first:
        outputs += [(shape(LENGTH, WIDTH, kind=f32), flat), (shape(LENGTH, WIDTH), flat), (shape(WIDTH, WIDTH), square)]
    if last:
        if carry:
            aliases = {3 + len(operands): len(outputs)}
            operands += [(e, ANY) for e in earlier]
        outputs += [(shape(*grad.shape), tall), (shape(LENGTH, WIDTH), flat)]
        outputs += [(shape(group, LENGTH), split)] * groups
    else:
        outputs += [(shape(WIDTH, LENGTH, kind=f32), wide)] * 2
    fixed = len(outputs)
    if settled:
        if plain:
            sizes = [shape(WIDTH, 2 * units), shape(WIDTH, WIDTH + 256)][: 1 + last]
        else:
            sizes = [shape(c, r, units) for kind in shapes for c, r in kind]
            if last:
                sizes += [shape(c, r, WIDTH // 2 + 128) for kind in shapes for c, r in kind]
        outputs += [
            (u, pl.BlockSpec(u.shape, lambda j, *_, n=len(u.shape): (0,) * n, pipeline_mode=once))
            for u in sizes
        ]
    else:
        sizes = [shape(units, WIDTH, kind=f32)] * 2
        if last:
            sizes += [shape(WIDTH, WIDTH, kind=f32), shape(1, WIDTH, kind=f32)]
        outputs += [(u, ANY) for u in sizes]
    scratch = [
        pltpu.VMEM((WIDTH, 2 * units + WIDTH * first), bf16),
        pltpu.VMEM((units, WIDTH), bf16),
        pltpu.VMEM((WIDTH, units), bf16),
        pltpu.VMEM((units, rows), bf16),
        pltpu.VMEM((units, rows), bf16),
        pltpu.VMEM((units, WIDTH), f32),
        pltpu.VMEM((units, WIDTH), f32),
        pltpu.SemaphoreType.DMA((4,)),
        pltpu.SemaphoreType.DMA((sum(w.shape[0] for w in weights),)),
    ]
    if first or last:
        scratch += [pltpu.VMEM((WIDTH, rows), bf16)]
    if last:
        scratch += [
            pltpu.VMEM((WIDTH, rows), bf16),
            pltpu.VMEM((WIDTH, WIDTH), f32),
            pltpu.VMEM((1, WIDTH), f32),
            pltpu.VMEM((WIDTH, WIDTH // 2 + 128), bf16),
            pltpu.VMEM((WIDTH, WIDTH // 2 + 128), bf16),
        ]
    outs = call(
        functools.partial(
            feed_kernel,
            first=first,
            last=last,
            carried=bool(carry),
            settled=settled,
            plain=plain,
            slices=slices,
            groups=groups,
            parts=parts,
            pieces=len(weights),
        ),
        "feed",
        (LENGTH // rows,),
        [where, units_at, weights_at],
        operands,
        outputs,
        scratch,
        12 * LENGTH * WIDTH * units,
        20 << 20,
        after,
        aliases,
    )
    main, sums = outs[:fixed], outs[fixed:]
    if settled and not plain:
        keep, both = parts[0], sum(parts)
        sums = [(sums[at : at + keep], sums[at + keep : at + both]) for at in range(0, len(sums), both)]
    return main, sums


def tokens_kernel(where, units_at, *refs, groups, parts, carried, settled, plain):
    refs = Refs(refs)
    x_ref, grad_ref, w_ref, grads = refs.take(), refs.take(), refs.take(), refs.take(groups)
    if carried:
        carry = refs.take(2)
        refs.take()
    result_ref = refs.take()
    if settled and plain:
        joint = refs.take()
    elif settled:
        keeps, sends = refs.take(parts[0]), refs.take(parts[1])
    else:
        handed = refs.take(2)
    turned, sum_w, sum_gain, low, high, sems = refs.take(6)
    step = pl.program_id(0)
    sums = [sum_w, sum_gain]

    @pl.when(step == 0)
    def _():
        if carried:
            copies = [pltpu.make_async_copy(carry[k], sums[k], sems.at[k]) for k in range(2)]
            for copy in copies:
                copy.start()
            for copy in copies:
                copy.wait()
        else:
            for total in sums:
                total[...] = jnp.zeros_like(total)

    spread(turned, grads, where[0])
    x = x_ref[0].astype(f32)
    scale = rms(x)
    scaled = (x * scale).astype(bf16)
    weighted = rows_by_rows(turned[...].T, w_ref[...])
    both = weighted * x
    mean = jnp.mean(both, axis=-1, keepdims=True)
    total = grad_ref[...].astype(f32) + scale * weighted - x * (scale**3 * mean)
    result_ref[0] = total.astype(bf16)
    sum_gain[...] += jnp.sum(both * scale, axis=0, keepdims=True)
    sum_w[...] += times(turned[...], scaled)

    @pl.when(step == pl.num_programs(0) - 1)
    def _():
        if settled:
            halves(sum_w[...].T, sum_gain[...], low, high)
            if plain:
                joint[:, pl.ds(0, low.shape[1])] = low[...]
                joint[:, pl.ds(low.shape[1], low.shape[1])] = high[...]
            else:
                share_two(where[2], units_at, 0, keeps, sends, low, high)
        else:
            copies = [pltpu.make_async_copy(sums[k], handed[k], sems.at[k]) for k in range(2)]
            for copy in copies:
                copy.start()
            for copy in copies:
                copy.wait()


def grad_tokens_of(where, units_at, item, tokens, grad_hidden, weight, grads, carry, earlier, shapes, settled, after=()):
    rows = 256
    groups, parts, plain = len(grads), [len(kind) for kind in shapes or ()], shapes is None
    group = grads[0].shape[0]
    tall = pl.BlockSpec((1, rows, WIDTH), lambda j, *_: (item, j, 0))
    whole = lambda j, *_: (0, 0)
    operands = [
        (tokens, tall),
        (grad_hidden, pl.BlockSpec((rows, WIDTH), lambda j, *_: (j, 0))),
        (weight, pl.BlockSpec((WIDTH, WIDTH), whole)),
    ] + [(g, pl.BlockSpec((group, rows), lambda j, *_: (0, j))) for g in grads]
    aliases = {}
    if carry:
        operands += [(c, ANY) for c in carry]
        aliases = {2 + len(operands): 0}
        operands += [(earlier, ANY)]
    outputs = [(shape(*tokens.shape), tall)]
    half = WIDTH // 2 + 128
    if settled:
        sizes = [shape(c, r, half) for kind in shapes or () for c, r in kind]
        outputs += [(u, pl.BlockSpec(u.shape, lambda j, *_: (0, 0, 0))) for u in sizes]
        if plain:
            outputs += [(shape(WIDTH, 2 * half), pl.BlockSpec((WIDTH, 2 * half), whole))]
    else:
        outputs += [(shape(WIDTH, WIDTH, kind=f32), ANY), (shape(1, WIDTH, kind=f32), ANY)]
    outs = call(
        functools.partial(tokens_kernel, groups=groups, parts=parts, carried=bool(carry), settled=settled, plain=plain),
        "grad_tokens",
        (LENGTH // rows,),
        [where, units_at],
        operands,
        outputs,
        [
            pltpu.VMEM((WIDTH, rows), bf16),
            pltpu.VMEM((WIDTH, WIDTH), f32),
            pltpu.VMEM((1, WIDTH), f32),
            pltpu.VMEM((WIDTH, half), bf16),
            pltpu.VMEM((WIDTH, half), bf16),
            pltpu.SemaphoreType.DMA((2,)),
        ],
        4 * LENGTH * WIDTH * WIDTH,
        8 << 20,
        after,
        aliases,
    )
    if settled and not plain:
        return outs[0], (outs[1 : 1 + parts[0]], outs[1 + parts[0] :])
    return outs[0], outs[1:]


def halved(array):
    half = array.shape[1] // 2
    return array[:, :half], array[:, half:]


def hold(*values):
    return lax.optimization_barrier(values)


def exchange(parts):
    got = [parts[0]]
    for r in range(1, len(parts)):
        got.append(lax.ppermute(parts[r], "dp", [(i, i ^ r) for i in range(len(parts))]))
    return got


def add(*terms):
    return functools.reduce(jnp.add, [t.astype(f32) for t in terms]).astype(bf16)


class Chips:
    def __init__(self, groups, seqs):
        self.groups, self.seqs, self.rings = groups, seqs, seqs // 2
        self.here, self.row = lax.axis_index("dp"), lax.axis_index("seq")
        self.core, self.z = self.row % 2, self.row // 2

    def across(self, array):
        return lax.ppermute(array, "seq", [(i, i ^ 1) for i in range(self.seqs)])

    def along(self, array, step):
        n = self.seqs
        return lax.ppermute(array, "seq", [(i, (i + 2 * step) % n) for i in range(n)])

    def over(self, array, bits):
        return lax.ppermute(array, "dp", [(i, i ^ bits) for i in range(self.groups)])

    def hop(self, array, step):
        return lax.ppermute(array, "seq", [(i, i ^ (2 * step)) for i in range(self.seqs)])

    def chip(self, bits, step):
        return (self.here ^ bits) * self.rings + (self.z ^ step)

    def chips(self):
        return [self.chip(b, s) for b in range(self.groups) for s in range(self.rings)]

    def gather_line(self, mine):
        return jnp.stack([mine] + [self.hop(mine, s) for s in range(1, self.rings)])

    def gather_plane(self, ring):
        return [ring] + [self.over(ring, bits) for bits in range(1, self.groups)]

    def gathered_at(self, rows):
        return jnp.stack([v for c in self.chips() for v in (c * rows, 0 * c)]).astype(jnp.int32)

    def unit_order(self, rows):
        return jnp.stack([c * rows for c in self.chips()]).astype(jnp.int32)

    def scatter_core(self, shares):
        keeps, (send,) = shares
        got, n = self.across(send), self.rings
        return [add(keep, got[b * n : (b + 1) * n]) for b, keep in enumerate(keeps)]

    def scatter_plane(self, parts):
        parts = [parts[0]] + [self.over(parts[b], b) for b in range(1, self.groups)]
        return [add(*[part[s] for part in parts]) for s in range(self.rings)]

    def scatter_line(self, own):
        return add(own[0], *[self.hop(own[s], s) for s in range(1, self.rings)])

    def settle(self, total):
        rows = total.shape[0] // 2
        mine = lax.dynamic_slice_in_dim(total, self.core * rows, rows)
        other = self.across(lax.dynamic_slice_in_dim(total, (1 - self.core) * rows, rows))
        first = self.core == 0
        return jnp.where(first, mine, other), jnp.where(first, other, mine)


def body(tokens, lengths, mixer, gain_one, gain_two, w_value, w_out, w_up, w_down, cotangent, groups, seqs):
    ranks = groups * seqs
    fast = groups == 4 and seqs == 8
    chips = Chips(groups, seqs)
    here, row, core = chips.here, chips.row, chips.core
    where = jnp.stack([here, row, core]).astype(jnp.int32)
    items = tokens.shape[0]
    shard = w_value.shape[0]
    slices = HIDDEN // WIDTH
    width = slices // CHUNKS
    half = WIDTH // 2

    first_gain = gain_one.astype(f32)[:, None]
    second_gain = gain_two.astype(f32)[:, None]
    value_mine = (w_value.astype(f32) * first_gain).astype(bf16)
    up_mine = (w_up.astype(f32) * second_gain).astype(bf16)
    up_mine = up_mine.reshape(shard, ranks, slices, shard).swapaxes(1, 2)
    down_mine = w_down.reshape(slices, shard, WIDTH).swapaxes(0, 1)
    weights = [value_mine]
    for chunk in range(CHUNKS):
        at = slice(chunk * width, (chunk + 1) * width)
        columns = [m[:, at].reshape(shard, width * WIDTH) for m in (up_mine, down_mine)]
        weights.append(jnp.concatenate(columns + [w_out][chunk:], axis=1))

    logits = jnp.exp(mixer.astype(f32))
    logits_low = logits.astype(bf16)
    block = logits.shape[1]
    shares_at, shares = [0], ((1, LENGTH),)
    whole = [lax.all_gather(w, ALL, axis=0, tiled=True)[None] for w in weights[fast:]]
    weights_at = [jnp.zeros((2,), jnp.int32)] * (1 + CHUNKS)
    if fast:
        rings = chips.rings
        whole = [None] + whole
        value_mine, lengths_here = hold(value_mine, exchange([lengths] * groups))
        other = chips.across(value_mine)
        value_unit = jnp.where(
            core == 0, jnp.concatenate([value_mine, other]), jnp.concatenate([other, value_mine])
        )
        weights_at[0] = chips.gathered_at(2 * shard)
        zs = [(chips.z - s) % rings for s in range(rings)]
        logits_at = [(2 * z + c) * block for c in (core, 1 - core) for z in zs]
        shapes = (((rings, 2 * shard),) * groups, ((groups * rings, 2 * shard),))
        order = chips.unit_order(2 * shard)
    else:
        value_parts = whole[:1]
        logits_parts = [lax.all_gather(logits_low, "seq", axis=1, tiled=True)]
        logits_at = [0]
        shapes = None
        order = jnp.zeros((1,), jnp.int32)
    logits_at, shares_at = (
        jnp.stack([jnp.asarray(v, jnp.int32) for v in at]) for at in (logits_at, shares_at)
    )
    if not fast:
        lengths_here = exchange([lengths] * groups)
    lengths_here = jnp.stack(lengths_here, axis=1).reshape(-1)

    def values_of(after=()):
        return project_values(where, weights_at[0], tokens, value_parts, groups, after)

    def mix(item, values, after=()):
        return mix_items(lengths_here, logits_at, values, logits_parts, item, after)

    def run_feed(item, chunk, packed, w_out_all, mixed, state, carry, result, after=()):
        return feed(
            where, order, item, chunk, cotangent, (packed, weights_at[1 + chunk]), w_out_all, tokens,
            mixed, state, carry, (result,), shapes if chunk else None, item == items - 1, after,
        )

    def back(item, grads, mixed_out, sums, after=()):
        return values_back(
            lengths_here, logits_at, grads, mixed_out, sums, logits_parts, item * groups, after
        )

    def close(item, grad_hidden, grads, carry, earlier, after=()):
        return grad_tokens_of(
            where, order, item, tokens, grad_hidden, value_all, grads, carry, earlier, shapes,
            item == items - 1, after,
        )

    if fast:
        assert items == 2 and CHUNKS == 2
        value_ring = chips.gather_line(value_unit)
        value_ring, logits_low = hold(value_ring, logits_low)
        value_parts = chips.gather_plane(value_ring)
        ring_one = chips.along(logits_low, 1)
        values, value_all = values_of()
        values, ring_one = hold(values, ring_one)
        values = exchange(values)
        ring_two = chips.along(ring_one, 1)
        cross_zero = chips.across(logits_low)
        values, ring_two, cross_zero = hold(values, ring_two, cross_zero)
        ring_three = chips.along(ring_two, 1)
        cross_one, cross_two = chips.across(ring_one), chips.across(ring_two)
        ring_three, cross_one, cross_two = hold(ring_three, cross_one, cross_two)
        logits_parts = [logits_low, ring_one, ring_two, ring_three]
        logits_parts += [cross_zero, cross_one, cross_two, chips.across(ring_three)]
        mixed_out_a, sums_a = mix(0, values)
        mixed_out_a, sums_a = hold(mixed_out_a, sums_a)
        mixed_a = exchange(mixed_out_a)
        mixed_out_b, sums_b = mix(1, values)
        mixed_out_b, mixed_a = hold(mixed_out_b, mixed_a)
        mixed_b = exchange(mixed_out_b)
        state_a, carry = run_feed(0, 0, whole[1:2], None, mixed_a, None, (), None)
        state_a, carry, mixed_b = hold(state_a, carry, mixed_b)
        w_out_all = state_a[2]
        state_b, (shared,) = run_feed(1, 0, whole[1:2], None, mixed_b, None, carry, None)
        first_sums = lax.psum_scatter(shared, ALL, scatter_dimension=0, tiled=True)
        state_a = state_a[:2] + state_a[3:]
        state_b = state_b[:2] + state_b[3:]
        out_a, carry = run_feed(0, 1, whole[2:3], w_out_all, mixed_a, state_a, (), None)
        out_a, carry = hold(out_a, carry)
        grads_a = exchange(out_a[2:])
        out_b, (second_shared, out_shared) = run_feed(
            1, 1, whole[2:3], w_out_all, mixed_b, state_b, carry, out_a[0]
        )
        out_b, grads_a, second_shared, out_shared = hold(out_b, grads_a, second_shared, out_shared)
        result = out_b[0]
        grads_b = exchange(out_b[2:])
        back_a, left_a = back(0, grads_a, mixed_out_a, sums_a)
        back_a, left_a, grads_b, second_shared, out_shared = hold(
            back_a, left_a, grads_b, second_shared, out_shared
        )
        back_a = exchange(back_a)
        back_b, left_b = back(1, grads_b, mixed_out_b, sums_b)
        second_sums = chips.scatter_core(second_shared)
        back_b, left_b, second_sums = hold(back_b, left_b, second_sums)
        back_b = exchange(back_b)
        grad_logits = logits_back(lengths_here, shares_at, [left_a, left_b], values, shares)
        grad_logits, back_a, second_sums, out_shared = hold(grad_logits, back_a, second_sums, out_shared)
        grad_mixer = lax.psum_scatter(grad_logits[0][0], "seq", scatter_dimension=1, tiled=True)
        grad_tokens, carry = close(0, out_a[1], back_a, (), None)
        carry, back_b, grad_tokens, second_sums, out_shared = hold(
            carry, back_b, grad_tokens, second_sums, out_shared
        )
        second_sums = chips.scatter_plane(second_sums)
        out_sums = chips.scatter_core(out_shared)
        grad_tokens, shared = close(1, out_b[1], back_b, carry, grad_tokens)
        shared, second_sums, out_sums = hold(shared, second_sums, out_sums)
        second_sums = chips.scatter_line(second_sums)
        value_sums = chips.scatter_core(shared)
        small_sums = [jnp.concatenate(pair, axis=2) for pair in zip(value_sums, out_sums)]
        small_sums, second_sums = hold(small_sums, second_sums)
        small_sums = chips.scatter_plane(small_sums)
        second_sums = chips.settle(second_sums)
        small_sums, second_sums = hold(small_sums, second_sums)
        low, high = chips.settle(chips.scatter_line(small_sums))
        small = half + 128
        settled = [halved(first_sums), second_sums, (low[:, small:], high[:, small:]), (low[:, :small], high[:, :small])]
    else:
        values, value_all = values_of()
        values = exchange(values)
        mixed_out, sums, mixed = [], [], []
        for item in range(items):
            out, total = mix(item, values)
            mixed_out.append(out)
            sums.append(total)
            mixed.append(exchange(out))
        states, w_out_all, result = [None] * items, None, None
        grads, grad_hidden, shared = [None] * items, [None] * items, []
        for chunk in range(CHUNKS):
            carry = ()
            for item in range(items):
                state, carry = run_feed(
                    item, chunk, whole[1 + chunk : 2 + chunk], w_out_all, mixed[item], states[item], carry, result
                )
                if chunk == CHUNKS - 1:
                    result, grad_hidden[item], grads[item] = state[0], state[1], exchange(state[2:])
                elif chunk == 0:
                    if item == items - 1:
                        w_out_all = state[2]
                    states[item] = list(state[:2]) + list(state[3:])
                else:
                    states[item] = list(states[item][:2]) + list(state)
            shared += carry
        lefts, grad_values = [], []
        for item in range(items):
            out, left = back(item, grads[item], mixed_out[item], sums[item])
            lefts.append(left)
            grad_values.append(exchange(out))
        grad_logits = logits_back(lengths_here, shares_at, lefts, values, shares)
        carry, grad_tokens = (), None
        for item in range(items):
            grad_tokens, carry = close(item, grad_hidden[item], grad_values[item], carry, grad_tokens)
        shared += carry
        grad_mixer = lax.psum_scatter(grad_logits[0][0], "seq", scatter_dimension=1, tiled=True)
        settled = [halved(lax.psum_scatter(x, ALL, scatter_dimension=0, tiled=True)) for x in shared]
    grad_mixer = grad_mixer.astype(f32) * logits
    ups = jnp.concatenate([pair[0] for pair in settled[:CHUNKS]], axis=1)
    downs = jnp.concatenate([pair[1] for pair in settled[:CHUNKS]], axis=1)
    sum_up = ups.astype(f32).reshape(shard, slices, ranks, shard).swapaxes(1, 2).reshape(shard, HIDDEN)
    sum_up = sum_up * second_gain
    sum_down = downs.astype(f32).reshape(shard, slices, WIDTH).swapaxes(0, 1).reshape(shard * slices, WIDTH)

    def joined(pair):
        low, high = (part.astype(f32) for part in pair)
        return jnp.concatenate([low[:, :half], high[:, :half]], axis=1), low[:, half] + high[:, half]

    sum_out, gain_two_sum = joined(settled[CHUNKS])
    sum_value, gain_one_sum = joined(settled[CHUNKS + 1])
    return (
        result,
        grad_tokens,
        grad_mixer,
        gain_one_sum / first_gain[:, 0],
        gain_two_sum / second_gain[:, 0],
        sum_value * first_gain,
        sum_out,
        sum_up,
        sum_down,
    )


def solution(mesh):
    rows = P(ALL, None)
    line = P(ALL)
    cube = P(ALL, None, None)
    logits = P("dp", "seq", None)
    return jax.shard_map(
        functools.partial(body, groups=mesh.shape["dp"], seqs=mesh.shape["seq"]),
        mesh=mesh,
        in_specs=(cube, line, logits, line, line, rows, rows, rows, rows, cube),
        out_specs=(cube, cube, logits, line, line, rows, rows, rows, rows),
        check_vma=False,
    )
```

time: 1740 us -> 503 us (0.29)
  waiting for transfers between devices: 976 us -> 184 us
  matrix products: 364 us -> 0 us
  Pallas kernels: 0 us -> 201 us
  other arithmetic: 178 us -> 15.8 us
  local copies, waits for them, and re-layouts: 119 us -> 17.7 us
  blocking collectives: 78.7 us -> 0 us
  starting transfers between devices: 0.85 us -> 62.9 us
    reduce_scatter x5 -> x2, waiting for transfers between devices: 423 us -> 0.01 us  [the longest x1 0.01 us: body(): first_sums = lax.psum_scatter(shared, ALL, scatter_dimension=0, tiled=True)]
    all_gather x6 -> x2, waiting for transfers between devices: 329 us -> 0.02 us  [body(): lax.all_gather(w, ALL, axis=0, tiled=True)[None]]
    dot_general x16 -> x0, matrix products: 241 us -> none  [the longest x2 37.8 us: single(): jnp.einsum('hij,jhd->ihd', probs, split, preferred_element_type=jnp.float32)]
    unnamed x13 -> x4, waiting for transfers between devices: 224 us -> 0.07 us
    pallas_call x0 -> x12, Pallas kernels: none -> 201 us  [call(): pl.pallas_call(run, grid_spec=pltpu.PrefetchScalarGridSpec(num_scalar_pre...]
    ppermute x0 -> x55, waiting for transfers between devices: none -> 184 us  [the longest x24 79.8 us: exchange(): lax.ppermute(parts[r], 'dp', [(i, i ^ r) for i in range(len(parts))])]
    sub x4 -> x0, other arithmetic: 160 us -> none  [softmax_rows(): expos = jnp.where(keep_keys, jnp.exp(masked - top), 0.0)]
    sub x2 -> x0, matrix products: 123 us -> none  [single(): grad_probs - jnp.sum(probs * grad_probs, axis=2, keepdims=True)]
  transfers between devices with their start and end apart: 12 -> 59, of which waited for: 9 -> 32; matrix products, arithmetic and copies ran while one was open for 15% -> 4% of each run, Pallas kernels for 0% -> 41%
where the time goes in v2:
time: 503 us; the launch traced here: 497 us
  Pallas kernels  201 us (40%)
  waiting for transfers between devices  184 us (37%)
  starting transfers between devices  62.9 us (13%)
  local copies, waits for them, and re-layouts  17.7 us (4%)
  other arithmetic  15.8 us (3%)
  between operations  15 us (3%)
    pallas_call x12, Pallas kernels, call(): pl.pallas_call(run, grid_spec=pltpu.PrefetchScalarGridSpec(num_scalar_pre...  201 us
    ppermute x24, waiting for transfers between devices, exchange(): lax.ppermute(parts[r], 'dp', [(i, i ^ r) for i in range(len(parts))])  79.8 us
    ppermute x9, waiting for transfers between devices, over(): lax.ppermute(array, 'dp', [(i, i ^ bits) for i in range(self.groups)])  45.2 us
    ppermute x9, waiting for transfers between devices, hop(): lax.ppermute(array, 'seq', [(i, i ^ 2 * step) for i in range(self.seqs)])  31.9 us
    ppermute x24, starting transfers between devices, exchange(): lax.ppermute(parts[r], 'dp', [(i, i ^ r) for i in range(len(parts))])  30.9 us
    ppermute x3, waiting for transfers between devices, along(): lax.ppermute(array, 'seq', [(i, (i + 2 * step) % n) for i in range(n)])  23.2 us
    ppermute x9, starting transfers between devices, hop(): lax.ppermute(array, 'seq', [(i, i ^ 2 * step) for i in range(self.seqs)])  20.2 us
    ppermute x9, starting transfers between devices, over(): lax.ppermute(array, 'dp', [(i, i ^ bits) for i in range(self.groups)])  10.6 us
  transfers between devices with their start and end apart: 59, of which 32 were waited for; matrix products, arithmetic and copies ran while one was open for 4% of the time, Pallas kernels for 41%

profile of v2, /device:TPU:0, one launch (start us, length us, event | category | flops | bytes accessed | tf_op | source)
XLA Modules:
  0.0 496.7 jit_solution(13182913425395502532)
XLA Ops:
  14.6 3.0 collective-permute-start.1
  19.3 1.9 collective-permute-done
  21.2 2.4 collective-permute-done.2
  24.8 3.7 collective-permute-start.6
  29.3 3.0 collective-permute-done.6
  32.3 6.2 %collective-permute-done.5 = bf16[48,768]{1,0:T(8,128)(2,1)S(1)} collective-permute-done((bf16[48,768]{1,0:T(8,128)(2,1)S(1)}, bf16[48,768]{1,0:T(8,128)(2,1)S(1)}, u32[]{:S(2)}, u32[]{:S(2)}) %collective-permute-start.5) | collective-permute-done | bytes 73760 | tf_op jit(solution)/shard_map/ppermute | solution.py:760
  40.3 1.9 collective-permute-start.7
  43.5 7.3 %collective-permute-done.9.refs_6_ = bf16[4,48,768]{2,1,0:T(8,128)(2,1)S(1)} collective-permute-done((bf16[4,48,768]{2,1,0:T(8,128)(2,1)S(1)}, bf16[4,48,768]{2,1,0:T(8,128)(2,1)S(1)}, u32[]{:S(2)}, u32[]{:S(2)}) %collective-permute-start.9) | collective-permute-done | bytes 294944 | tf_op jit(solution)/shard_map/ppermute | solution.py:757
  50.7 5.9 %collective-permute-done.8.refs_5_ = bf16[4,48,768]{2,1,0:T(8,128)(2,1)S(1)} collective-permute-done((bf16[4,48,768]{2,1,0:T(8,128)(2,1)S(1)}, bf16[4,48,768]{2,1,0:T(8,128)(2,1)S(1)}, u32[]{:S(2)}, u32[]{:S(2)}) %collective-permute-start.8) | collective-permute-done | bytes 294944 | tf_op jit(solution)/shard_map/ppermute | solution.py:757
  58.9 8.8 %project_values.1 = (bf16[2,192,1024]{2,1,0:T(8,128)(2,1)}, bf16[2,192,1024]{2,1,0:T(8,128)(2,1)}, bf16[2,192,1024]{2,1,0:T(8,128)(2,1)}, bf16[2,192,1024]{2,1,0:T(8,128)(2,1)}, bf16[768,768]{1,0:T(8,128)(2,1)}) custom-call(s32[3]{0:T(128)} %pad_add_fusion.1.refs_0_, s32[32]{0:T(128)} %stack.172.refs_1_, bf16[2,1024,768]{2,1,0:T(8,128)(2,1)} %refs_2_.5, ...), custom_call_target="tpu_custom_call" | custom-call | flops 2415919 | bytes 6291 | tf_op jit(solution)/shard_map/project_values/pallas_call | solution.py:68
  71.9 26.9 %collective-permute-done.11.refs_3_.refs_5_ = bf16[2,192,1024]{2,1,0:T(8,128)(2,1)S(1)} collective-permute-done((bf16[2,192,1024]{2,1,0:T(8,128)(2,1)}, bf16[2,192,1024]{2,1,0:T(8,128)(2,1)S(1)}, u32[]{:S(2)}, u32[]{:S(2)}) %collective-permute-start.11) | collective-permute-done | bytes 786464 | tf_op jit(solution)/shard_map/ppermute | solution.py:735
  98.8 14.8 %collective-permute-done.12.refs_4_.refs_6_ = bf16[2,192,1024]{2,1,0:T(8,128)(2,1)S(1)} collective-permute-done((bf16[2,192,1024]{2,1,0:T(8,128)(2,1)}, bf16[2,192,1024]{2,1,0:T(8,128)(2,1)S(1)}, u32[]{:S(2)}, u32[]{:S(2)}) %collective-permute-start.12) | collective-permute-done | bytes 786464 | tf_op jit(solution)/shard_map/ppermute | solution.py:735
  113.6 2.5 collective-permute-done.13.refs_5_.refs_7_
  118.4 23.2 %collective-permute-done.16.refs_9_.refs_14_ = bf16[3,128,1024]{2,1,0:T(8,128)(2,1)} collective-permute-done((bf16[3,128,1024]{2,1,0:T(8,128)(2,1)S(1)}, bf16[3,128,1024]{2,1,0:T(8,128)(2,1)}, u32[]{:S(2)}, u32[]{:S(2)}) %collective-permute-start.16) | collective-permute-done | bytes 786464 | tf_op jit(solution)/shard_map/ppermute | solution.py:754
  144.3 7.4 %mix_items.3 = (bf16[192,1024]{1,0:T(8,128)(2,1)}, bf16[192,1024]{1,0:T(8,128)(2,1)}, bf16[192,1024]{1,0:T(8,128)(2,1)}, bf16[192,1024]{1,0:T(8,128)(2,1)}, f32[3,8,1024]{2,1,0:T(8,128)}) custom-call(s32[8]{0:T(128)} %reshape.186.refs_0_, s32[8]{0:T(128)} %stack.171.refs_1_, bf16[2,192,1024]{2,1,0:T(8,128)(2,1)} %get-tuple-element.239.refs_2_.refs_4_, ...), custom_call_target="tpu_custom_call" | custom-call | flops 1711276 | bytes 12582 | tf_op jit(solution)/shard_map/mix_items/pallas_call | solution.py:68
  153.5 1.9 collective-permute-start.22
  155.3 7.4 %mix_items.2 = (bf16[192,1024]{1,0:T(8,128)(2,1)}, bf16[192,1024]{1,0:T(8,128)(2,1)}, bf16[192,1024]{1,0:T(8,128)(2,1)}, bf16[192,1024]{1,0:T(8,128)(2,1)}, f32[3,8,1024]{2,1,0:T(8,128)}) custom-call(s32[8]{0:T(128)} %reshape.186.refs_0_, s32[8]{0:T(128)} %stack.171.refs_1_, bf16[2,192,1024]{2,1,0:T(8,128)(2,1)} %get-tuple-element.239.refs_2_.refs_4_, ...), custom_call_target="tpu_custom_call" | custom-call | flops 1711276 | bytes 12582 | tf_op jit(solution)/shard_map/mix_items/pallas_call | solution.py:68
  164.0 8.1 %collective-permute-done.21.refs_7_ = bf16[192,1024]{1,0:T(8,128)(2,1)S(1)} collective-permute-done((bf16[192,1024]{1,0:T(8,128)(2,1)}, bf16[192,1024]{1,0:T(8,128)(2,1)S(1)}, u32[]{:S(2)}, u32[]{:S(2)}) %collective-permute-start.21) | collective-permute-done | bytes 393248 | tf_op jit(solution)/shard_map/ppermute | solution.py:735
  172.1 5.3 %collective-permute-done.22.refs_8_ = bf16[192,1024]{1,0:T(8,128)(2,1)S(1)} collective-permute-done((bf16[192,1024]{1,0:T(8,128)(2,1)}, bf16[192,1024]{1,0:T(8,128)(2,1)S(1)}, u32[]{:S(2)}, u32[]{:S(2)}) %collective-permute-start.22) | collective-permute-done | bytes 393248 | tf_op jit(solution)/shard_map/ppermute | solution.py:735
  177.4 2.0 collective-permute-start.23
  179.5 1.8 collective-permute-start.24
  183.0 30.7 %feed.4 = (f32[1024,768]{1,0:T(8,128)}, bf16[1024,768]{1,0:T(8,128)(2,1)}, bf16[768,768]{1,0:T(8,128)(2,1)}, f32[768,1024]{1,0:T(8,128)}, f32[768,1024]{1,0:T(8,...) custom-call(s32[3]{0:T(128)} %pad_add_fusion.1.refs_0_, s32[16]{0:T(128)} %stack.157.refs_1_, ...), custom_call_target="tpu_custom_call" | custom-call | flops 14495514 | bytes 20971 | tf_op jit(solution)/shard_map/feed/pallas_call | solution.py:68
  214.7 33.4 %feed.5 = (f32[1024,768]{1,0:T(8,128)}, bf16[1024,768]{1,0:T(8,128)(2,1)}, bf16[768,768]{1,0:T(8,128)(2,1)}, f32[768,1024]{1,0:T(8,128)}, f32[768,1024]{1,0:T(8,128)}, /*index=5*/bf16[768,3072]{1,0:T(8,128)(2,1)}) custom-call(s32[3]{0:T(128)} %pad_add_fusion.1.refs_0_, s32[16]{0:T(128)} %stack.157.refs_1_, s32[2]{0:T(128)} %broadcast_1_refs_2_.2.refs_2_, ...), custom_call_target="tpu_custom_call" | custom-call | flops 14495514 | bytes 20971 | tf_op jit(solution)/shard_map/feed/pallas_call | solution.py:68
  248.2 31.7 %feed.6 = (bf16[2,1024,768]{2,1,0:T(8,128)(2,1)}, bf16[1024,768]{1,0:T(8,128)(2,1)}, bf16[192,1024]{1,0:T(8,128)(2,1)}, bf16[192,1024]{1,0:T(8,128)(2,1)}, bf16[...) custom-call(s32[3]{0:T(128)} %pad_add_fusion.1.refs_0_, ...), custom_call_target="tpu_custom_call" | custom-call | flops 14495514 | bytes 20971 | tf_op jit(solution)/shard_map/feed/pallas_call | solution.py:68
  281.1 1.8 collective-permute-start.27
  283.7 35.9 %feed.7 = (bf16[2,1024,768]{2,1,0:T(8,128)(2,1)}, bf16[1024,768]{1,0:T(8,128)(2,1)}, bf16[192,1024]{1,0:T(8,128)(2,1)}, bf16[192,1024]{1,0:T(8,128)(2,1)}, bf16[...) custom-call(s32[3]{0:T(128)} %pad_add_fusion.1.refs_0_, ...), custom_call_target="tpu_custom_call", output_to_operand_aliasing={{0}: (18, {})} | custom-call | flops 14495514 | bytes 20971 | tf_op jit(solution)/shard_map/feed/pallas_call | solution.py:68
  320.7 1.8 collective-permute-start.30
  323.3 7.8 %values_back.2 = (bf16[192,1024]{1,0:T(8,128)(2,1)}, bf16[192,1024]{1,0:T(8,128)(2,1)}, bf16[192,1024]{1,0:T(8,128)(2,1)}, bf16[192,1024]{1,0:T(8,128)(2,1)}, bf16[3,272,1024]{2,1,0:T(8,128)(2,1)}) custom-call(s32[8]{0:T(128)} %reshape.186.refs_0_, s32[8]{0:T(128)} %stack.171.refs_1_, bf16[192,1024]{1,0:T(8,128)(2,1)} %get-tuple-element.315.refs_2_, ...), custom_call_target="tpu_custom_call" | custom-call | flops 1711276 | bytes 14680 | tf_op jit(solution)/shard_map/values_back/pallas_call | solution.py:68
  331.1 2.2 collective-permute-done.29.refs_3_
  333.3 7.2 %collective-permute-done.30.refs_4_ = bf16[192,1024]{1,0:T(8,128)(2,1)S(1)} collective-permute-done((bf16[192,1024]{1,0:T(8,128)(2,1)}, bf16[192,1024]{1,0:T(8,128)(2,1)S(1)}, u32[]{:S(2)}, u32[]{:S(2)}) %collective-permute-start.30) | collective-permute-done | bytes 393248 | tf_op jit(solution)/shard_map/ppermute | solution.py:735
  344.9 8.0 %values_back.3 = (bf16[192,1024]{1,0:T(8,128)(2,1)}, bf16[192,1024]{1,0:T(8,128)(2,1)}, bf16[192,1024]{1,0:T(8,128)(2,1)}, bf16[192,1024]{1,0:T(8,128)(2,1)}, bf16[3,272,1024]{2,1,0:T(8,128)(2,1)}) custom-call(s32[8]{0:T(128)} %reshape.186.refs_0_, s32[8]{0:T(128)} %stack.171.refs_1_, bf16[192,1024]{1,0:T(8,128)(2,1)} %get-tuple-element.340.refs_2_, ...), custom_call_target="tpu_custom_call" | custom-call | flops 1711276 | bytes 14680 | tf_op jit(solution)/shard_map/values_back/pallas_call | solution.py:68
  352.9 2.7 add_convert_fusion
  355.6 10.2 %logits_back.1 = bf16[1,3,1024,1024]{3,2,1,0:T(8,128)(2,1)} custom-call(s32[8]{0:T(128)} %reshape.186.refs_0_, s32[1]{0:T(128)} %constant.69.clone.1.refs_1_, bf16[3,272,1024]{2,1,0:T(8,128)(2,1)} %get-tuple-element.339.refs_2_, bf16[3,272,1024]{2,1,0:T(8,128)(2,1)} %get-tuple-element.355.refs_3_, bf16[2,192,1024]{2,1,0:T(8,128)(2,1)} %get-tuple-element.239.refs_2_.refs_4_, ...), custom_call_target="tpu_custom_call" | custom-call | flops 3422552 | bytes 14680 | tf_op jit(solution)/shard_map/logits_back/pallas_call | solution.py:68
  370.3 9.5 %grad_tokens.2 = (bf16[2,1024,768]{2,1,0:T(8,128)(2,1)}, f32[768,768]{1,0:T(8,128)}, f32[1,768]{1,0:T(1,128)}) custom-call(s32[3]{0:T(128)} %pad_add_fusion.1.refs_0_, s32[16]{0:T(128)} %stack.157.refs_1_, bf16[2,1024,768]{2,1,0:T(8,128)(2,1)} %refs_2_.5, bf16[1024,768]{1,0:T(8,128)(2,1)} %get-tuple-element.314.refs_3_, ...), custom_call_target="tpu_custom_call" | custom-call | flops 2415919 | bytes 8388 | tf_op jit(solution)/shard_map/grad_tokens/pallas_call | solution.py:68
  379.9 6.0 %collective-permute-done.37.refs_7_ = bf16[192,1024]{1,0:T(8,128)(2,1)S(1)} collective-permute-done((bf16[192,1024]{1,0:T(8,128)(2,1)S(1)}, bf16[192,1024]{1,0:T(8,128)(2,1)S(1)}, u32[]{:S(2)}, u32[]{:S(2)}) %collective-permute-start.37) | collective-permute-done | bytes 393248 | tf_op jit(solution)/shard_map/ppermute | solution.py:735
  391.4 10.4 %grad_tokens.3 = (bf16[2,1024,768]{2,1,0:T(8,128)(2,1)}, bf16[4,48,512]{2,1,0:T(8,128)(2,1)}, bf16[4,48,512]{2,1,0:T(8,128)(2,1)}, bf16[4,48,512]{2,1,0:T(8,128)...) custom-call(s32[3]{0:T(128)} %pad_add_fusion.1.refs_0_, ...), custom_call_target="tpu_custom_call", output_to_operand_aliasing={{0}: (11, {})} | custom-call | flops 2415919 | bytes 8388 | tf_op jit(solution)/shard_map/grad_tokens/pallas_call | solution.py:68
  401.9 2.2 collective-permute-done.39
  404.1 11.3 %collective-permute-done.40 = bf16[4,48,1536]{2,1,0:T(8,128)(2,1)S(1)} collective-permute-done((bf16[4,48,1536]{2,1,0:T(8,128)(2,1)S(1)}, bf16[4,48,1536]{2,1,0:T(8,128)(2,1)S(1)}, u32[]{:S(2)}, u32[]{:S(2)}) %collective-permute-start.40) | collective-permute-done | bytes 589856 | tf_op jit(solution)/shard_map/ppermute | solution.py:757
  416.9 4.3 collective-permute-start.46
  421.2 8.7 %collective-permute-done.44 = bf16[48,1536]{1,0:T(8,128)(2,1)S(1)} collective-permute-done((bf16[48,1536]{1,0:T(8,128)(2,1)}, bf16[48,1536]{1,0:T(8,128)(2,1)S(1)}, u32[]{:S(2)}, u32[]{:S(2)}) %collective-permute-start.44) | collective-permute-done | bytes 147488 | tf_op jit(solution)/shard_map/ppermute | solution.py:760
  429.9 5.6 %collective-permute-done.45 = bf16[48,1536]{1,0:T(8,128)(2,1)S(1)} collective-permute-done((bf16[48,1536]{1,0:T(8,128)(2,1)}, bf16[48,1536]{1,0:T(8,128)(2,1)S(1)}, u32[]{:S(2)}, u32[]{:S(2)}) %collective-permute-start.45) | collective-permute-done | bytes 147488 | tf_op jit(solution)/shard_map/ppermute | solution.py:760
  441.4 8.4 %collective-permute-done.47 = bf16[4,48,1024]{2,1,0:T(8,128)(2,1)S(1)} collective-permute-done((bf16[4,48,1024]{2,1,0:T(8,128)(2,1)S(1)}, bf16[4,48,1024]{2,1,0:T(8,128)(2,1)S(1)}, u32[]{:S(2)}, u32[]{:S(2)}) %collective-permute-start.47) | collective-permute-done | bytes 393248 | tf_op jit(solution)/shard_map/ppermute | solution.py:757
  449.8 8.7 %collective-permute-done.48 = bf16[4,48,1024]{2,1,0:T(8,128)(2,1)S(1)} collective-permute-done((bf16[4,48,1024]{2,1,0:T(8,128)(2,1)S(1)}, bf16[4,48,1024]{2,1,0:T(8,128)(2,1)S(1)}, u32[]{:S(2)}, u32[]{:S(2)}) %collective-permute-start.48) | collective-permute-done | bytes 393248 | tf_op jit(solution)/shard_map/ppermute | solution.py:757
  458.8 8.8 %collective-permute-start.51 = (bf16[48,1024]{1,0:T(8,128)(2,1)S(1)}, bf16[48,1024]{1,0:T(8,128)(2,1)S(1)}, u32[]{:S(2)}, u32[]{:S(2)}) collective-permute-start(bf16[48,1024]{1,0:T(8,128)(2,1)S(1)} %get-tuple-element.431), channel_id=1, source_target_pairs={{0,2},{1,3},{2,0},{3,1},{4,6},{5,7},{6,4},{7,5},{8,10},{9,11},{10,... | collective-permute-start | bytes 294920 | tf_op jit(solution)/shard_map/ppermute | solution.py:760
  467.6 2.4 collective-permute-start.53
  470.9 5.9 %collective-permute-done.52 = bf16[48,1024]{1,0:T(8,128)(2,1)S(1)} collective-permute-done((bf16[48,1024]{1,0:T(8,128)(2,1)S(1)}, bf16[48,1024]{1,0:T(8,128)(2,1)S(1)}, u32[]{:S(2)}, u32[]{:S(2)}) %collective-permute-start.52) | collective-permute-done | bytes 98336 | tf_op jit(solution)/shard_map/ppermute | solution.py:760
  484.8 1.8 reshape.192
  487.5 2.6 convert_multiply_fusion
  (261 shorter events, 66.3 us)
Async XLA Ops:
  7.2 175.2 %all-gather.5.cloned.1.call-start = ((), (), s32[]{:S(2)}) async-start(), calls=%async_computation.3 | async-start | bytes 6082560 | tf_op jit(solution)/shard_map/all_gather | solution.py:828
  13.2 235.1 %all-gather.3.cloned.1.call-start = ((), (), s32[]{:S(2)}) async-start(), calls=%async_computation.2 | async-start | bytes 4866048 | tf_op jit(solution)/shard_map/all_gather | solution.py:828
  14.5 466.3 %reduce-scatter.5.cloned.1.call-start = ((), (), s32[]{:S(2)}) async-start(), calls=%async_computation.5 | async-start | bytes 4866048 | tf_op jit(solution)/shard_map/reduce_scatter | solution.py:906
  28.5 10.0 %collective-permute-start.5 = (bf16[48,768]{1,0:T(8,128)(2,1)S(1)}, bf16[48,768]{1,0:T(8,128)(2,1)S(1)}, u32[]{:S(2)}, u32[]{:S(2)}) collective-permute-start(bf16[48,768]{1,0:T(8,128)(2,1)S(1)} %maximum_select_fusion.1), channel_id=1, source_target_pairs={{0,4},{1,5},{2,6},{3,7},{4,0},{5,1},{6,2},{7,3},{8,12},{9,13},{10,... | collective-permute-start | bytes 221192 | tf_op jit(solution)/shard_map/ppermute | solution.py:760
  28.5 10.0 %collective-permute-start.4 = (bf16[48,768]{1,0:T(8,128)(2,1)S(1)}, bf16[48,768]{1,0:T(8,128)(2,1)S(1)}, u32[]{:S(2)}, u32[]{:S(2)}) collective-permute-start(bf16[48,768]{1,0:T(8,128)(2,1)S(1)} %maximum_select_fusion.1), channel_id=1, source_target_pairs={{0,2},{1,3},{2,0},{3,1},{4,6},{5,7},{6,4},{7,5},{8,10},{9,11},{10,... | collective-permute-start | bytes 221192 | tf_op jit(solution)/shard_map/ppermute | solution.py:760
  38.6 29.2 %collective-permute-start.10 = (bf16[3,128,1024]{2,1,0:T(8,128)(2,1)S(1)}, bf16[3,128,1024]{2,1,0:T(8,128)(2,1)S(1)}, u32[]{:S(2)}, u32[]{:S(2)}) collective-permute-start(bf16[3,128,1024]{2,1,0:T(8,128)(2,1)S(1)} %fusion.refs_6_.refs_11_), channel_id=1, source_target_pairs={{0,2},{1,3},{2,4},{3,5},{4,6},{5,7},{6,0},{7,1},{8,10},{9,11},{10,... | collective-permute-start | bytes 2359304 | tf_op jit(solution)/shard_map/ppermute | solution.py:754
  38.6 12.1 %collective-permute-start.9 = (bf16[4,48,768]{2,1,0:T(8,128)(2,1)S(1)}, bf16[4,48,768]{2,1,0:T(8,128)(2,1)S(1)}, u32[]{:S(2)}, u32[]{:S(2)}) collective-permute-start(bf16[4,48,768]{2,1,0:T(8,128)(2,1)S(1)} %pad_maximum_fusion.4.refs_3_), channel_id=1, source_target_pairs={{0,24},{8,16},{16,8},{24,0},{1,25},{9,17},{17,9},{25,1},{2,26},{10... | collective-permute-start | bytes 884744 | tf_op jit(solution)/shard_map/ppermute | solution.py:757
  38.7 17.9 %collective-permute-start.8 = (bf16[4,48,768]{2,1,0:T(8,128)(2,1)S(1)}, bf16[4,48,768]{2,1,0:T(8,128)(2,1)S(1)}, u32[]{:S(2)}, u32[]{:S(2)}) collective-permute-start(bf16[4,48,768]{2,1,0:T(8,128)(2,1)S(1)} %pad_maximum_fusion.4.refs_3_), channel_id=1, source_target_pairs={{0,16},{8,24},{16,0},{24,8},{1,17},{9,25},{17,1},{25,9},{2,18},{10... | collective-permute-start | bytes 884744 | tf_op jit(solution)/shard_map/ppermute | solution.py:757
  40.3 17.8 %collective-permute-start.7 = (bf16[4,48,768]{2,1,0:T(8,128)(2,1)S(1)}, bf16[4,48,768]{2,1,0:T(8,128)(2,1)S(1)}, u32[]{:S(2)}, u32[]{:S(2)}) collective-permute-start(bf16[4,48,768]{2,1,0:T(8,128)(2,1)S(1)} %pad_maximum_fusion.4.refs_3_), channel_id=1, source_target_pairs={{0,8},{8,0},{16,24},{24,16},{1,9},{9,1},{17,25},{25,17},{2,10},{10... | collective-permute-start | bytes 884744 | tf_op jit(solution)/shard_map/ppermute | solution.py:757
  43.5 28.3 %collective-permute-start.15 = (bf16[3,128,1024]{2,1,0:T(8,128)(2,1)S(1)}, bf16[3,128,1024]{2,1,0:T(8,128)(2,1)S(1)}, u32[]{:S(2)}, u32[]{:S(2)}) collective-permute-start(bf16[3,128,1024]{2,1,0:T(8,128)(2,1)S(1)} %fusion.refs_6_.refs_11_), channel_id=1, source_target_pairs={{0,1},{1,0},{2,3},{3,2},{4,5},{5,4},{6,7},{7,6},{8,9},{9,8},{10,11... | collective-permute-start | bytes 2359304 | tf_op jit(solution)/shard_map/ppermute | solution.py:750
  67.8 31.0 %collective-permute-start.11 = (bf16[2,192,1024]{2,1,0:T(8,128)(2,1)}, bf16[2,192,1024]{2,1,0:T(8,128)(2,1)S(1)}, u32[]{:S(2)}, u32[]{:S(2)}) collective-permute-start(bf16[2,192,1024]{2,1,0:T(8,128)(2,1)} %get-tuple-element.235), channel_id=1, source_target_pairs={{0,8},{8,0},{16,24},{24,16},{1,9},{9,1},{17,25},{25,17},{2,10},{10... | collective-permute-start | bytes 2359304 | tf_op jit(solution)/shard_map/ppermute | solution.py:735
  69.1 44.4 %collective-permute-start.12 = (bf16[2,192,1024]{2,1,0:T(8,128)(2,1)}, bf16[2,192,1024]{2,1,0:T(8,128)(2,1)S(1)}, u32[]{:S(2)}, u32[]{:S(2)}) collective-permute-start(bf16[2,192,1024]{2,1,0:T(8,128)(2,1)} %get-tuple-element.236), channel_id=1, source_target_pairs={{0,16},{8,24},{16,0},{24,8},{1,17},{9,25},{17,1},{25,9},{2,18},{10... | collective-permute-start | bytes 2359304 | tf_op jit(solution)/shard_map/ppermute | solution.py:735
  70.4 45.7 %collective-permute-start.13 = (bf16[2,192,1024]{2,1,0:T(8,128)(2,1)}, bf16[2,192,1024]{2,1,0:T(8,128)(2,1)S(1)}, u32[]{:S(2)}, u32[]{:S(2)}) collective-permute-start(bf16[2,192,1024]{2,1,0:T(8,128)(2,1)} %get-tuple-element.237), channel_id=1, source_target_pairs={{0,24},{8,16},{16,8},{24,0},{1,25},{9,17},{17,9},{25,1},{2,26},{10... | collective-permute-start | bytes 2359304 | tf_op jit(solution)/shard_map/ppermute | solution.py:735
  71.8 44.3 %collective-permute-start.14 = (bf16[3,128,1024]{2,1,0:T(8,128)(2,1)S(1)}, bf16[3,128,1024]{2,1,0:T(8,128)(2,1)S(1)}, u32[]{:S(2)}, u32[]{:S(2)}) collective-permute-start(bf16[3,128,1024]{2,1,0:T(8,128)(2,1)S(1)} %collective-permute-done.10.refs_7_.refs_12_), channel_id=1, source_target_pairs={{0,2},{1,3},{2,4},{3,5},{4,6},{5,7},{6,0},{7,1},{8,10},{9,11},{10,... | collective-permute-start | bytes 2359304 | tf_op jit(solution)/shard_map/ppermute | solution.py:754
  71.8 44.9 %collective-permute-start.17 = (bf16[3,128,1024]{2,1,0:T(8,128)(2,1)S(1)}, bf16[3,128,1024]{2,1,0:T(8,128)(2,1)S(1)}, u32[]{:S(2)}, u32[]{:S(2)}) collective-permute-start(bf16[3,128,1024]{2,1,0:T(8,128)(2,1)S(1)} %collective-permute-done.10.refs_7_.refs_12_), channel_id=1, source_target_pairs={{0,1},{1,0},{2,3},{3,2},{4,5},{5,4},{6,7},{7,6},{8,9},{9,8},{10,11... | collective-permute-start | bytes 2359304 | tf_op jit(solution)/shard_map/ppermute | solution.py:750
  116.1 25.5 %collective-permute-start.16 = (bf16[3,128,1024]{2,1,0:T(8,128)(2,1)S(1)}, bf16[3,128,1024]{2,1,0:T(8,128)(2,1)}, u32[]{:S(2)}, u32[]{:S(2)}) collective-permute-start(bf16[3,128,1024]{2,1,0:T(8,128)(2,1)S(1)} %collective-permute-done.14.refs_8_.refs_13_), channel_id=1, source_target_pairs={{0,2},{1,3},{2,4},{3,5},{4,6},{5,7},{6,0},{7,1},{8,10},{9,11},{10,... | collective-permute-start | bytes 2359304 | tf_op jit(solution)/shard_map/ppermute | solution.py:754
  151.8 12.2 %collective-permute-start.20 = (bf16[192,1024]{1,0:T(8,128)(2,1)}, bf16[192,1024]{1,0:T(8,128)(2,1)S(1)}, u32[]{:S(2)}, u32[]{:S(2)}) collective-permute-start(bf16[192,1024]{1,0:T(8,128)(2,1)} %get-tuple-element.253.refs_7_), channel_id=1, source_target_pairs={{0,8},{8,0},{16,24},{24,16},{1,9},{9,1},{17,25},{25,17},{2,10},{10... | collective-permute-start | bytes 1179656 | tf_op jit(solution)/shard_map/ppermute | solution.py:735
  152.6 19.6 %collective-permute-start.21 = (bf16[192,1024]{1,0:T(8,128)(2,1)}, bf16[192,1024]{1,0:T(8,128)(2,1)S(1)}, u32[]{:S(2)}, u32[]{:S(2)}) collective-permute-start(bf16[192,1024]{1,0:T(8,128)(2,1)} %get-tuple-element.254.refs_8_), channel_id=1, source_target_pairs={{0,16},{8,24},{16,0},{24,8},{1,17},{9,25},{17,1},{25,9},{2,18},{10... | collective-permute-start | bytes 1179656 | tf_op jit(solution)/shard_map/ppermute | solution.py:735
  153.5 23.9 %collective-permute-start.22 = (bf16[192,1024]{1,0:T(8,128)(2,1)}, bf16[192,1024]{1,0:T(8,128)(2,1)S(1)}, u32[]{:S(2)}, u32[]{:S(2)}) collective-permute-start(bf16[192,1024]{1,0:T(8,128)(2,1)} %get-tuple-element.255.refs_9_), channel_id=1, source_target_pairs={{0,24},{8,16},{16,8},{24,0},{1,25},{9,17},{17,9},{25,1},{2,26},{10... | collective-permute-start | bytes 1179656 | tf_op jit(solution)/shard_map/ppermute | solution.py:735
  177.4 36.3 %collective-permute-start.23 = (bf16[192,1024]{1,0:T(8,128)(2,1)}, bf16[192,1024]{1,0:T(8,128)(2,1)S(1)}, u32[]{:S(2)}, u32[]{:S(2)}) collective-permute-start(bf16[192,1024]{1,0:T(8,128)(2,1)} %get-tuple-element.268.refs_7_), channel_id=1, source_target_pairs={{0,8},{8,0},{16,24},{24,16},{1,9},{9,1},{17,25},{25,17},{2,10},{10... | collective-permute-start | bytes 1179656 | tf_op jit(solution)/shard_map/ppermute | solution.py:735
  179.5 34.2 %collective-permute-start.24 = (bf16[192,1024]{1,0:T(8,128)(2,1)}, bf16[192,1024]{1,0:T(8,128)(2,1)S(1)}, u32[]{:S(2)}, u32[]{:S(2)}) collective-permute-start(bf16[192,1024]{1,0:T(8,128)(2,1)} %get-tuple-element.269.refs_8_), channel_id=1, source_target_pairs={{0,16},{8,24},{16,0},{24,8},{1,17},{9,25},{17,1},{25,9},{2,18},{10... | collective-permute-start | bytes 1179656 | tf_op jit(solution)/shard_map/ppermute | solution.py:735
  181.3 32.5 %collective-permute-start.25 = (bf16[192,1024]{1,0:T(8,128)(2,1)}, bf16[192,1024]{1,0:T(8,128)(2,1)S(1)}, u32[]{:S(2)}, u32[]{:S(2)}) collective-permute-start(bf16[192,1024]{1,0:T(8,128)(2,1)} %get-tuple-element.270.refs_9_), channel_id=1, source_target_pairs={{0,24},{8,16},{16,8},{24,0},{1,25},{9,17},{17,9},{25,1},{2,26},{10... | collective-permute-start | bytes 1179656 | tf_op jit(solution)/shard_map/ppermute | solution.py:735
  248.2 239.3 %reduce-scatter.3.cloned.1.call-start = ((), (), s32[]{:S(2)}) async-start(), calls=%async_computation.4 | async-start | bytes 7077888 | tf_op jit(solution)/shard_map/reduce_scatter | solution.py:929
  279.9 39.7 %collective-permute-start.26 = (bf16[192,1024]{1,0:T(8,128)(2,1)}, bf16[192,1024]{1,0:T(8,128)(2,1)S(1)}, u32[]{:S(2)}, u32[]{:S(2)}) collective-permute-start(bf16[192,1024]{1,0:T(8,128)(2,1)} %get-tuple-element.298), channel_id=1, source_target_pairs={{0,8},{8,0},{16,24},{24,16},{1,9},{9,1},{17,25},{25,17},{2,10},{10... | collective-permute-start | bytes 1179656 | tf_op jit(solution)/shard_map/ppermute | solution.py:735
  281.1 38.5 %collective-permute-start.27 = (bf16[192,1024]{1,0:T(8,128)(2,1)}, bf16[192,1024]{1,0:T(8,128)(2,1)S(1)}, u32[]{:S(2)}, u32[]{:S(2)}) collective-permute-start(bf16[192,1024]{1,0:T(8,128)(2,1)} %get-tuple-element.299), channel_id=1, source_target_pairs={{0,16},{8,24},{16,0},{24,8},{1,17},{9,25},{17,1},{25,9},{2,18},{10... | collective-permute-start | bytes 1179656 | tf_op jit(solution)/shard_map/ppermute | solution.py:735
  283.0 36.7 %collective-permute-start.28 = (bf16[192,1024]{1,0:T(8,128)(2,1)}, bf16[192,1024]{1,0:T(8,128)(2,1)S(1)}, u32[]{:S(2)}, u32[]{:S(2)}) collective-permute-start(bf16[192,1024]{1,0:T(8,128)(2,1)} %get-tuple-element.300), channel_id=1, source_target_pairs={{0,24},{8,16},{16,8},{24,0},{1,25},{9,17},{17,9},{25,1},{2,26},{10... | collective-permute-start | bytes 1179656 | tf_op jit(solution)/shard_map/ppermute | solution.py:735
  319.7 13.6 %collective-permute-start.29 = (bf16[192,1024]{1,0:T(8,128)(2,1)}, bf16[192,1024]{1,0:T(8,128)(2,1)S(1)}, u32[]{:S(2)}, u32[]{:S(2)}) collective-permute-start(bf16[192,1024]{1,0:T(8,128)(2,1)} %get-tuple-element.326), channel_id=1, source_target_pairs={{0,8},{8,0},{16,24},{24,16},{1,9},{9,1},{17,25},{25,17},{2,10},{10... | collective-permute-start | bytes 1179656 | tf_op jit(solution)/shard_map/ppermute | solution.py:735
  320.7 19.9 %collective-permute-start.30 = (bf16[192,1024]{1,0:T(8,128)(2,1)}, bf16[192,1024]{1,0:T(8,128)(2,1)S(1)}, u32[]{:S(2)}, u32[]{:S(2)}) collective-permute-start(bf16[192,1024]{1,0:T(8,128)(2,1)} %get-tuple-element.327), channel_id=1, source_target_pairs={{0,16},{8,24},{16,0},{24,8},{1,17},{9,25},{17,1},{25,9},{2,18},{10... | collective-permute-start | bytes 1179656 | tf_op jit(solution)/shard_map/ppermute | solution.py:735
  322.5 18.1 %collective-permute-start.31 = (bf16[192,1024]{1,0:T(8,128)(2,1)}, bf16[192,1024]{1,0:T(8,128)(2,1)S(1)}, u32[]{:S(2)}, u32[]{:S(2)}) collective-permute-start(bf16[192,1024]{1,0:T(8,128)(2,1)} %get-tuple-element.328), channel_id=1, source_target_pairs={{0,24},{8,16},{16,8},{24,0},{1,25},{9,17},{17,9},{25,1},{2,26},{10... | collective-permute-start | bytes 1179656 | tf_op jit(solution)/shard_map/ppermute | solution.py:735
  341.4 11.5 %collective-permute-start.32 = (bf16[16,48,1536]{2,1,0:T(8,128)(2,1)}, bf16[16,48,1536]{2,1,0:T(8,128)(2,1)S(1)}, u32[]{:S(2)}, u32[]{:S(2)}) collective-permute-start(bf16[16,48,1536]{2,1,0:T(8,128)(2,1)} %get-tuple-element.351), channel_id=1, source_target_pairs={{0,1},{1,0},{2,3},{3,2},{4,5},{5,4},{6,7},{7,6},{8,9},{9,8},{10,11... | collective-permute-start | bytes 7077896 | tf_op jit(solution)/shard_map/ppermute | solution.py:750
  341.4 24.4 %collective-permute-start.33 = (bf16[192,1024]{1,0:T(8,128)(2,1)}, bf16[192,1024]{1,0:T(8,128)(2,1)}, u32[]{:S(2)}, u32[]{:S(2)}) collective-permute-start(bf16[192,1024]{1,0:T(8,128)(2,1)} %get-tuple-element.357), channel_id=1, source_target_pairs={{0,8},{8,0},{16,24},{24,16},{1,9},{9,1},{17,25},{25,17},{2,10},{10... | collective-permute-start | bytes 1179656 | tf_op jit(solution)/shard_map/ppermute | solution.py:735
  342.3 23.5 %collective-permute-start.34 = (bf16[192,1024]{1,0:T(8,128)(2,1)}, bf16[192,1024]{1,0:T(8,128)(2,1)}, u32[]{:S(2)}, u32[]{:S(2)}) collective-permute-start(bf16[192,1024]{1,0:T(8,128)(2,1)} %get-tuple-element.358), channel_id=1, source_target_pairs={{0,16},{8,24},{16,0},{24,8},{1,17},{9,25},{17,1},{25,9},{2,18},{10... | collective-permute-start | bytes 1179656 | tf_op jit(solution)/shard_map/ppermute | solution.py:735
  344.0 21.8 %collective-permute-start.35 = (bf16[192,1024]{1,0:T(8,128)(2,1)}, bf16[192,1024]{1,0:T(8,128)(2,1)}, u32[]{:S(2)}, u32[]{:S(2)}) collective-permute-start(bf16[192,1024]{1,0:T(8,128)(2,1)} %get-tuple-element.359), channel_id=1, source_target_pairs={{0,24},{8,16},{16,8},{24,0},{1,25},{9,17},{17,9},{25,1},{2,26},{10... | collective-permute-start | bytes 1179656 | tf_op jit(solution)/shard_map/ppermute | solution.py:735
  366.8 13.0 %collective-permute-start.36 = (bf16[192,1024]{1,0:T(8,128)(2,1)S(1)}, bf16[192,1024]{1,0:T(8,128)(2,1)S(1)}, u32[]{:S(2)}, u32[]{:S(2)}) collective-permute-start(bf16[192,1024]{1,0:T(8,128)(2,1)S(1)} %copy-done.51), channel_id=1, source_target_pairs={{0,8},{8,0},{16,24},{24,16},{1,9},{9,1},{17,25},{25,17},{2,10},{10... | collective-permute-start | bytes 1179656 | tf_op jit(solution)/shard_map/ppermute | solution.py:735
  367.8 18.1 %collective-permute-start.37 = (bf16[192,1024]{1,0:T(8,128)(2,1)S(1)}, bf16[192,1024]{1,0:T(8,128)(2,1)S(1)}, u32[]{:S(2)}, u32[]{:S(2)}) collective-permute-start(bf16[192,1024]{1,0:T(8,128)(2,1)S(1)} %copy-done.50), channel_id=1, source_target_pairs={{0,16},{8,24},{16,0},{24,8},{1,17},{9,25},{17,1},{25,9},{2,18},{10... | collective-permute-start | bytes 1179656 | tf_op jit(solution)/shard_map/ppermute | solution.py:735
  369.5 17.5 %collective-permute-start.38 = (bf16[192,1024]{1,0:T(8,128)(2,1)S(1)}, bf16[192,1024]{1,0:T(8,128)(2,1)S(1)}, u32[]{:S(2)}, u32[]{:S(2)}) collective-permute-start(bf16[192,1024]{1,0:T(8,128)(2,1)S(1)} %copy-done.49), channel_id=1, source_target_pairs={{0,24},{8,16},{16,8},{24,0},{1,25},{9,17},{17,9},{25,1},{2,26},{10... | collective-permute-start | bytes 1179656 | tf_op jit(solution)/shard_map/ppermute | solution.py:735
  387.8 16.3 %collective-permute-start.39 = (bf16[4,48,1536]{2,1,0:T(8,128)(2,1)S(1)}, bf16[4,48,1536]{2,1,0:T(8,128)(2,1)S(1)}, u32[]{:S(2)}, u32[]{:S(2)}) collective-permute-start(bf16[4,48,1536]{2,1,0:T(8,128)(2,1)S(1)} %copy-done.23), channel_id=1, source_target_pairs={{0,8},{8,0},{16,24},{24,16},{1,9},{9,1},{17,25},{25,17},{2,10},{10... | collective-permute-start | bytes 1769480 | tf_op jit(solution)/shard_map/ppermute | solution.py:757
  388.8 26.5 %collective-permute-start.40 = (bf16[4,48,1536]{2,1,0:T(8,128)(2,1)S(1)}, bf16[4,48,1536]{2,1,0:T(8,128)(2,1)S(1)}, u32[]{:S(2)}, u32[]{:S(2)}) collective-permute-start(bf16[4,48,1536]{2,1,0:T(8,128)(2,1)S(1)} %copy-done.22), channel_id=1, source_target_pairs={{0,16},{8,24},{16,0},{24,8},{1,17},{9,25},{17,1},{25,9},{2,18},{10... | collective-permute-start | bytes 1769480 | tf_op jit(solution)/shard_map/ppermute | solution.py:757
  390.2 25.2 %collective-permute-start.41 = (bf16[4,48,1536]{2,1,0:T(8,128)(2,1)S(1)}, bf16[4,48,1536]{2,1,0:T(8,128)(2,1)S(1)}, u32[]{:S(2)}, u32[]{:S(2)}) collective-permute-start(bf16[4,48,1536]{2,1,0:T(8,128)(2,1)S(1)} %copy-done.21), channel_id=1, source_target_pairs={{0,24},{8,16},{16,8},{24,0},{1,25},{9,17},{17,9},{25,1},{2,26},{10... | collective-permute-start | bytes 1769480 | tf_op jit(solution)/shard_map/ppermute | solution.py:757
  391.4 25.0 %collective-permute-start.42 = (bf16[16,48,512]{2,1,0:T(8,128)(2,1)}, bf16[16,48,512]{2,1,0:T(8,128)(2,1)S(1)}, u32[]{:S(2)}, u32[]{:S(2)}) collective-permute-start(bf16[16,48,512]{2,1,0:T(8,128)(2,1)} %get-tuple-element.408), channel_id=1, source_target_pairs={{0,1},{1,0},{2,3},{3,2},{4,5},{5,4},{6,7},{7,6},{8,9},{9,8},{10,11... | collective-permute-start | bytes 2359304 | tf_op jit(solution)/shard_map/ppermute | solution.py:750
  416.7 20.6 %collective-permute-start.43 = (bf16[16,48,512]{2,1,0:T(8,128)(2,1)}, bf16[16,48,512]{2,1,0:T(8,128)(2,1)S(1)}, u32[]{:S(2)}, u32[]{:S(2)}) collective-permute-start(bf16[16,48,512]{2,1,0:T(8,128)(2,1)} %get-tuple-element.413), channel_id=1, source_target_pairs={{0,1},{1,0},{2,3},{3,2},{4,5},{5,4},{6,7},{7,6},{8,9},{9,8},{10,11... | collective-permute-start | bytes 2359304 | tf_op jit(solution)/shard_map/ppermute | solution.py:750
  416.7 13.2 %collective-permute-start.44 = (bf16[48,1536]{1,0:T(8,128)(2,1)}, bf16[48,1536]{1,0:T(8,128)(2,1)S(1)}, u32[]{:S(2)}, u32[]{:S(2)}) collective-permute-start(bf16[48,1536]{1,0:T(8,128)(2,1)} %get-tuple-element.422), channel_id=1, source_target_pairs={{0,2},{1,3},{2,0},{3,1},{4,6},{5,7},{6,4},{7,5},{8,10},{9,11},{10,... | collective-permute-start | bytes 442376 | tf_op jit(solution)/shard_map/ppermute | solution.py:760
  416.8 18.7 %collective-permute-start.45 = (bf16[48,1536]{1,0:T(8,128)(2,1)}, bf16[48,1536]{1,0:T(8,128)(2,1)S(1)}, u32[]{:S(2)}, u32[]{:S(2)}) collective-permute-start(bf16[48,1536]{1,0:T(8,128)(2,1)} %get-tuple-element.423), channel_id=1, source_target_pairs={{0,4},{1,5},{2,6},{3,7},{4,0},{5,1},{6,2},{7,3},{8,12},{9,13},{10,... | collective-permute-start | bytes 442376 | tf_op jit(solution)/shard_map/ppermute | solution.py:760
  416.9 20.2 %collective-permute-start.46 = (bf16[48,1536]{1,0:T(8,128)(2,1)}, bf16[48,1536]{1,0:T(8,128)(2,1)S(1)}, u32[]{:S(2)}, u32[]{:S(2)}) collective-permute-start(bf16[48,1536]{1,0:T(8,128)(2,1)} %get-tuple-element.424), channel_id=1, source_target_pairs={{0,6},{1,7},{2,4},{3,5},{4,2},{5,3},{6,0},{7,1},{8,14},{9,15},{10,... | collective-permute-start | bytes 442376 | tf_op jit(solution)/shard_map/ppermute | solution.py:760
  437.8 12.0 %collective-permute-start.47 = (bf16[4,48,1024]{2,1,0:T(8,128)(2,1)S(1)}, bf16[4,48,1024]{2,1,0:T(8,128)(2,1)S(1)}, u32[]{:S(2)}, u32[]{:S(2)}) collective-permute-start(bf16[4,48,1024]{2,1,0:T(8,128)(2,1)S(1)} %get-tuple-element.426), channel_id=1, source_target_pairs={{0,8},{8,0},{16,24},{24,16},{1,9},{9,1},{17,25},{25,17},{2,10},{10... | collective-permute-start | bytes 1179656 | tf_op jit(solution)/shard_map/ppermute | solution.py:757
  438.9 19.6 %collective-permute-start.48 = (bf16[4,48,1024]{2,1,0:T(8,128)(2,1)S(1)}, bf16[4,48,1024]{2,1,0:T(8,128)(2,1)S(1)}, u32[]{:S(2)}, u32[]{:S(2)}) collective-permute-start(bf16[4,48,1024]{2,1,0:T(8,128)(2,1)S(1)} %get-tuple-element.427), channel_id=1, source_target_pairs={{0,16},{8,24},{16,0},{24,8},{1,17},{9,25},{17,1},{25,9},{2,18},{10... | collective-permute-start | bytes 1179656 | tf_op jit(solution)/shard_map/ppermute | solution.py:757
  439.6 18.8 %collective-permute-start.49 = (bf16[4,48,1024]{2,1,0:T(8,128)(2,1)S(1)}, bf16[4,48,1024]{2,1,0:T(8,128)(2,1)S(1)}, u32[]{:S(2)}, u32[]{:S(2)}) collective-permute-start(bf16[4,48,1024]{2,1,0:T(8,128)(2,1)S(1)} %get-tuple-element.428), channel_id=1, source_target_pairs={{0,24},{8,16},{16,8},{24,0},{1,25},{9,17},{17,9},{25,1},{2,26},{10... | collective-permute-start | bytes 1179656 | tf_op jit(solution)/shard_map/ppermute | solution.py:757
  458.8 12.1 %collective-permute-start.51 = (bf16[48,1024]{1,0:T(8,128)(2,1)S(1)}, bf16[48,1024]{1,0:T(8,128)(2,1)S(1)}, u32[]{:S(2)}, u32[]{:S(2)}) collective-permute-start(bf16[48,1024]{1,0:T(8,128)(2,1)S(1)} %get-tuple-element.431), channel_id=1, source_target_pairs={{0,2},{1,3},{2,0},{3,1},{4,6},{5,7},{6,4},{7,5},{8,10},{9,11},{10,... | collective-permute-start | bytes 294920 | tf_op jit(solution)/shard_map/ppermute | solution.py:760
  (66 other events, 818.7 us)
Sparse Core Ops, SparseCore 0:
  13.3 94.4 all-gather.4
  110.8 78.6 all-gather.2
  248.3 115.1 reduce-scatter.4
  366.0 83.3 reduce-scatter.2

commit v3 on v2

--- a/solution.py
+++ b/solution.py
@@ -20,6 +20,14 @@
 
 def rows_by_rows(left, right):
     return lax.dot_general(left, right, (((1,), (1,)), ((), ())), preferred_element_type=f32)
+
+
+def turned_by_rows(left, right):
+    return lax.dot_general(left, right, (((0,), (1,)), ((), ())), preferred_element_type=f32)
+
+
+def turned_times(left, right):
+    return lax.dot_general(left, right, (((0,), (0,)), ((), ())), preferred_element_type=f32)
 
 
 def times(left, right):
@@ -364,9 +372,9 @@
         return self.refs[self.at - count : self.at]
 
 
-def feed_kernel(where, units_at, pieces_at, *refs, first, last, carried, settled, plain, slices, groups, parts, pieces):
+def feed_kernel(where, units_at, *refs, first, last, carried, settled, plain, slices, groups, parts):
     refs = Refs(refs)
-    grad_ref, weights = refs.take(), refs.take(pieces)
+    grad_ref, weights = refs.take(), refs.take()
     mixed = refs.take(groups) if first or last else None
     w_ref = refs.take() if last and not first else None
     if first:
@@ -391,7 +399,8 @@
             w_keeps, w_sends = refs.take(parts[0]), refs.take(parts[1])
     else:
         handed = refs.take(2 + 2 * last)
-    held, up_turned, down_turned, active, grad_pre, sum_up, sum_down, sems, loaded = refs.take(9)
+    held, active, grad_pre, sum_up, sum_down, sems, loaded = refs.take(7)
+    brought = refs.take(2 + 2 * last) if carried else ()
     if first or last:
         turned = refs.take()
     if last:
@@ -407,22 +416,23 @@
     sums = [sum_up, sum_down] + ([sum_w, sum_gain] if last else [])
 
     def bring():
-        return [pltpu.make_async_copy(carry[k], sums[k], sems.at[k]) for k in range(len(sums))]
+        return [pltpu.make_async_copy(carry[k], brought[k], sems.at[k]) for k in range(len(brought))]
+
+    def load(at):
+        side = pl.ds(at * units, WIDTH if at == 2 else units)
+        return pltpu.make_async_copy(weights.at[0, :, side], held.at[:, side], loaded.at[at])
 
     @pl.when(step == 0)
     def _():
-        if carried:
-            for copy in bring():
-                copy.start()
-        else:
-            for total in sums:
-                total[...] = jnp.zeros_like(total)
-        load_weight(pieces_at, weights, held, loaded)
+        for at in (2, 0, 1) if first else (0, 1):
+            load(at).start()
+        for copy in bring():
+            copy.start()
+        for total in sums:
+            total[...] = jnp.zeros_like(total)
         if first:
+            load(2).wait()
             w_out[...] = w_ref[...]
-        up_turned[...] = up_ref[...].T
-        for q in range(slices):
-            down_turned[:, pl.ds(q * WIDTH, WIDTH)] = downs[q][...].T
 
     if first or last:
         spread(turned, mixed, where[0])
@@ -433,12 +443,18 @@
         scaled_out[...] = scaled
     else:
         scaled = scaled_ref[...]
+
+    @pl.when(step == 0)
+    def _():
+        load(0).wait()
+        load(1).wait()
+
     grad = grad_ref[0]
     slab = 256
     for k in range(units // slab):
         at = pl.ds(k * slab, slab)
         inner = pl.ds(k * slab % WIDTH, slab)
-        pre = rows_by_rows(up_turned[at, :], scaled)
+        pre = turned_by_rows(up_ref[:, at], scaled)
         grad_active = rows_by_rows(downs[k * slab // WIDTH][inner, :], grad)
         square = pre * pre
         half = 0.5 + 0.5 * jnp.tanh(pre * (FIRST + SECOND * square))
@@ -446,17 +462,12 @@
         active[at, :] = act.astype(bf16)
         slope = half + act * (1.0 - half) * (2.0 * FIRST + 6.0 * SECOND * square)
         grad_pre[at, :] = (grad_active * slope).astype(bf16)
-    out = times(down_turned[...], active[...])
+    out = sum(
+        turned_times(downs[q][...], active[pl.ds(q * WIDTH, WIDTH), :]) for q in range(slices)
+    )
     back = times(up_ref[...], grad_pre[...])
     if not first:
         out, back = out + out_ref[...], back + back_ref[...]
-    if carried:
-
-        @pl.when(step == 0)
-        def _():
-            for copy in bring():
-                copy.wait()
-
     for q in range(slices):
         at = pl.ds(q * WIDTH, WIDTH)
         sum_down[at, :] += times(active[at, :], grad)
@@ -480,6 +491,10 @@
 
     @pl.when(final)
     def _():
+        for copy in bring():
+            copy.wait()
+        for total, more in zip(sums, brought):
+            total[...] += more[...].astype(f32)
         if settled:
             for q in range(slices):
                 at = pl.ds(q * WIDTH, WIDTH)
@@ -497,13 +512,8 @@
                 if last:
                     share_two(where[2], units_at, 0, w_keeps, w_sends, low, high)
         else:
-            copies = [
-                pltpu.make_async_copy(sums[k], handed[k], sems.at[k]) for k in range(len(sums))
-            ]
-            for copy in copies:
-                copy.start()
-            for copy in copies:
-                copy.wait()
+            for total, ref in zip(sums, handed):
+                ref[...] = total[...].astype(ref.dtype)
 
 
 def feed(where, units_at, item, chunk, grad, packed, w_out, tokens, mixed, state, carry, earlier, shapes, settled, after=()):
@@ -519,8 +529,7 @@
     wide = pl.BlockSpec((WIDTH, rows), lambda j, *_: (0, j))
     split = pl.BlockSpec((group, rows), lambda j, *_: (0, j))
     square = pl.BlockSpec((WIDTH, WIDTH), lambda j, *_: (0, 0), pipeline_mode=once)
-    weights, weights_at = packed
-    operands = [(grad, tall)] + [(w, ANY) for w in weights]
+    operands = [(grad, tall), (packed, ANY)]
     if first or last:
         operands += [(m, split) for m in mixed]
     if last and not first:
@@ -537,13 +546,16 @@
         outputs += [(shape(LENGTH, WIDTH, kind=f32), flat), (shape(LENGTH, WIDTH), flat), (shape(WIDTH, WIDTH), square)]
     if last:
         if carry:
-            aliases = {3 + len(operands): len(outputs)}
+            aliases = {2 + len(operands): len(outputs)}
             operands += [(e, ANY) for e in earlier]
         outputs += [(shape(*grad.shape), tall), (shape(LENGTH, WIDTH), flat)]
         outputs += [(shape(group, LENGTH), split)] * groups
     else:
         outputs += [(shape(WIDTH, LENGTH, kind=f32), wide)] * 2
     fixed = len(outputs)
+    handed = [shape(units, WIDTH)] * 2
+    if last:
+        handed += [shape(WIDTH, WIDTH), shape(1, WIDTH, kind=f32)]
     if settled:
         if plain:
             sizes = [shape(WIDTH, 2 * units), shape(WIDTH, WIDTH + 256)][: 1 + last]
@@ -556,21 +568,19 @@
             for u in sizes
         ]
     else:
-        sizes = [shape(units, WIDTH, kind=f32)] * 2
-        if last:
-            sizes += [shape(WIDTH, WIDTH, kind=f32), shape(1, WIDTH, kind=f32)]
-        outputs += [(u, ANY) for u in sizes]
+        sizes = handed
+        outputs += [(u, pl.BlockSpec(u.shape, lambda j, *_: (0, 0), pipeline_mode=once)) for u in sizes]
     scratch = [
         pltpu.VMEM((WIDTH, 2 * units + WIDTH * first), bf16),
-        pltpu.VMEM((units, WIDTH), bf16),
-        pltpu.VMEM((WIDTH, units), bf16),
         pltpu.VMEM((units, rows), bf16),
         pltpu.VMEM((units, rows), bf16),
         pltpu.VMEM((units, WIDTH), f32),
         pltpu.VMEM((units, WIDTH), f32),
         pltpu.SemaphoreType.DMA((4,)),
-        pltpu.SemaphoreType.DMA((sum(w.shape[0] for w in weights),)),
+        pltpu.SemaphoreType.DMA((3,)),
     ]
+    if carry:
+        scratch += [pltpu.VMEM(u.shape, u.dtype) for u in handed]
     if first or last:
         scratch += [pltpu.VMEM((WIDTH, rows), bf16)]
     if last:
@@ -592,11 +602,10 @@
             slices=slices,
             groups=groups,
             parts=parts,
-            pieces=len(weights),
         ),
         "feed",
         (LENGTH // rows,),
-        [where, units_at, weights_at],
+        [where, units_at],
         operands,
         outputs,
         scratch,
@@ -626,20 +635,19 @@
     else:
         handed = refs.take(2)
     turned, sum_w, sum_gain, low, high, sems = refs.take(6)
+    brought = refs.take(2) if carried else ()
     step = pl.program_id(0)
     sums = [sum_w, sum_gain]
 
+    def bring():
+        return [pltpu.make_async_copy(carry[k], brought[k], sems.at[k]) for k in range(2)] if carried else []
+
     @pl.when(step == 0)
     def _():
-        if carried:
-            copies = [pltpu.make_async_copy(carry[k], sums[k], sems.at[k]) for k in range(2)]
-            for copy in copies:
-                copy.start()
-            for copy in copies:
-                copy.wait()
-        else:
-            for total in sums:
-                total[...] = jnp.zeros_like(total)
+        for copy in bring():
+            copy.start()
+        for total in sums:
+            total[...] = jnp.zeros_like(total)
 
     spread(turned, grads, where[0])
     x = x_ref[0].astype(f32)
@@ -655,6 +663,10 @@
 
     @pl.when(step == pl.num_programs(0) - 1)
     def _():
+        for copy in bring():
+            copy.wait()
+        for total, more in zip(sums, brought):
+            total[...] += more[...]
         if settled:
             halves(sum_w[...].T, sum_gain[...], low, high)
             if plain:
@@ -709,7 +721,8 @@
             pltpu.VMEM((WIDTH, half), bf16),
             pltpu.VMEM((WIDTH, half), bf16),
             pltpu.SemaphoreType.DMA((2,)),
-        ],
+        ]
+        + [pltpu.VMEM((WIDTH, WIDTH), f32), pltpu.VMEM((1, WIDTH), f32)][: 2 * bool(carry)],
         4 * LENGTH * WIDTH * WIDTH,
         8 << 20,
         after,
@@ -783,7 +796,9 @@
         return [add(keep, got[b * n : (b + 1) * n]) for b, keep in enumerate(keeps)]
 
     def scatter_plane(self, parts):
-        parts = [parts[0]] + [self.over(parts[b], b) for b in range(1, self.groups)]
+        return self.join_plane([parts[0]] + [self.over(parts[b], b) for b in range(1, self.groups)])
+
+    def join_plane(self, parts):
         return [add(*[part[s] for part in parts]) for s in range(self.rings)]
 
     def scatter_line(self, own):
@@ -825,18 +840,18 @@
     logits_low = logits.astype(bf16)
     block = logits.shape[1]
     shares_at, shares = [0], ((1, LENGTH),)
-    whole = [lax.all_gather(w, ALL, axis=0, tiled=True)[None] for w in weights[fast:]]
+    early = weights[1:2] if fast else weights
+    whole = [lax.all_gather(w, ALL, axis=0, tiled=True)[None] for w in early]
     weights_at = [jnp.zeros((2,), jnp.int32)] * (1 + CHUNKS)
     if fast:
         rings = chips.rings
         whole = [None] + whole
-        value_mine, lengths_here = hold(value_mine, exchange([lengths] * groups))
         other = chips.across(value_mine)
         value_unit = jnp.where(
             core == 0, jnp.concatenate([value_mine, other]), jnp.concatenate([other, value_mine])
         )
         weights_at[0] = chips.gathered_at(2 * shard)
-        zs = [(chips.z - s) % rings for s in range(rings)]
+        zs = [(chips.z - s) % rings for s in (0, 1, 3, 2)]
         logits_at = [(2 * z + c) * block for c in (core, 1 - core) for z in zs]
         shapes = (((rings, 2 * shard),) * groups, ((groups * rings, 2 * shard),))
         order = chips.unit_order(2 * shard)
@@ -849,9 +864,18 @@
     logits_at, shares_at = (
         jnp.stack([jnp.asarray(v, jnp.int32) for v in at]) for at in (logits_at, shares_at)
     )
-    if not fast:
-        lengths_here = exchange([lengths] * groups)
-    lengths_here = jnp.stack(lengths_here, axis=1).reshape(-1)
+    def fed(pairs):
+        ups, downs = (jnp.concatenate(parts, axis=1).astype(f32) for parts in zip(*pairs))
+        sum_up = ups.reshape(shard, slices, ranks, shard).swapaxes(1, 2).reshape(shard, HIDDEN)
+        sum_down = downs.reshape(shard, slices, WIDTH).swapaxes(0, 1)
+        return sum_up * second_gain, sum_down.reshape(shard * slices, WIDTH)
+
+    def joined(pair):
+        low, high = (part.astype(f32) for part in pair)
+        return jnp.concatenate([low[:, :half], high[:, :half]], axis=1), low[:, half] + high[:, half]
+
+    def lengths_of():
+        return jnp.stack(exchange([lengths] * groups), axis=1).reshape(-1)
 
     def values_of(after=()):
         return project_values(where, weights_at[0], tokens, value_parts, groups, after)
@@ -861,7 +885,7 @@
 
     def run_feed(item, chunk, packed, w_out_all, mixed, state, carry, result, after=()):
         return feed(
-            where, order, item, chunk, cotangent, (packed, weights_at[1 + chunk]), w_out_all, tokens,
+            where, order, item, chunk, cotangent, packed, w_out_all, tokens,
             mixed, state, carry, (result,), shapes if chunk else None, item == items - 1, after,
         )
 
@@ -879,38 +903,39 @@
     if fast:
         assert items == 2 and CHUNKS == 2
         value_ring = chips.gather_line(value_unit)
-        value_ring, logits_low = hold(value_ring, logits_low)
+        value_ring, logits_low, second, lengths_here = hold(
+            value_ring, logits_low, weights[2], lengths_of()
+        )
         value_parts = chips.gather_plane(value_ring)
-        ring_one = chips.along(logits_low, 1)
+        next_one, last_one = chips.along(logits_low, 1), chips.along(logits_low, 3)
         values, value_all = values_of()
-        values, ring_one = hold(values, ring_one)
         values = exchange(values)
-        ring_two = chips.along(ring_one, 1)
-        cross_zero = chips.across(logits_low)
-        values, ring_two, cross_zero = hold(values, ring_two, cross_zero)
-        ring_three = chips.along(ring_two, 1)
-        cross_one, cross_two = chips.across(ring_one), chips.across(ring_two)
-        ring_three, cross_one, cross_two = hold(ring_three, cross_one, cross_two)
-        logits_parts = [logits_low, ring_one, ring_two, ring_three]
-        logits_parts += [cross_zero, cross_one, cross_two, chips.across(ring_three)]
+        next_two = chips.along(next_one, 1)
+        values, logits_low = hold(values, logits_low)
+        next_two, last_one, values = hold(next_two, last_one, values)
+        logits_parts = [logits_low, next_one, last_one, next_two]
+        logits_parts += [chips.across(r) for r in logits_parts]
         mixed_out_a, sums_a = mix(0, values)
-        mixed_out_a, sums_a = hold(mixed_out_a, sums_a)
+        mixed_out_a, sums_a, second = hold(mixed_out_a, sums_a, second)
+        second = lax.all_gather(second, ALL, axis=0, tiled=True)
         mixed_a = exchange(mixed_out_a)
         mixed_out_b, sums_b = mix(1, values)
         mixed_out_b, mixed_a = hold(mixed_out_b, mixed_a)
         mixed_b = exchange(mixed_out_b)
-        state_a, carry = run_feed(0, 0, whole[1:2], None, mixed_a, None, (), None)
+        first = whole[1]
+        state_a, carry = run_feed(0, 0, first, None, mixed_a, None, (), None)
         state_a, carry, mixed_b = hold(state_a, carry, mixed_b)
         w_out_all = state_a[2]
-        state_b, (shared,) = run_feed(1, 0, whole[1:2], None, mixed_b, None, carry, None)
+        state_b, (shared,) = run_feed(1, 0, first, None, mixed_b, None, carry, None)
         first_sums = lax.psum_scatter(shared, ALL, scatter_dimension=0, tiled=True)
         state_a = state_a[:2] + state_a[3:]
         state_b = state_b[:2] + state_b[3:]
-        out_a, carry = run_feed(0, 1, whole[2:3], w_out_all, mixed_a, state_a, (), None)
+        second = second[None]
+        out_a, carry = run_feed(0, 1, second, w_out_all, mixed_a, state_a, (), None)
         out_a, carry = hold(out_a, carry)
         grads_a = exchange(out_a[2:])
         out_b, (second_shared, out_shared) = run_feed(
-            1, 1, whole[2:3], w_out_all, mixed_b, state_b, carry, out_a[0]
+            1, 1, second, w_out_all, mixed_b, state_b, carry, out_a[0]
         )
         out_b, grads_a, second_shared, out_shared = hold(out_b, grads_a, second_shared, out_shared)
         result = out_b[0]
@@ -921,31 +946,36 @@
         )
         back_a = exchange(back_a)
         back_b, left_b = back(1, grads_b, mixed_out_b, sums_b)
-        second_sums = chips.scatter_core(second_shared)
+        second_sums, out_sums = chips.scatter_core(second_shared), chips.scatter_core(out_shared)
+        second_sums = [jnp.concatenate(pair, axis=2) for pair in zip(second_sums, out_sums)]
         back_b, left_b, second_sums = hold(back_b, left_b, second_sums)
         back_b = exchange(back_b)
         grad_logits = logits_back(lengths_here, shares_at, [left_a, left_b], values, shares)
-        grad_logits, back_a, second_sums, out_shared = hold(grad_logits, back_a, second_sums, out_shared)
+        grad_logits, back_a, second_sums = hold(grad_logits, back_a, second_sums)
         grad_mixer = lax.psum_scatter(grad_logits[0][0], "seq", scatter_dimension=1, tiled=True)
         grad_tokens, carry = close(0, out_a[1], back_a, (), None)
-        carry, back_b, grad_tokens, second_sums, out_shared = hold(
-            carry, back_b, grad_tokens, second_sums, out_shared
+        carry, back_b, grad_tokens, second_sums = hold(carry, back_b, grad_tokens, second_sums)
+        second_plane = [chips.over(second_sums[b], b) for b in range(1, groups)]
+        grad_tokens, shared = close(1, out_b[1], back_b, carry, grad_tokens)
+        shared, second_plane[:2] = hold(shared, second_plane[:2])
+        value_sums = chips.scatter_core(shared)
+        value_sums, second_plane[2:] = hold(value_sums, second_plane[2:])
+        second_sums = chips.join_plane([second_sums[0]] + list(second_plane))
+        second_line = [chips.hop(second_sums[k], k) for k in range(1, rings)]
+        value_sums = chips.scatter_plane(value_sums)
+        value_sums, second_line = hold(value_sums, second_line)
+        value_line = [chips.hop(value_sums[k], k) for k in range(1, rings)]
+        second_sums = chips.settle(add(second_sums[0], *second_line))
+        wide = width * WIDTH
+        sum_up, sum_down = fed([halved(first_sums), tuple(part[:, :wide] for part in second_sums)])
+        sum_out, gain_two_sum = joined([part[:, wide:] for part in second_sums])
+        grad_mixer = grad_mixer.astype(f32) * logits
+        value_line, grad_mixer, sum_up, sum_down, sum_out, gain_two_sum = hold(
+            value_line, grad_mixer, sum_up, sum_down, sum_out, gain_two_sum
         )
-        second_sums = chips.scatter_plane(second_sums)
-        out_sums = chips.scatter_core(out_shared)
-        grad_tokens, shared = close(1, out_b[1], back_b, carry, grad_tokens)
-        shared, second_sums, out_sums = hold(shared, second_sums, out_sums)
-        second_sums = chips.scatter_line(second_sums)
-        value_sums = chips.scatter_core(shared)
-        small_sums = [jnp.concatenate(pair, axis=2) for pair in zip(value_sums, out_sums)]
-        small_sums, second_sums = hold(small_sums, second_sums)
-        small_sums = chips.scatter_plane(small_sums)
-        second_sums = chips.settle(second_sums)
-        small_sums, second_sums = hold(small_sums, second_sums)
-        low, high = chips.settle(chips.scatter_line(small_sums))
-        small = half + 128
-        settled = [halved(first_sums), second_sums, (low[:, small:], high[:, small:]), (low[:, :small], high[:, :small])]
-    else:
+        settled = [chips.settle(add(value_sums[0], *value_line))]
+    else:
+        lengths_here = lengths_of()
         values, value_all = values_of()
         values = exchange(values)
         mixed_out, sums, mixed = [], [], []
@@ -960,7 +990,7 @@
             carry = ()
             for item in range(items):
                 state, carry = run_feed(
-                    item, chunk, whole[1 + chunk : 2 + chunk], w_out_all, mixed[item], states[item], carry, result
+                    item, chunk, whole[1 + chunk], w_out_all, mixed[item], states[item], carry, result
                 )
                 if chunk == CHUNKS - 1:
                     result, grad_hidden[item], grads[item] = state[0], state[1], exchange(state[2:])
@@ -983,19 +1013,11 @@
         shared += carry
         grad_mixer = lax.psum_scatter(grad_logits[0][0], "seq", scatter_dimension=1, tiled=True)
         settled = [halved(lax.psum_scatter(x, ALL, scatter_dimension=0, tiled=True)) for x in shared]
-    grad_mixer = grad_mixer.astype(f32) * logits
-    ups = jnp.concatenate([pair[0] for pair in settled[:CHUNKS]], axis=1)
-    downs = jnp.concatenate([pair[1] for pair in settled[:CHUNKS]], axis=1)
-    sum_up = ups.astype(f32).reshape(shard, slices, ranks, shard).swapaxes(1, 2).reshape(shard, HIDDEN)
-    sum_up = sum_up * second_gain
-    sum_down = downs.astype(f32).reshape(shard, slices, WIDTH).swapaxes(0, 1).reshape(shard * slices, WIDTH)
-
-    def joined(pair):
-        low, high = (part.astype(f32) for part in pair)
-        return jnp.concatenate([low[:, :half], high[:, :half]], axis=1), low[:, half] + high[:, half]
-
-    sum_out, gain_two_sum = joined(settled[CHUNKS])
-    sum_value, gain_one_sum = joined(settled[CHUNKS + 1])
+    if not fast:
+        sum_up, sum_down = fed(settled[:CHUNKS])
+        sum_out, gain_two_sum = joined(settled[CHUNKS])
+        grad_mixer = grad_mixer.astype(f32) * logits
+    sum_value, gain_one_sum = joined(settled[-1])
     return (
         result,
         grad_tokens,

time: 503 us -> 457 us (0.909)
  waiting for transfers between devices: 184 us -> 140 us
  Pallas kernels: 201 us -> 191 us
  starting transfers between devices: 62.9 us -> 68.2 us
    ppermute x24, waiting for transfers between devices: 79.8 us -> 63.9 us  [exchange(): lax.ppermute(parts[r], 'dp', [(i, i ^ r) for i in range(len(parts))])]
    ppermute x3, waiting for transfers between devices: 23.2 us -> 9.09 us  [along(): lax.ppermute(array, 'seq', [(i, (i + 2 * step) % n) for i in range(n)])]
    ppermute x9, waiting for transfers between devices: 45.2 us -> 34.2 us  [over(): lax.ppermute(array, 'dp', [(i, i ^ bits) for i in range(self.groups)])]
    pallas_call x12, Pallas kernels: 201 us -> 191 us  [call(): pl.pallas_call(run, grid_spec=pltpu.PrefetchScalarGridSpec(num_scalar_pre...]
  transfers between devices with their start and end apart: 59 -> 59, of which waited for: 32 -> 25; matrix products, arithmetic and copies ran while one was open for 4% -> 6% of each run, Pallas kernels for 41% -> 42%
where the time goes in v3:
time: 457 us; the launch traced here: 450 us
  Pallas kernels  191 us (42%)
  waiting for transfers between devices  140 us (31%)
  starting transfers between devices  68.2 us (15%)
  other arithmetic  19.5 us (4%)
  local copies, waits for them, and re-layouts  17.4 us (4%)
  between operations  14.8 us (3%)
    pallas_call x12, Pallas kernels, call(): pl.pallas_call(run, grid_spec=pltpu.PrefetchScalarGridSpec(num_scalar_pre...  191 us
    ppermute x24, waiting for transfers between devices, exchange(): lax.ppermute(parts[r], 'dp', [(i, i ^ r) for i in range(len(parts))])  63.9 us
    ppermute x9, waiting for transfers between devices, over(): lax.ppermute(array, 'dp', [(i, i ^ bits) for i in range(self.groups)])  34.2 us
    ppermute x24, starting transfers between devices, exchange(): lax.ppermute(parts[r], 'dp', [(i, i ^ r) for i in range(len(parts))])  29.3 us
    ppermute x9, waiting for transfers between devices, hop(): lax.ppermute(array, 'seq', [(i, i ^ 2 * step) for i in range(self.seqs)])  28.6 us
    ppermute x9, starting transfers between devices, hop(): lax.ppermute(array, 'seq', [(i, i ^ 2 * step) for i in range(self.seqs)])  22.2 us
    ppermute x9, starting transfers between devices, over(): lax.ppermute(array, 'dp', [(i, i ^ bits) for i in range(self.groups)])  10.6 us
  transfers between devices with their start and end apart: 59, of which 25 were waited for; matrix products, arithmetic and copies ran while one was open for 6% of the time, Pallas kernels for 42%

profile of v3, /device:TPU:0, one launch (start us, length us, event | category | flops | bytes accessed | tf_op | source)
XLA Modules:
  0.0 450.3 jit_solution(13120701589153304570)
XLA Ops:
  13.2 3.0 collective-permute-start.4
  22.1 3.7 collective-permute-start.3
  26.5 2.4 collective-permute-done.3
  28.9 4.7 %collective-permute-done.2 = bf16[48,768]{1,0:T(8,128)(2,1)S(1)} collective-permute-done((bf16[48,768]{1,0:T(8,128)(2,1)S(1)}, bf16[48,768]{1,0:T(8,128)(2,1)S(1)}, u32[]{:S(2)}, u32[]{:S(2)}) %collective-permute-start.2) | collective-permute-done | bytes 73760 | tf_op jit(solution)/shard_map/ppermute | solution.py:773
  34.7 2.7 collective-permute-start.12
  39.4 6.2 %collective-permute-done.12.refs_6_ = bf16[4,48,768]{2,1,0:T(8,128)(2,1)S(1)} collective-permute-done((bf16[4,48,768]{2,1,0:T(8,128)(2,1)S(1)}, bf16[4,48,768]{2,1,0:T(8,128)(2,1)S(1)}, u32[]{:S(2)}, u32[]{:S(2)}) %collective-permute-start.12) | collective-permute-done | bytes 294944 | tf_op jit(solution)/shard_map/ppermute | solution.py:770
  45.6 4.1 collective-permute-done.11.refs_5_
  51.1 8.8 %project_values.1 = (bf16[2,192,1024]{2,1,0:T(8,128)(2,1)}, bf16[2,192,1024]{2,1,0:T(8,128)(2,1)}, bf16[2,192,1024]{2,1,0:T(8,128)(2,1)}, bf16[2,192,1024]{2,1,0:T(8,128)(2,1)}, bf16[768,768]{1,0:T(8,128)(2,1)}) custom-call(s32[3]{0:T(128)} %pad_add_fusion.1.refs_0_, s32[32]{0:T(128)} %stack.176.refs_1_, bf16[2,1024,768]{2,1,0:T(8,128)(2,1)} %refs_2_.13, ...), custom_call_target="tpu_custom_call" | custom-call | flops 2415919 | bytes 6291 | tf_op jit(solution)/shard_map/project_values/pallas_call | solution.py:76
  63.5 3.3 collective-permute-start.9
  66.8 16.9 %collective-permute-done.13.refs_3_.refs_5_ = bf16[2,192,1024]{2,1,0:T(8,128)(2,1)S(1)} collective-permute-done((bf16[2,192,1024]{2,1,0:T(8,128)(2,1)}, bf16[2,192,1024]{2,1,0:T(8,128)(2,1)S(1)}, u32[]{:S(2)}, u32[]{:S(2)}) %collective-permute-start.13) | collective-permute-done | bytes 786464 | tf_op jit(solution)/shard_map/ppermute | solution.py:748
  83.8 20.0 %collective-permute-done.15.refs_5_.refs_7_ = bf16[2,192,1024]{2,1,0:T(8,128)(2,1)S(1)} collective-permute-done((bf16[2,192,1024]{2,1,0:T(8,128)(2,1)}, bf16[2,192,1024]{2,1,0:T(8,128)(2,1)S(1)}, u32[]{:S(2)}, u32[]{:S(2)}) %collective-permute-start.15) | collective-permute-done | bytes 786464 | tf_op jit(solution)/shard_map/ppermute | solution.py:748
  103.8 9.1 %collective-permute-done.8.refs_9_.refs_14_ = bf16[3,128,1024]{2,1,0:T(8,128)(2,1)S(1)} collective-permute-done((bf16[3,128,1024]{2,1,0:T(8,128)(2,1)S(1)}, bf16[3,128,1024]{2,1,0:T(8,128)(2,1)S(1)}, u32[]{:S(2)}, u32[]{:S(2)}) %collective-permute-start.8) | collective-permute-done | bytes 786464 | tf_op jit(solution)/shard_map/ppermute | solution.py:767
  116.5 7.6 %mix_items.2 = (bf16[192,1024]{1,0:T(8,128)(2,1)}, bf16[192,1024]{1,0:T(8,128)(2,1)}, bf16[192,1024]{1,0:T(8,128)(2,1)}, bf16[192,1024]{1,0:T(8,128)(2,1)}, f32[3,8,1024]{2,1,0:T(8,128)}) custom-call(s32[8]{0:T(128)} %reshape.184.refs_0_, s32[8]{0:T(128)} %stack.175.refs_1_, bf16[2,192,1024]{2,1,0:T(8,128)(2,1)} %get-tuple-element.227.refs_2_.refs_4_, ...), custom_call_target="tpu_custom_call" | custom-call | flops 1711276 | bytes 12582 | tf_op jit(solution)/shard_map/mix_items/pallas_call | solution.py:76
  126.0 2.2 collective-permute-start.22
  128.3 7.4 %mix_items.3 = (bf16[192,1024]{1,0:T(8,128)(2,1)}, bf16[192,1024]{1,0:T(8,128)(2,1)}, bf16[192,1024]{1,0:T(8,128)(2,1)}, bf16[192,1024]{1,0:T(8,128)(2,1)}, f32[3,8,1024]{2,1,0:T(8,128)}) custom-call(s32[8]{0:T(128)} %reshape.184.refs_0_, s32[8]{0:T(128)} %stack.175.refs_1_, bf16[2,192,1024]{2,1,0:T(8,128)(2,1)} %get-tuple-element.227.refs_2_.refs_4_, ...), custom_call_target="tpu_custom_call" | custom-call | flops 1711276 | bytes 12582 | tf_op jit(solution)/shard_map/mix_items/pallas_call | solution.py:76
  137.0 7.3 %collective-permute-done.21.refs_6_ = bf16[192,1024]{1,0:T(8,128)(2,1)S(1)} collective-permute-done((bf16[192,1024]{1,0:T(8,128)(2,1)}, bf16[192,1024]{1,0:T(8,128)(2,1)S(1)}, u32[]{:S(2)}, u32[]{:S(2)}) %collective-permute-start.21) | collective-permute-done | bytes 393248 | tf_op jit(solution)/shard_map/ppermute | solution.py:748
  145.5 2.0 collective-permute-start.23
  149.6 27.4 %feed.4 = (f32[1024,768]{1,0:T(8,128)}, bf16[1024,768]{1,0:T(8,128)(2,1)}, bf16[768,768]{1,0:T(8,128)(2,1)}, f32[768,1024]{1,0:T(8,128)}, f32[768,1024]{1,0:T(8,...) custom-call(s32[3]{0:T(128)} %pad_add_fusion.1.refs_0_, s32[16]{0:T(128)} %stack.157.refs_1_, ...), custom_call_target="tpu_custom_call" | custom-call | flops 14495514 | bytes 20971 | tf_op jit(solution)/shard_map/feed/pallas_call | solution.py:76
  178.1 29.7 %feed.5 = (f32[1024,768]{1,0:T(8,128)}, bf16[1024,768]{1,0:T(8,128)(2,1)}, bf16[768,768]{1,0:T(8,128)(2,1)}, f32[768,1024]{1,0:T(8,128)}, f32[768,1024]{1,0:T(8,128)}, /*index=5*/bf16[768,3072]{1,0:T(8,128)(2,1)}) custom-call(s32[3]{0:T(128)} %pad_add_fusion.1.refs_0_, s32[16]{0:T(128)} %stack.157.refs_1_, bf16[2,1024,768]{2,1,0:T(8,128)(2,1)} %refs_2_.11, ...), custom_call_target="tpu_custom_call" | custom-call | flops 14495514 | bytes 20971 | tf_op jit(solution)/shard_map/feed/pallas_call | solution.py:76
  207.9 30.4 %feed.6 = (bf16[2,1024,768]{2,1,0:T(8,128)(2,1)}, bf16[1024,768]{1,0:T(8,128)(2,1)}, bf16[192,1024]{1,0:T(8,128)(2,1)}, bf16[192,1024]{1,0:T(8,128)(2,1)}, bf16[...) custom-call(s32[3]{0:T(128)} %pad_add_fusion.1.refs_0_, ...), custom_call_target="tpu_custom_call" | custom-call | flops 14495514 | bytes 20971 | tf_op jit(solution)/shard_map/feed/pallas_call | solution.py:76
  238.3 2.0 collective-permute-start.26
  241.9 35.0 %feed.7 = (bf16[2,1024,768]{2,1,0:T(8,128)(2,1)}, bf16[1024,768]{1,0:T(8,128)(2,1)}, bf16[192,1024]{1,0:T(8,128)(2,1)}, bf16[192,1024]{1,0:T(8,128)(2,1)}, bf16[...) custom-call(s32[3]{0:T(128)} %pad_add_fusion.1.refs_0_, ...), custom_call_target="tpu_custom_call", output_to_operand_aliasing={{0}: (17, {})} | custom-call | flops 14495514 | bytes 20971 | tf_op jit(solution)/shard_map/feed/pallas_call | solution.py:76
  277.0 2.0 collective-permute-start.29
  280.5 7.9 %values_back.2 = (bf16[192,1024]{1,0:T(8,128)(2,1)}, bf16[192,1024]{1,0:T(8,128)(2,1)}, bf16[192,1024]{1,0:T(8,128)(2,1)}, bf16[192,1024]{1,0:T(8,128)(2,1)}, bf16[3,272,1024]{2,1,0:T(8,128)(2,1)}) custom-call(s32[8]{0:T(128)} %reshape.184.refs_0_, s32[8]{0:T(128)} %stack.175.refs_1_, bf16[192,1024]{1,0:T(8,128)(2,1)} %get-tuple-element.308.refs_2_, ...), custom_call_target="tpu_custom_call" | custom-call | flops 1711276 | bytes 14680 | tf_op jit(solution)/shard_map/values_back/pallas_call | solution.py:76
  289.3 2.7 collective-permute-done.30.refs_4_
  292.0 5.4 %collective-permute-done.31.refs_5_ = bf16[192,1024]{1,0:T(8,128)(2,1)S(1)} collective-permute-done((bf16[192,1024]{1,0:T(8,128)(2,1)}, bf16[192,1024]{1,0:T(8,128)(2,1)S(1)}, u32[]{:S(2)}, u32[]{:S(2)}) %collective-permute-start.31) | collective-permute-done | bytes 393248 | tf_op jit(solution)/shard_map/ppermute | solution.py:748
  300.5 1.8 collective-permute-start.36
  302.3 8.3 %values_back.3 = (bf16[192,1024]{1,0:T(8,128)(2,1)}, bf16[192,1024]{1,0:T(8,128)(2,1)}, bf16[192,1024]{1,0:T(8,128)(2,1)}, bf16[192,1024]{1,0:T(8,128)(2,1)}, bf16[3,272,1024]{2,1,0:T(8,128)(2,1)}) custom-call(s32[8]{0:T(128)} %reshape.184.refs_0_, s32[8]{0:T(128)} %stack.175.refs_1_, bf16[192,1024]{1,0:T(8,128)(2,1)} %get-tuple-element.333.refs_2_, ...), custom_call_target="tpu_custom_call" | custom-call | flops 1711276 | bytes 14680 | tf_op jit(solution)/shard_map/values_back/pallas_call | solution.py:76
  310.6 1.6 add_convert_fusion.12
  315.4 9.8 %logits_back.1 = bf16[1,3,1024,1024]{3,2,1,0:T(8,128)(2,1)} custom-call(s32[8]{0:T(128)} %reshape.184.refs_0_, s32[1]{0:T(128)} %constant.68.clone.1.refs_1_, bf16[3,272,1024]{2,1,0:T(8,128)(2,1)} %get-tuple-element.332.refs_2_, bf16[3,272,1024]{2,1,0:T(8,128)(2,1)} %get-tuple-element.353.refs_3_, bf16[2,192,1024]{2,1,0:T(8,128)(2,1)} %get-tuple-element.227.refs_2_.refs_4_, ...), custom_call_target="tpu_custom_call" | custom-call | flops 3422552 | bytes 14680 | tf_op jit(solution)/shard_map/logits_back/pallas_call | solution.py:76
  327.9 1.8 collective-permute-start.39
  329.7 9.2 %grad_tokens.2 = (bf16[2,1024,768]{2,1,0:T(8,128)(2,1)}, f32[768,768]{1,0:T(8,128)}, f32[1,768]{1,0:T(1,128)}) custom-call(s32[3]{0:T(128)} %pad_add_fusion.1.refs_0_, s32[16]{0:T(128)} %stack.157.refs_1_, bf16[2,1024,768]{2,1,0:T(8,128)(2,1)} %refs_2_.13, bf16[1024,768]{1,0:T(8,128)(2,1)} %get-tuple-element.307.refs_3_, ...), custom_call_target="tpu_custom_call" | custom-call | flops 2415919 | bytes 8388 | tf_op jit(solution)/shard_map/grad_tokens/pallas_call | solution.py:76
  338.9 6.4 %collective-permute-done.38.refs_7_ = bf16[192,1024]{1,0:T(8,128)(2,1)S(1)} collective-permute-done((bf16[192,1024]{1,0:T(8,128)(2,1)}, bf16[192,1024]{1,0:T(8,128)(2,1)S(1)}, u32[]{:S(2)}, u32[]{:S(2)}) %collective-permute-start.38) | collective-permute-done | bytes 393248 | tf_op jit(solution)/shard_map/ppermute | solution.py:748
  345.3 1.5 collective-permute-start.40
  347.1 9.1 %grad_tokens.3 = (bf16[2,1024,768]{2,1,0:T(8,128)(2,1)}, bf16[4,48,512]{2,1,0:T(8,128)(2,1)}, bf16[4,48,512]{2,1,0:T(8,128)(2,1)}, bf16[4,48,512]{2,1,0:T(8,128)...) custom-call(s32[3]{0:T(128)} %pad_add_fusion.1.refs_0_, ...), custom_call_target="tpu_custom_call", output_to_operand_aliasing={{0}: (11, {})} | custom-call | flops 2415919 | bytes 8388 | tf_op jit(solution)/shard_map/grad_tokens/pallas_call | solution.py:76
  356.3 6.5 %collective-permute-done.40 = bf16[4,48,2048]{2,1,0:T(8,128)(2,1)S(1)} collective-permute-done((bf16[4,48,2048]{2,1,0:T(8,128)(2,1)}, bf16[4,48,2048]{2,1,0:T(8,128)(2,1)S(1)}, u32[]{:S(2)}, u32[]{:S(2)}) %collective-permute-start.40) | collective-permute-done | bytes 786464 | tf_op jit(solution)/shard_map/ppermute | solution.py:770
  363.6 1.8 collective-permute-start.43
  366.2 1.7 add_convert_fusion.8
  368.0 16.6 %collective-permute-done.43 = bf16[4,48,2048]{2,1,0:T(8,128)(2,1)} collective-permute-done((bf16[4,48,2048]{2,1,0:T(8,128)(2,1)S(1)}, bf16[4,48,2048]{2,1,0:T(8,128)(2,1)}, u32[]{:S(2)}, u32[]{:S(2)}) %collective-permute-start.43) | collective-permute-done | bytes 786464 | tf_op jit(solution)/shard_map/ppermute | solution.py:770
  385.2 1.7 collective-permute-start.45
  388.0 1.5 fusion.6
  389.5 12.6 %collective-permute-start.49 = (bf16[48,2048]{1,0:T(8,128)(2,1)S(1)}, bf16[48,2048]{1,0:T(8,128)(2,1)S(1)}, u32[]{:S(2)}, u32[]{:S(2)}) collective-permute-start(bf16[48,2048]{1,0:T(8,128)(2,1)S(1)} %get-tuple-element.423), channel_id=1, source_target_pairs={{0,6},{1,7},{2,4},{3,5},{4,2},{5,3},{6,0},{7,1},{8,14},{9,15},{10,... | collective-permute-start | bytes 589832 | tf_op jit(solution)/shard_map/ppermute | solution.py:773
  402.9 9.4 %collective-permute-done.49 = bf16[48,2048]{1,0:T(8,128)(2,1)S(1)} collective-permute-done((bf16[48,2048]{1,0:T(8,128)(2,1)S(1)}, bf16[48,2048]{1,0:T(8,128)(2,1)S(1)}, u32[]{:S(2)}, u32[]{:S(2)}) %collective-permute-start.49) | collective-permute-done | bytes 196640 | tf_op jit(solution)/shard_map/ppermute | solution.py:773
  412.3 12.2 %collective-permute-done.48 = bf16[48,2048]{1,0:T(8,128)(2,1)S(1)} collective-permute-done((bf16[48,2048]{1,0:T(8,128)(2,1)S(1)}, bf16[48,2048]{1,0:T(8,128)(2,1)S(1)}, u32[]{:S(2)}, u32[]{:S(2)}) %collective-permute-start.48) | collective-permute-done | bytes 196640 | tf_op jit(solution)/shard_map/ppermute | solution.py:773
  425.8 1.6 collective-permute-start.51
  427.4 2.8 collective-permute-start.52
  435.7 1.8 reshape.193
  438.3 2.6 convert_multiply_fusion
  (237 shorter events, 59.4 us)
Async XLA Ops:
  7.2 142.4 %all-gather.5.cloned.1.call-start = ((), (), s32[]{:S(2)}) async-start(), calls=%async_computation.3 | async-start | bytes 6082560 | tf_op jit(solution)/shard_map/all_gather | solution.py:844
  13.2 194.7 %all-gather.3.cloned.1.call-start = ((), (), s32[]{:S(2)}) async-start(), calls=%async_computation.2 | async-start | bytes 4866048 | tf_op jit(solution)/shard_map/all_gather | solution.py:920
  25.7 7.9 %collective-permute-start.2 = (bf16[48,768]{1,0:T(8,128)(2,1)S(1)}, bf16[48,768]{1,0:T(8,128)(2,1)S(1)}, u32[]{:S(2)}, u32[]{:S(2)}) collective-permute-start(bf16[48,768]{1,0:T(8,128)(2,1)S(1)} %maximum_select_fusion.1), channel_id=1, source_target_pairs={{0,4},{1,5},{2,6},{3,7},{4,0},{5,1},{6,2},{7,3},{8,12},{9,13},{10,... | collective-permute-start | bytes 221192 | tf_op jit(solution)/shard_map/ppermute | solution.py:773
  33.6 33.2 %collective-permute-start.7 = (bf16[3,128,1024]{2,1,0:T(8,128)(2,1)S(1)}, bf16[3,128,1024]{2,1,0:T(8,128)(2,1)S(1)}, u32[]{:S(2)}, u32[]{:S(2)}) collective-permute-start(bf16[3,128,1024]{2,1,0:T(8,128)(2,1)S(1)} %fusion.refs_6_.refs_11_), channel_id=1, source_target_pairs={{0,2},{1,3},{2,4},{3,5},{4,6},{5,7},{6,0},{7,1},{8,10},{9,11},{10,... | collective-permute-start | bytes 2359304 | tf_op jit(solution)/shard_map/ppermute | solution.py:767
  34.7 10.9 %collective-permute-start.12 = (bf16[4,48,768]{2,1,0:T(8,128)(2,1)S(1)}, bf16[4,48,768]{2,1,0:T(8,128)(2,1)S(1)}, u32[]{:S(2)}, u32[]{:S(2)}) collective-permute-start(bf16[4,48,768]{2,1,0:T(8,128)(2,1)S(1)} %pad_maximum_fusion.4.refs_3_), channel_id=1, source_target_pairs={{0,24},{8,16},{16,8},{24,0},{1,25},{9,17},{17,9},{25,1},{2,26},{10... | collective-permute-start | bytes 884744 | tf_op jit(solution)/shard_map/ppermute | solution.py:770
  37.4 12.3 %collective-permute-start.11 = (bf16[4,48,768]{2,1,0:T(8,128)(2,1)S(1)}, bf16[4,48,768]{2,1,0:T(8,128)(2,1)S(1)}, u32[]{:S(2)}, u32[]{:S(2)}) collective-permute-start(bf16[4,48,768]{2,1,0:T(8,128)(2,1)S(1)} %pad_maximum_fusion.4.refs_3_), channel_id=1, source_target_pairs={{0,16},{8,24},{16,0},{24,8},{1,17},{9,25},{17,1},{25,9},{2,18},{10... | collective-permute-start | bytes 884744 | tf_op jit(solution)/shard_map/ppermute | solution.py:770
  37.7 12.0 %collective-permute-start.10 = (bf16[4,48,768]{2,1,0:T(8,128)(2,1)S(1)}, bf16[4,48,768]{2,1,0:T(8,128)(2,1)S(1)}, u32[]{:S(2)}, u32[]{:S(2)}) collective-permute-start(bf16[4,48,768]{2,1,0:T(8,128)(2,1)S(1)} %pad_maximum_fusion.4.refs_3_), channel_id=1, source_target_pairs={{0,8},{8,0},{16,24},{24,16},{1,9},{9,1},{17,25},{25,17},{2,10},{10... | collective-permute-start | bytes 884744 | tf_op jit(solution)/shard_map/ppermute | solution.py:770
  59.9 23.8 %collective-permute-start.13 = (bf16[2,192,1024]{2,1,0:T(8,128)(2,1)}, bf16[2,192,1024]{2,1,0:T(8,128)(2,1)S(1)}, u32[]{:S(2)}, u32[]{:S(2)}) collective-permute-start(bf16[2,192,1024]{2,1,0:T(8,128)(2,1)} %get-tuple-element.220), channel_id=1, source_target_pairs={{0,8},{8,0},{16,24},{24,16},{1,9},{9,1},{17,25},{25,17},{2,10},{10... | collective-permute-start | bytes 2359304 | tf_op jit(solution)/shard_map/ppermute | solution.py:748
  61.3 22.5 %collective-permute-start.14 = (bf16[2,192,1024]{2,1,0:T(8,128)(2,1)}, bf16[2,192,1024]{2,1,0:T(8,128)(2,1)S(1)}, u32[]{:S(2)}, u32[]{:S(2)}) collective-permute-start(bf16[2,192,1024]{2,1,0:T(8,128)(2,1)} %get-tuple-element.221), channel_id=1, source_target_pairs={{0,16},{8,24},{16,0},{24,8},{1,17},{9,25},{17,1},{25,9},{2,18},{10... | collective-permute-start | bytes 2359304 | tf_op jit(solution)/shard_map/ppermute | solution.py:748
  62.3 41.4 %collective-permute-start.15 = (bf16[2,192,1024]{2,1,0:T(8,128)(2,1)}, bf16[2,192,1024]{2,1,0:T(8,128)(2,1)S(1)}, u32[]{:S(2)}, u32[]{:S(2)}) collective-permute-start(bf16[2,192,1024]{2,1,0:T(8,128)(2,1)} %get-tuple-element.222), channel_id=1, source_target_pairs={{0,24},{8,16},{16,8},{24,0},{1,25},{9,17},{17,9},{25,1},{2,26},{10... | collective-permute-start | bytes 2359304 | tf_op jit(solution)/shard_map/ppermute | solution.py:748
  63.5 40.3 %collective-permute-start.9 = (bf16[3,128,1024]{2,1,0:T(8,128)(2,1)S(1)}, bf16[3,128,1024]{2,1,0:T(8,128)(2,1)S(1)}, u32[]{:S(2)}, u32[]{:S(2)}) collective-permute-start(bf16[3,128,1024]{2,1,0:T(8,128)(2,1)S(1)} %fusion.refs_6_.refs_11_), channel_id=1, source_target_pairs={{0,6},{1,7},{2,0},{3,1},{4,2},{5,3},{6,4},{7,5},{8,14},{9,15},{10,... | collective-permute-start | bytes 2359304 | tf_op jit(solution)/shard_map/ppermute | solution.py:767
  66.8 46.1 %collective-permute-start.8 = (bf16[3,128,1024]{2,1,0:T(8,128)(2,1)S(1)}, bf16[3,128,1024]{2,1,0:T(8,128)(2,1)S(1)}, u32[]{:S(2)}, u32[]{:S(2)}) collective-permute-start(bf16[3,128,1024]{2,1,0:T(8,128)(2,1)S(1)} %collective-permute-done.7.refs_7_.refs_12_), channel_id=1, source_target_pairs={{0,2},{1,3},{2,4},{3,5},{4,6},{5,7},{6,0},{7,1},{8,10},{9,11},{10,... | collective-permute-start | bytes 2359304 | tf_op jit(solution)/shard_map/ppermute | solution.py:767
  83.8 30.2 %collective-permute-start.17 = (bf16[3,128,1024]{2,1,0:T(8,128)(2,1)S(1)}, bf16[3,128,1024]{2,1,0:T(8,128)(2,1)}, u32[]{:S(2)}, u32[]{:S(2)}) collective-permute-start(bf16[3,128,1024]{2,1,0:T(8,128)(2,1)S(1)} %collective-permute-done.7.refs_7_.refs_12_), channel_id=1, source_target_pairs={{0,1},{1,0},{2,3},{3,2},{4,5},{5,4},{6,7},{7,6},{8,9},{9,8},{10,11... | collective-permute-start | bytes 2359304 | tf_op jit(solution)/shard_map/ppermute | solution.py:763
  103.8 10.2 %collective-permute-start.16 = (bf16[3,128,1024]{2,1,0:T(8,128)(2,1)S(1)}, bf16[3,128,1024]{2,1,0:T(8,128)(2,1)}, u32[]{:S(2)}, u32[]{:S(2)}) collective-permute-start(bf16[3,128,1024]{2,1,0:T(8,128)(2,1)S(1)} %fusion.refs_6_.refs_11_), channel_id=1, source_target_pairs={{0,1},{1,0},{2,3},{3,2},{4,5},{5,4},{6,7},{7,6},{8,9},{9,8},{10,11... | collective-permute-start | bytes 2359304 | tf_op jit(solution)/shard_map/ppermute | solution.py:763
  124.1 307.6 %reduce-scatter.5.cloned.1.call-start = ((), (), s32[]{:S(2)}) async-start(), calls=%async_computation.5 | async-start | bytes 4866048 | tf_op jit(solution)/shard_map/reduce_scatter | solution.py:930
  124.7 12.2 %collective-permute-start.20 = (bf16[192,1024]{1,0:T(8,128)(2,1)}, bf16[192,1024]{1,0:T(8,128)(2,1)S(1)}, u32[]{:S(2)}, u32[]{:S(2)}) collective-permute-start(bf16[192,1024]{1,0:T(8,128)(2,1)} %get-tuple-element.246.refs_7_), channel_id=1, source_target_pairs={{0,8},{8,0},{16,24},{24,16},{1,9},{9,1},{17,25},{25,17},{2,10},{10... | collective-permute-start | bytes 1179656 | tf_op jit(solution)/shard_map/ppermute | solution.py:748
  125.2 19.1 %collective-permute-start.21 = (bf16[192,1024]{1,0:T(8,128)(2,1)}, bf16[192,1024]{1,0:T(8,128)(2,1)S(1)}, u32[]{:S(2)}, u32[]{:S(2)}) collective-permute-start(bf16[192,1024]{1,0:T(8,128)(2,1)} %get-tuple-element.247.refs_8_), channel_id=1, source_target_pairs={{0,16},{8,24},{16,0},{24,8},{1,17},{9,25},{17,1},{25,9},{2,18},{10... | collective-permute-start | bytes 1179656 | tf_op jit(solution)/shard_map/ppermute | solution.py:748
  126.0 19.4 %collective-permute-start.22 = (bf16[192,1024]{1,0:T(8,128)(2,1)}, bf16[192,1024]{1,0:T(8,128)(2,1)S(1)}, u32[]{:S(2)}, u32[]{:S(2)}) collective-permute-start(bf16[192,1024]{1,0:T(8,128)(2,1)} %get-tuple-element.248.refs_9_), channel_id=1, source_target_pairs={{0,24},{8,16},{16,8},{24,0},{1,25},{9,17},{17,9},{25,1},{2,26},{10... | collective-permute-start | bytes 1179656 | tf_op jit(solution)/shard_map/ppermute | solution.py:748
  145.5 31.6 %collective-permute-start.23 = (bf16[192,1024]{1,0:T(8,128)(2,1)}, bf16[192,1024]{1,0:T(8,128)(2,1)S(1)}, u32[]{:S(2)}, u32[]{:S(2)}) collective-permute-start(bf16[192,1024]{1,0:T(8,128)(2,1)} %get-tuple-element.261.refs_7_), channel_id=1, source_target_pairs={{0,8},{8,0},{16,24},{24,16},{1,9},{9,1},{17,25},{25,17},{2,10},{10... | collective-permute-start | bytes 1179656 | tf_op jit(solution)/shard_map/ppermute | solution.py:748
  147.4 29.6 %collective-permute-start.24 = (bf16[192,1024]{1,0:T(8,128)(2,1)}, bf16[192,1024]{1,0:T(8,128)(2,1)S(1)}, u32[]{:S(2)}, u32[]{:S(2)}) collective-permute-start(bf16[192,1024]{1,0:T(8,128)(2,1)} %get-tuple-element.262.refs_8_), channel_id=1, source_target_pairs={{0,16},{8,24},{16,0},{24,8},{1,17},{9,25},{17,1},{25,9},{2,18},{10... | collective-permute-start | bytes 1179656 | tf_op jit(solution)/shard_map/ppermute | solution.py:748
  147.6 29.4 %collective-permute-start.25 = (bf16[192,1024]{1,0:T(8,128)(2,1)}, bf16[192,1024]{1,0:T(8,128)(2,1)S(1)}, u32[]{:S(2)}, u32[]{:S(2)}) collective-permute-start(bf16[192,1024]{1,0:T(8,128)(2,1)} %get-tuple-element.263.refs_9_), channel_id=1, source_target_pairs={{0,24},{8,16},{16,8},{24,0},{1,25},{9,17},{17,9},{25,1},{2,26},{10... | collective-permute-start | bytes 1179656 | tf_op jit(solution)/shard_map/ppermute | solution.py:748
  207.8 230.5 %reduce-scatter.3.cloned.1.call-start = ((), (), s32[]{:S(2)}) async-start(), calls=%async_computation.4 | async-start | bytes 7077888 | tf_op jit(solution)/shard_map/reduce_scatter | solution.py:955
  238.3 38.6 %collective-permute-start.26 = (bf16[192,1024]{1,0:T(8,128)(2,1)}, bf16[192,1024]{1,0:T(8,128)(2,1)S(1)}, u32[]{:S(2)}, u32[]{:S(2)}) collective-permute-start(bf16[192,1024]{1,0:T(8,128)(2,1)} %get-tuple-element.291), channel_id=1, source_target_pairs={{0,8},{8,0},{16,24},{24,16},{1,9},{9,1},{17,25},{25,17},{2,10},{10... | collective-permute-start | bytes 1179656 | tf_op jit(solution)/shard_map/ppermute | solution.py:748
  240.3 36.6 %collective-permute-start.27 = (bf16[192,1024]{1,0:T(8,128)(2,1)}, bf16[192,1024]{1,0:T(8,128)(2,1)S(1)}, u32[]{:S(2)}, u32[]{:S(2)}) collective-permute-start(bf16[192,1024]{1,0:T(8,128)(2,1)} %get-tuple-element.292), channel_id=1, source_target_pairs={{0,16},{8,24},{16,0},{24,8},{1,17},{9,25},{17,1},{25,9},{2,18},{10... | collective-permute-start | bytes 1179656 | tf_op jit(solution)/shard_map/ppermute | solution.py:748
  240.5 36.5 %collective-permute-start.28 = (bf16[192,1024]{1,0:T(8,128)(2,1)}, bf16[192,1024]{1,0:T(8,128)(2,1)S(1)}, u32[]{:S(2)}, u32[]{:S(2)}) collective-permute-start(bf16[192,1024]{1,0:T(8,128)(2,1)} %get-tuple-element.293), channel_id=1, source_target_pairs={{0,24},{8,16},{16,8},{24,0},{1,25},{9,17},{17,9},{25,1},{2,26},{10... | collective-permute-start | bytes 1179656 | tf_op jit(solution)/shard_map/ppermute | solution.py:748
  277.0 12.3 %collective-permute-start.29 = (bf16[192,1024]{1,0:T(8,128)(2,1)}, bf16[192,1024]{1,0:T(8,128)(2,1)S(1)}, u32[]{:S(2)}, u32[]{:S(2)}) collective-permute-start(bf16[192,1024]{1,0:T(8,128)(2,1)} %get-tuple-element.319), channel_id=1, source_target_pairs={{0,8},{8,0},{16,24},{24,16},{1,9},{9,1},{17,25},{25,17},{2,10},{10... | collective-permute-start | bytes 1179656 | tf_op jit(solution)/shard_map/ppermute | solution.py:748
  279.0 13.1 %collective-permute-start.30 = (bf16[192,1024]{1,0:T(8,128)(2,1)}, bf16[192,1024]{1,0:T(8,128)(2,1)S(1)}, u32[]{:S(2)}, u32[]{:S(2)}) collective-permute-start(bf16[192,1024]{1,0:T(8,128)(2,1)} %get-tuple-element.320), channel_id=1, source_target_pairs={{0,16},{8,24},{16,0},{24,8},{1,17},{9,25},{17,1},{25,9},{2,18},{10... | collective-permute-start | bytes 1179656 | tf_op jit(solution)/shard_map/ppermute | solution.py:748
  279.1 18.4 %collective-permute-start.31 = (bf16[192,1024]{1,0:T(8,128)(2,1)}, bf16[192,1024]{1,0:T(8,128)(2,1)S(1)}, u32[]{:S(2)}, u32[]{:S(2)}) collective-permute-start(bf16[192,1024]{1,0:T(8,128)(2,1)} %get-tuple-element.321), channel_id=1, source_target_pairs={{0,24},{8,16},{16,8},{24,0},{1,25},{9,17},{17,9},{25,1},{2,26},{10... | collective-permute-start | bytes 1179656 | tf_op jit(solution)/shard_map/ppermute | solution.py:748
  298.3 14.0 %collective-permute-start.32 = (bf16[16,48,1536]{2,1,0:T(8,128)(2,1)}, bf16[16,48,1536]{2,1,0:T(8,128)(2,1)S(1)}, u32[]{:S(2)}, u32[]{:S(2)}) collective-permute-start(bf16[16,48,1536]{2,1,0:T(8,128)(2,1)} %get-tuple-element.344), channel_id=1, source_target_pairs={{0,1},{1,0},{2,3},{3,2},{4,5},{5,4},{6,7},{7,6},{8,9},{9,8},{10,11... | collective-permute-start | bytes 7077896 | tf_op jit(solution)/shard_map/ppermute | solution.py:763
  298.3 12.3 %collective-permute-start.33 = (bf16[16,48,512]{2,1,0:T(8,128)(2,1)}, bf16[16,48,512]{2,1,0:T(8,128)(2,1)S(1)}, u32[]{:S(2)}, u32[]{:S(2)}) collective-permute-start(bf16[16,48,512]{2,1,0:T(8,128)(2,1)} %get-tuple-element.346), channel_id=1, source_target_pairs={{0,1},{1,0},{2,3},{3,2},{4,5},{5,4},{6,7},{7,6},{8,9},{9,8},{10,11... | collective-permute-start | bytes 2359304 | tf_op jit(solution)/shard_map/ppermute | solution.py:763
  298.8 26.4 %collective-permute-start.34 = (bf16[192,1024]{1,0:T(8,128)(2,1)}, bf16[192,1024]{1,0:T(8,128)(2,1)S(1)}, u32[]{:S(2)}, u32[]{:S(2)}) collective-permute-start(bf16[192,1024]{1,0:T(8,128)(2,1)} %get-tuple-element.355), channel_id=1, source_target_pairs={{0,8},{8,0},{16,24},{24,16},{1,9},{9,1},{17,25},{25,17},{2,10},{10... | collective-permute-start | bytes 1179656 | tf_op jit(solution)/shard_map/ppermute | solution.py:748
  299.3 25.9 %collective-permute-start.35 = (bf16[192,1024]{1,0:T(8,128)(2,1)}, bf16[192,1024]{1,0:T(8,128)(2,1)S(1)}, u32[]{:S(2)}, u32[]{:S(2)}) collective-permute-start(bf16[192,1024]{1,0:T(8,128)(2,1)} %get-tuple-element.356), channel_id=1, source_target_pairs={{0,16},{8,24},{16,0},{24,8},{1,17},{9,25},{17,1},{25,9},{2,18},{10... | collective-permute-start | bytes 1179656 | tf_op jit(solution)/shard_map/ppermute | solution.py:748
  300.5 24.7 %collective-permute-start.36 = (bf16[192,1024]{1,0:T(8,128)(2,1)}, bf16[192,1024]{1,0:T(8,128)(2,1)S(1)}, u32[]{:S(2)}, u32[]{:S(2)}) collective-permute-start(bf16[192,1024]{1,0:T(8,128)(2,1)} %get-tuple-element.357), channel_id=1, source_target_pairs={{0,24},{8,16},{16,8},{24,0},{1,25},{9,17},{17,9},{25,1},{2,26},{10... | collective-permute-start | bytes 1179656 | tf_op jit(solution)/shard_map/ppermute | solution.py:748
  326.2 12.7 %collective-permute-start.37 = (bf16[192,1024]{1,0:T(8,128)(2,1)}, bf16[192,1024]{1,0:T(8,128)(2,1)S(1)}, u32[]{:S(2)}, u32[]{:S(2)}) collective-permute-start(bf16[192,1024]{1,0:T(8,128)(2,1)} %get-tuple-element.369), channel_id=1, source_target_pairs={{0,8},{8,0},{16,24},{24,16},{1,9},{9,1},{17,25},{25,17},{2,10},{10... | collective-permute-start | bytes 1179656 | tf_op jit(solution)/shard_map/ppermute | solution.py:748
  326.8 18.5 %collective-permute-start.38 = (bf16[192,1024]{1,0:T(8,128)(2,1)}, bf16[192,1024]{1,0:T(8,128)(2,1)S(1)}, u32[]{:S(2)}, u32[]{:S(2)}) collective-permute-start(bf16[192,1024]{1,0:T(8,128)(2,1)} %get-tuple-element.370), channel_id=1, source_target_pairs={{0,16},{8,24},{16,0},{24,8},{1,17},{9,25},{17,1},{25,9},{2,18},{10... | collective-permute-start | bytes 1179656 | tf_op jit(solution)/shard_map/ppermute | solution.py:748
  327.9 17.4 %collective-permute-start.39 = (bf16[192,1024]{1,0:T(8,128)(2,1)S(1)}, bf16[192,1024]{1,0:T(8,128)(2,1)S(1)}, u32[]{:S(2)}, u32[]{:S(2)}) collective-permute-start(bf16[192,1024]{1,0:T(8,128)(2,1)S(1)} %copy-done.39), channel_id=1, source_target_pairs={{0,24},{8,16},{16,8},{24,0},{1,25},{9,17},{17,9},{25,1},{2,26},{10... | collective-permute-start | bytes 1179656 | tf_op jit(solution)/shard_map/ppermute | solution.py:748
  345.3 17.4 %collective-permute-start.40 = (bf16[4,48,2048]{2,1,0:T(8,128)(2,1)}, bf16[4,48,2048]{2,1,0:T(8,128)(2,1)S(1)}, u32[]{:S(2)}, u32[]{:S(2)}) collective-permute-start(bf16[4,48,2048]{2,1,0:T(8,128)(2,1)} %get-tuple-element.390), channel_id=1, source_target_pairs={{0,8},{8,0},{16,24},{24,16},{1,9},{9,1},{17,25},{25,17},{2,10},{10... | collective-permute-start | bytes 2359304 | tf_op jit(solution)/shard_map/ppermute | solution.py:770
  346.8 16.7 %collective-permute-start.41 = (bf16[4,48,2048]{2,1,0:T(8,128)(2,1)S(1)}, bf16[4,48,2048]{2,1,0:T(8,128)(2,1)S(1)}, u32[]{:S(2)}, u32[]{:S(2)}) collective-permute-start(bf16[4,48,2048]{2,1,0:T(8,128)(2,1)S(1)} %copy-done.16), channel_id=1, source_target_pairs={{0,16},{8,24},{16,0},{24,8},{1,17},{9,25},{17,1},{25,9},{2,18},{10... | collective-permute-start | bytes 2359304 | tf_op jit(solution)/shard_map/ppermute | solution.py:770
  363.6 21.0 %collective-permute-start.43 = (bf16[4,48,2048]{2,1,0:T(8,128)(2,1)S(1)}, bf16[4,48,2048]{2,1,0:T(8,128)(2,1)}, u32[]{:S(2)}, u32[]{:S(2)}) collective-permute-start(bf16[4,48,2048]{2,1,0:T(8,128)(2,1)S(1)} %get-tuple-element.397), channel_id=1, source_target_pairs={{0,24},{8,16},{16,8},{24,0},{1,25},{9,17},{17,9},{25,1},{2,26},{10... | collective-permute-start | bytes 2359304 | tf_op jit(solution)/shard_map/ppermute | solution.py:770
  384.5 17.6 %collective-permute-start.44 = (bf16[4,48,512]{2,1,0:T(8,128)(2,1)S(1)}, bf16[4,48,512]{2,1,0:T(8,128)(2,1)S(1)}, u32[]{:S(2)}, u32[]{:S(2)}) collective-permute-start(bf16[4,48,512]{2,1,0:T(8,128)(2,1)S(1)} %get-tuple-element.399), channel_id=1, source_target_pairs={{0,8},{8,0},{16,24},{24,16},{1,9},{9,1},{17,25},{25,17},{2,10},{10... | collective-permute-start | bytes 589832 | tf_op jit(solution)/shard_map/ppermute | solution.py:770
  385.2 17.6 %collective-permute-start.45 = (bf16[4,48,512]{2,1,0:T(8,128)(2,1)S(1)}, bf16[4,48,512]{2,1,0:T(8,128)(2,1)S(1)}, u32[]{:S(2)}, u32[]{:S(2)}) collective-permute-start(bf16[4,48,512]{2,1,0:T(8,128)(2,1)S(1)} %get-tuple-element.400), channel_id=1, source_target_pairs={{0,16},{8,24},{16,0},{24,8},{1,17},{9,25},{17,1},{25,9},{2,18},{10... | collective-permute-start | bytes 589832 | tf_op jit(solution)/shard_map/ppermute | solution.py:770
  386.9 15.9 %collective-permute-start.46 = (bf16[4,48,512]{2,1,0:T(8,128)(2,1)S(1)}, bf16[4,48,512]{2,1,0:T(8,128)(2,1)S(1)}, u32[]{:S(2)}, u32[]{:S(2)}) collective-permute-start(bf16[4,48,512]{2,1,0:T(8,128)(2,1)S(1)} %get-tuple-element.401), channel_id=1, source_target_pairs={{0,24},{8,16},{16,8},{24,0},{1,25},{9,17},{17,9},{25,1},{2,26},{10... | collective-permute-start | bytes 589832 | tf_op jit(solution)/shard_map/ppermute | solution.py:770
  389.5 22.8 %collective-permute-start.49 = (bf16[48,2048]{1,0:T(8,128)(2,1)S(1)}, bf16[48,2048]{1,0:T(8,128)(2,1)S(1)}, u32[]{:S(2)}, u32[]{:S(2)}) collective-permute-start(bf16[48,2048]{1,0:T(8,128)(2,1)S(1)} %get-tuple-element.423), channel_id=1, source_target_pairs={{0,6},{1,7},{2,4},{3,5},{4,2},{5,3},{6,0},{7,1},{8,14},{9,15},{10,... | collective-permute-start | bytes 589832 | tf_op jit(solution)/shard_map/ppermute | solution.py:773
  402.2 22.3 %collective-permute-start.48 = (bf16[48,2048]{1,0:T(8,128)(2,1)S(1)}, bf16[48,2048]{1,0:T(8,128)(2,1)S(1)}, u32[]{:S(2)}, u32[]{:S(2)}) collective-permute-start(bf16[48,2048]{1,0:T(8,128)(2,1)S(1)} %get-tuple-element.424), channel_id=1, source_target_pairs={{0,4},{1,5},{2,6},{3,7},{4,0},{5,1},{6,2},{7,3},{8,12},{9,13},{10,... | collective-permute-start | bytes 589832 | tf_op jit(solution)/shard_map/ppermute | solution.py:773
  402.2 22.3 %collective-permute-start.47 = (bf16[48,2048]{1,0:T(8,128)(2,1)S(1)}, bf16[48,2048]{1,0:T(8,128)(2,1)S(1)}, u32[]{:S(2)}, u32[]{:S(2)}) collective-permute-start(bf16[48,2048]{1,0:T(8,128)(2,1)S(1)} %get-tuple-element.425), channel_id=1, source_target_pairs={{0,2},{1,3},{2,0},{3,1},{4,6},{5,7},{6,4},{7,5},{8,10},{9,11},{10,... | collective-permute-start | bytes 589832 | tf_op jit(solution)/shard_map/ppermute | solution.py:773
  425.7 15.2 %collective-permute-start.50 = (bf16[48,512]{1,0:T(8,128)(2,1)S(1)}, bf16[48,512]{1,0:T(8,128)(2,1)S(1)}, u32[]{:S(2)}, u32[]{:S(2)}) collective-permute-start(bf16[48,512]{1,0:T(8,128)(2,1)S(1)} %get-tuple-element.406), channel_id=1, source_target_pairs={{0,2},{1,3},{2,0},{3,1},{4,6},{5,7},{6,4},{7,5},{8,10},{9,11},{10,... | collective-permute-start | bytes 147464 | tf_op jit(solution)/shard_map/ppermute | solution.py:773
  425.8 15.1 %collective-permute-start.51 = (bf16[48,512]{1,0:T(8,128)(2,1)S(1)}, bf16[48,512]{1,0:T(8,128)(2,1)S(1)}, u32[]{:S(2)}, u32[]{:S(2)}) collective-permute-start(bf16[48,512]{1,0:T(8,128)(2,1)S(1)} %get-tuple-element.407), channel_id=1, source_target_pairs={{0,4},{1,5},{2,6},{3,7},{4,0},{5,1},{6,2},{7,3},{8,12},{9,13},{10,... | collective-permute-start | bytes 147464 | tf_op jit(solution)/shard_map/ppermute | solution.py:773
  427.4 13.5 %collective-permute-start.52 = (bf16[48,512]{1,0:T(8,128)(2,1)S(1)}, bf16[48,512]{1,0:T(8,128)(2,1)S(1)}, u32[]{:S(2)}, u32[]{:S(2)}) collective-permute-start(bf16[48,512]{1,0:T(8,128)(2,1)S(1)} %get-tuple-element.408), channel_id=1, source_target_pairs={{0,6},{1,7},{2,4},{3,5},{4,2},{5,3},{6,0},{7,1},{8,14},{9,15},{10,... | collective-permute-start | bytes 147464 | tf_op jit(solution)/shard_map/ppermute | solution.py:773
  (53 other events, 416.8 us)
Sparse Core Ops, SparseCore 0:
  13.3 110.2 all-gather.4
  126.6 78.2 all-gather.2
  210.4 128.1 reduce-scatter.4
  340.9 73.5 reduce-scatter.2

commit v4 on v3

--- a/solution.py
+++ b/solution.py
@@ -791,8 +791,10 @@
         return jnp.stack([c * rows for c in self.chips()]).astype(jnp.int32)
 
     def scatter_core(self, shares):
-        keeps, (send,) = shares
-        got, n = self.across(send), self.rings
+        return self.join_core(shares[0], self.across(shares[1][0]))
+
+    def join_core(self, keeps, got):
+        n = self.rings
         return [add(keep, got[b * n : (b + 1) * n]) for b, keep in enumerate(keeps)]
 
     def scatter_plane(self, parts):
@@ -827,6 +829,14 @@
     first_gain = gain_one.astype(f32)[:, None]
     second_gain = gain_two.astype(f32)[:, None]
     value_mine = (w_value.astype(f32) * first_gain).astype(bf16)
+    if fast:
+        other = chips.across(value_mine)
+        value_unit = jnp.where(
+            core == 0, jnp.concatenate([value_mine, other]), jnp.concatenate([other, value_mine])
+        )
+        value_unit, lengths_here, w_up, w_down, w_out, mixer = hold(
+            value_unit, jnp.stack(exchange([lengths] * groups), axis=1).reshape(-1), w_up, w_down, w_out, mixer
+        )
     up_mine = (w_up.astype(f32) * second_gain).astype(bf16)
     up_mine = up_mine.reshape(shard, ranks, slices, shard).swapaxes(1, 2)
     down_mine = w_down.reshape(slices, shard, WIDTH).swapaxes(0, 1)
@@ -846,10 +856,6 @@
     if fast:
         rings = chips.rings
         whole = [None] + whole
-        other = chips.across(value_mine)
-        value_unit = jnp.where(
-            core == 0, jnp.concatenate([value_mine, other]), jnp.concatenate([other, value_mine])
-        )
         weights_at[0] = chips.gathered_at(2 * shard)
         zs = [(chips.z - s) % rings for s in (0, 1, 3, 2)]
         logits_at = [(2 * z + c) * block for c in (core, 1 - core) for z in zs]
@@ -903,9 +909,7 @@
     if fast:
         assert items == 2 and CHUNKS == 2
         value_ring = chips.gather_line(value_unit)
-        value_ring, logits_low, second, lengths_here = hold(
-            value_ring, logits_low, weights[2], lengths_of()
-        )
+        value_ring, logits_low, second = hold(value_ring, logits_low, weights[2])
         value_parts = chips.gather_plane(value_ring)
         next_one, last_one = chips.along(logits_low, 1), chips.along(logits_low, 3)
         values, value_all = values_of()
@@ -941,20 +945,25 @@
         result = out_b[0]
         grads_b = exchange(out_b[2:])
         back_a, left_a = back(0, grads_a, mixed_out_a, sums_a)
-        back_a, left_a, grads_b, second_shared, out_shared = hold(
-            back_a, left_a, grads_b, second_shared, out_shared
-        )
+        back_a, left_a, second_shared, out_shared = hold(back_a, left_a, second_shared, out_shared)
         back_a = exchange(back_a)
         back_b, left_b = back(1, grads_b, mixed_out_b, sums_b)
-        second_sums, out_sums = chips.scatter_core(second_shared), chips.scatter_core(out_shared)
-        second_sums = [jnp.concatenate(pair, axis=2) for pair in zip(second_sums, out_sums)]
-        back_b, left_b, second_sums = hold(back_b, left_b, second_sums)
+        back_b, left_b, second_shared, out_shared = hold(back_b, left_b, second_shared, out_shared)
         back_b = exchange(back_b)
         grad_logits = logits_back(lengths_here, shares_at, [left_a, left_b], values, shares)
-        grad_logits, back_a, second_sums = hold(grad_logits, back_a, second_sums)
+        grad_logits, back_a, second_shared, out_shared = hold(
+            grad_logits, back_a, second_shared, out_shared
+        )
         grad_mixer = lax.psum_scatter(grad_logits[0][0], "seq", scatter_dimension=1, tiled=True)
+        second_got, out_got = chips.across(second_shared[1][0]), chips.across(out_shared[1][0])
         grad_tokens, carry = close(0, out_a[1], back_a, (), None)
-        carry, back_b, grad_tokens, second_sums = hold(carry, back_b, grad_tokens, second_sums)
+        carry, back_b, grad_tokens, second_got, out_got = hold(
+            carry, back_b, grad_tokens, second_got, out_got
+        )
+        second_sums = [
+            jnp.concatenate(pair, axis=2)
+            for pair in zip(chips.join_core(second_shared[0], second_got), chips.join_core(out_shared[0], out_got))
+        ]
         second_plane = [chips.over(second_sums[b], b) for b in range(1, groups)]
         grad_tokens, shared = close(1, out_b[1], back_b, carry, grad_tokens)
         shared, second_plane[:2] = hold(shared, second_plane[:2])

time: 457 us -> 451 us (0.987)
  waiting for transfers between devices: 140 us -> 135 us
    ppermute x9, waiting for transfers between devices: 28.6 us -> 20.9 us  [hop(): lax.ppermute(array, 'seq', [(i, i ^ 2 * step) for i in range(self.seqs)])]
  transfers between devices with their start and end apart: 59 -> 59, of which waited for: 25 -> 26; matrix products, arithmetic and copies ran while one was open for 6% -> 6% of each run, Pallas kernels for 42% -> 43%
where the time goes in v4:
time: 451 us; the launch traced here: 444 us
  Pallas kernels  191 us (42%)
  waiting for transfers between devices  135 us (30%)
  starting transfers between devices  65.6 us (15%)
  other arithmetic  19.2 us (4%)
  local copies, waits for them, and re-layouts  18.8 us (4%)
  between operations  14.8 us (3%)
    pallas_call x12, Pallas kernels, call(): pl.pallas_call(run, grid_spec=pltpu.PrefetchScalarGridSpec(num_scalar_pre...  191 us
    ppermute x24, waiting for transfers between devices, exchange(): lax.ppermute(parts[r], 'dp', [(i, i ^ r) for i in range(len(parts))])  63.7 us
    ppermute x9, waiting for transfers between devices, over(): lax.ppermute(array, 'dp', [(i, i ^ bits) for i in range(self.groups)])  35.6 us
    ppermute x24, starting transfers between devices, exchange(): lax.ppermute(parts[r], 'dp', [(i, i ^ r) for i in range(len(parts))])  29.3 us
    ppermute x9, waiting for transfers between devices, hop(): lax.ppermute(array, 'seq', [(i, i ^ 2 * step) for i in range(self.seqs)])  20.9 us
    ppermute x9, starting transfers between devices, hop(): lax.ppermute(array, 'seq', [(i, i ^ 2 * step) for i in range(self.seqs)])  19.6 us
    ppermute x3, waiting for transfers between devices, along(): lax.ppermute(array, 'seq', [(i, (i + 2 * step) % n) for i in range(n)])  11 us
    ppermute x9, starting transfers between devices, over(): lax.ppermute(array, 'dp', [(i, i ^ bits) for i in range(self.groups)])  10.7 us
  transfers between devices with their start and end apart: 59, of which 26 were waited for; matrix products, arithmetic and copies ran while one was open for 6% of the time, Pallas kernels for 43%

profile of v4, /device:TPU:0, one launch (start us, length us, event | category | flops | bytes accessed | tf_op | source)
XLA Modules:
  0.0 444.1 jit_solution(2270877962909704104)
XLA Ops:
  7.2 3.0 collective-permute-start.1
  10.2 1.5 collective-permute-start.3
  22.1 3.7 collective-permute-start.6
  29.2 2.5 collective-permute-done.5
  32.8 2.4 collective-permute-start.12
  37.5 6.2 %collective-permute-done.12.refs_6_ = bf16[4,48,768]{2,1,0:T(8,128)(2,1)S(1)} collective-permute-done((bf16[4,48,768]{2,1,0:T(8,128)(2,1)S(1)}, bf16[4,48,768]{2,1,0:T(8,128)(2,1)S(1)}, u32[]{:S(2)}, u32[]{:S(2)}) %collective-permute-start.12) | collective-permute-done | bytes 294944 | tf_op jit(solution)/shard_map/ppermute | solution.py:770
  43.7 5.2 %collective-permute-done.11.refs_5_ = bf16[4,48,768]{2,1,0:T(8,128)(2,1)S(1)} collective-permute-done((bf16[4,48,768]{2,1,0:T(8,128)(2,1)S(1)}, bf16[4,48,768]{2,1,0:T(8,128)(2,1)S(1)}, u32[]{:S(2)}, u32[]{:S(2)}) %collective-permute-start.11) | collective-permute-done | bytes 294944 | tf_op jit(solution)/shard_map/ppermute | solution.py:770
  50.3 8.8 %project_values.1 = (bf16[2,192,1024]{2,1,0:T(8,128)(2,1)}, bf16[2,192,1024]{2,1,0:T(8,128)(2,1)}, bf16[2,192,1024]{2,1,0:T(8,128)(2,1)}, bf16[2,192,1024]{2,1,0:T(8,128)(2,1)}, bf16[768,768]{1,0:T(8,128)(2,1)}) custom-call(s32[3]{0:T(128)} %pad_add_fusion.1.refs_0_, s32[32]{0:T(128)} %stack.179.refs_1_, bf16[2,1024,768]{2,1,0:T(8,128)(2,1)} %refs_2_.13, ...), custom_call_target="tpu_custom_call" | custom-call | flops 2415919 | bytes 6291 | tf_op jit(solution)/shard_map/project_values/pallas_call | solution.py:76
  60.8 1.9 collective-permute-start.15
  62.7 3.1 collective-permute-start.9
  65.8 19.2 %collective-permute-done.13.refs_3_.refs_5_ = bf16[2,192,1024]{2,1,0:T(8,128)(2,1)S(1)} collective-permute-done((bf16[2,192,1024]{2,1,0:T(8,128)(2,1)}, bf16[2,192,1024]{2,1,0:T(8,128)(2,1)S(1)}, u32[]{:S(2)}, u32[]{:S(2)}) %collective-permute-start.13) | collective-permute-done | bytes 786464 | tf_op jit(solution)/shard_map/ppermute | solution.py:748
  85.1 16.5 %collective-permute-done.15.refs_5_.refs_7_ = bf16[2,192,1024]{2,1,0:T(8,128)(2,1)S(1)} collective-permute-done((bf16[2,192,1024]{2,1,0:T(8,128)(2,1)}, bf16[2,192,1024]{2,1,0:T(8,128)(2,1)S(1)}, u32[]{:S(2)}, u32[]{:S(2)}) %collective-permute-start.15) | collective-permute-done | bytes 786464 | tf_op jit(solution)/shard_map/ppermute | solution.py:748
  101.6 11.0 %collective-permute-done.8.refs_9_.refs_14_ = bf16[3,128,1024]{2,1,0:T(8,128)(2,1)S(1)} collective-permute-done((bf16[3,128,1024]{2,1,0:T(8,128)(2,1)S(1)}, bf16[3,128,1024]{2,1,0:T(8,128)(2,1)S(1)}, u32[]{:S(2)}, u32[]{:S(2)}) %collective-permute-start.8) | collective-permute-done | bytes 786464 | tf_op jit(solution)/shard_map/ppermute | solution.py:767
  116.3 7.4 %mix_items.2 = (bf16[192,1024]{1,0:T(8,128)(2,1)}, bf16[192,1024]{1,0:T(8,128)(2,1)}, bf16[192,1024]{1,0:T(8,128)(2,1)}, bf16[192,1024]{1,0:T(8,128)(2,1)}, f32[3,8,1024]{2,1,0:T(8,128)}) custom-call(s32[8]{0:T(128)} %reshape.125.refs_0_, s32[8]{0:T(128)} %stack.173.refs_1_, bf16[2,192,1024]{2,1,0:T(8,128)(2,1)} %get-tuple-element.242.refs_2_.refs_4_, ...), custom_call_target="tpu_custom_call" | custom-call | flops 1711276 | bytes 12582 | tf_op jit(solution)/shard_map/mix_items/pallas_call | solution.py:76
  125.9 2.0 collective-permute-start.22
  127.9 7.4 %mix_items.3 = (bf16[192,1024]{1,0:T(8,128)(2,1)}, bf16[192,1024]{1,0:T(8,128)(2,1)}, bf16[192,1024]{1,0:T(8,128)(2,1)}, bf16[192,1024]{1,0:T(8,128)(2,1)}, f32[3,8,1024]{2,1,0:T(8,128)}) custom-call(s32[8]{0:T(128)} %reshape.125.refs_0_, s32[8]{0:T(128)} %stack.173.refs_1_, bf16[2,192,1024]{2,1,0:T(8,128)(2,1)} %get-tuple-element.242.refs_2_.refs_4_, ...), custom_call_target="tpu_custom_call" | custom-call | flops 1711276 | bytes 12582 | tf_op jit(solution)/shard_map/mix_items/pallas_call | solution.py:76
  136.6 4.6 %collective-permute-done.21.refs_6_ = bf16[192,1024]{1,0:T(8,128)(2,1)S(1)} collective-permute-done((bf16[192,1024]{1,0:T(8,128)(2,1)}, bf16[192,1024]{1,0:T(8,128)(2,1)S(1)}, u32[]{:S(2)}, u32[]{:S(2)}) %collective-permute-start.21) | collective-permute-done | bytes 393248 | tf_op jit(solution)/shard_map/ppermute | solution.py:748
  141.2 4.9 %collective-permute-done.22.refs_7_ = bf16[192,1024]{1,0:T(8,128)(2,1)S(1)} collective-permute-done((bf16[192,1024]{1,0:T(8,128)(2,1)}, bf16[192,1024]{1,0:T(8,128)(2,1)S(1)}, u32[]{:S(2)}, u32[]{:S(2)}) %collective-permute-start.22) | collective-permute-done | bytes 393248 | tf_op jit(solution)/shard_map/ppermute | solution.py:748
  150.2 27.4 %feed.4 = (f32[1024,768]{1,0:T(8,128)}, bf16[1024,768]{1,0:T(8,128)(2,1)}, bf16[768,768]{1,0:T(8,128)(2,1)}, f32[768,1024]{1,0:T(8,128)}, f32[768,1024]{1,0:T(8,...) custom-call(s32[3]{0:T(128)} %pad_add_fusion.1.refs_0_, s32[16]{0:T(128)} %stack.159.refs_1_, ...), custom_call_target="tpu_custom_call" | custom-call | flops 14495514 | bytes 20971 | tf_op jit(solution)/shard_map/feed/pallas_call | solution.py:76
  178.6 30.0 %feed.5 = (f32[1024,768]{1,0:T(8,128)}, bf16[1024,768]{1,0:T(8,128)(2,1)}, bf16[768,768]{1,0:T(8,128)(2,1)}, f32[768,1024]{1,0:T(8,128)}, f32[768,1024]{1,0:T(8,128)}, /*index=5*/bf16[768,3072]{1,0:T(8,128)(2,1)}) custom-call(s32[3]{0:T(128)} %pad_add_fusion.1.refs_0_, s32[16]{0:T(128)} %stack.159.refs_1_, bf16[2,1024,768]{2,1,0:T(8,128)(2,1)} %refs_2_.11, ...), custom_call_target="tpu_custom_call" | custom-call | flops 14495514 | bytes 20971 | tf_op jit(solution)/shard_map/feed/pallas_call | solution.py:76
  208.7 30.4 %feed.6 = (bf16[2,1024,768]{2,1,0:T(8,128)(2,1)}, bf16[1024,768]{1,0:T(8,128)(2,1)}, bf16[192,1024]{1,0:T(8,128)(2,1)}, bf16[192,1024]{1,0:T(8,128)(2,1)}, bf16[...) custom-call(s32[3]{0:T(128)} %pad_add_fusion.1.refs_0_, ...), custom_call_target="tpu_custom_call" | custom-call | flops 14495514 | bytes 20971 | tf_op jit(solution)/shard_map/feed/pallas_call | solution.py:76
  240.9 1.8 collective-permute-start.28
  242.7 35.0 %feed.7 = (bf16[2,1024,768]{2,1,0:T(8,128)(2,1)}, bf16[1024,768]{1,0:T(8,128)(2,1)}, bf16[192,1024]{1,0:T(8,128)(2,1)}, bf16[192,1024]{1,0:T(8,128)(2,1)}, bf16[...) custom-call(s32[3]{0:T(128)} %pad_add_fusion.1.refs_0_, ...), custom_call_target="tpu_custom_call", output_to_operand_aliasing={{0}: (17, {})} | custom-call | flops 14495514 | bytes 20971 | tf_op jit(solution)/shard_map/feed/pallas_call | solution.py:76
  279.6 1.8 collective-permute-start.31
  281.3 7.9 %values_back.2 = (bf16[192,1024]{1,0:T(8,128)(2,1)}, bf16[192,1024]{1,0:T(8,128)(2,1)}, bf16[192,1024]{1,0:T(8,128)(2,1)}, bf16[192,1024]{1,0:T(8,128)(2,1)}, bf16[3,272,1024]{2,1,0:T(8,128)(2,1)}) custom-call(s32[8]{0:T(128)} %reshape.125.refs_0_, s32[8]{0:T(128)} %stack.173.refs_1_, bf16[192,1024]{1,0:T(8,128)(2,1)} %get-tuple-element.324.refs_2_, ...), custom_call_target="tpu_custom_call" | custom-call | flops 1711276 | bytes 14680 | tf_op jit(solution)/shard_map/values_back/pallas_call | solution.py:76
  291.0 1.8 collective-permute-start.34
  292.8 2.3 collective-permute-done.30.refs_4_
  295.0 5.4 %collective-permute-done.31.refs_5_ = bf16[192,1024]{1,0:T(8,128)(2,1)S(1)} collective-permute-done((bf16[192,1024]{1,0:T(8,128)(2,1)}, bf16[192,1024]{1,0:T(8,128)(2,1)S(1)}, u32[]{:S(2)}, u32[]{:S(2)}) %collective-permute-start.31) | collective-permute-done | bytes 393248 | tf_op jit(solution)/shard_map/ppermute | solution.py:748
  301.2 7.8 %values_back.3 = (bf16[192,1024]{1,0:T(8,128)(2,1)}, bf16[192,1024]{1,0:T(8,128)(2,1)}, bf16[192,1024]{1,0:T(8,128)(2,1)}, bf16[192,1024]{1,0:T(8,128)(2,1)}, bf16[3,272,1024]{2,1,0:T(8,128)(2,1)}) custom-call(s32[8]{0:T(128)} %reshape.125.refs_0_, s32[8]{0:T(128)} %stack.173.refs_1_, bf16[192,1024]{1,0:T(8,128)(2,1)} %get-tuple-element.345.refs_2_, ...), custom_call_target="tpu_custom_call" | custom-call | flops 1711276 | bytes 14680 | tf_op jit(solution)/shard_map/values_back/pallas_call | solution.py:76
  309.0 10.3 %logits_back.1 = bf16[1,3,1024,1024]{3,2,1,0:T(8,128)(2,1)} custom-call(s32[8]{0:T(128)} %reshape.125.refs_0_, s32[1]{0:T(128)} %constant.68.clone.1.refs_1_, bf16[3,272,1024]{2,1,0:T(8,128)(2,1)} %get-tuple-element.344.refs_2_, bf16[3,272,1024]{2,1,0:T(8,128)(2,1)} %get-tuple-element.365.refs_3_, bf16[2,192,1024]{2,1,0:T(8,128)(2,1)} %get-tuple-element.242.refs_2_.refs_4_, ...), custom_call_target="tpu_custom_call" | custom-call | flops 3422552 | bytes 14680 | tf_op jit(solution)/shard_map/logits_back/pallas_call | solution.py:76
  324.3 9.2 %grad_tokens.2 = (bf16[2,1024,768]{2,1,0:T(8,128)(2,1)}, f32[768,768]{1,0:T(8,128)}, f32[1,768]{1,0:T(1,128)}) custom-call(s32[3]{0:T(128)} %pad_add_fusion.1.refs_0_, s32[16]{0:T(128)} %stack.159.refs_1_, bf16[2,1024,768]{2,1,0:T(8,128)(2,1)} %refs_2_.13, bf16[1024,768]{1,0:T(8,128)(2,1)} %get-tuple-element.323.refs_3_, ...), custom_call_target="tpu_custom_call" | custom-call | flops 2415919 | bytes 8388 | tf_op jit(solution)/shard_map/grad_tokens/pallas_call | solution.py:76
  333.6 6.6 %collective-permute-done.36.refs_7_ = bf16[192,1024]{1,0:T(8,128)(2,1)S(1)} collective-permute-done((bf16[192,1024]{1,0:T(8,128)(2,1)}, bf16[192,1024]{1,0:T(8,128)(2,1)S(1)}, u32[]{:S(2)}, u32[]{:S(2)}) %collective-permute-start.36) | collective-permute-done | bytes 393248 | tf_op jit(solution)/shard_map/ppermute | solution.py:748
  342.6 1.5 add_convert_fusion.8
  345.8 1.9 collective-permute-start.41
  347.6 9.2 %grad_tokens.3 = (bf16[2,1024,768]{2,1,0:T(8,128)(2,1)}, bf16[4,48,512]{2,1,0:T(8,128)(2,1)}, bf16[4,48,512]{2,1,0:T(8,128)(2,1)}, bf16[4,48,512]{2,1,0:T(8,128)...) custom-call(s32[3]{0:T(128)} %pad_add_fusion.1.refs_0_, ...), custom_call_target="tpu_custom_call", output_to_operand_aliasing={{0}: (11, {})} | custom-call | flops 2415919 | bytes 8388 | tf_op jit(solution)/shard_map/grad_tokens/pallas_call | solution.py:76
  356.8 6.8 %collective-permute-done.40 = bf16[4,48,2048]{2,1,0:T(8,128)(2,1)S(1)} collective-permute-done((bf16[4,48,2048]{2,1,0:T(8,128)(2,1)S(1)}, bf16[4,48,2048]{2,1,0:T(8,128)(2,1)S(1)}, u32[]{:S(2)}, u32[]{:S(2)}) %collective-permute-start.40) | collective-permute-done | bytes 786464 | tf_op jit(solution)/shard_map/ppermute | solution.py:770
  366.8 1.6 add_convert_fusion.10
  368.4 16.9 %collective-permute-done.43 = bf16[4,48,2048]{2,1,0:T(8,128)(2,1)} collective-permute-done((bf16[4,48,2048]{2,1,0:T(8,128)(2,1)S(1)}, bf16[4,48,2048]{2,1,0:T(8,128)(2,1)}, u32[]{:S(2)}, u32[]{:S(2)}) %collective-permute-start.43) | collective-permute-done | bytes 786464 | tf_op jit(solution)/shard_map/ppermute | solution.py:770
  387.0 1.7 collective-permute-start.46
  388.8 1.5 fusion.6
  390.2 10.0 %collective-permute-start.49 = (bf16[48,2048]{1,0:T(8,128)(2,1)S(1)}, bf16[48,2048]{1,0:T(8,128)(2,1)S(1)}, u32[]{:S(2)}, u32[]{:S(2)}) collective-permute-start(bf16[48,2048]{1,0:T(8,128)(2,1)S(1)} %get-tuple-element.445), channel_id=1, source_target_pairs={{0,6},{1,7},{2,4},{3,5},{4,2},{5,3},{6,0},{7,1},{8,14},{9,15},{10,... | collective-permute-start | bytes 589832 | tf_op jit(solution)/shard_map/ppermute | solution.py:773
  401.0 6.0 %collective-permute-done.49 = bf16[48,2048]{1,0:T(8,128)(2,1)S(1)} collective-permute-done((bf16[48,2048]{1,0:T(8,128)(2,1)S(1)}, bf16[48,2048]{1,0:T(8,128)(2,1)S(1)}, u32[]{:S(2)}, u32[]{:S(2)}) %collective-permute-start.49) | collective-permute-done | bytes 196640 | tf_op jit(solution)/shard_map/ppermute | solution.py:773
  407.0 2.5 collective-permute-done.47
  409.5 8.8 %collective-permute-done.48 = bf16[48,2048]{1,0:T(8,128)(2,1)S(1)} collective-permute-done((bf16[48,2048]{1,0:T(8,128)(2,1)S(1)}, bf16[48,2048]{1,0:T(8,128)(2,1)S(1)}, u32[]{:S(2)}, u32[]{:S(2)}) %collective-permute-start.48) | collective-permute-done | bytes 196640 | tf_op jit(solution)/shard_map/ppermute | solution.py:773
  419.6 1.6 collective-permute-start.51
  421.1 2.8 collective-permute-start.52
  429.4 1.8 reshape.138
  432.1 2.6 convert_multiply_fusion
  (243 shorter events, 63.4 us)
Async XLA Ops:
  7.2 143.0 %all-gather.5.cloned.1.call-start = ((), (), s32[]{:S(2)}) async-start(), calls=%async_computation.3 | async-start | bytes 6082560 | tf_op jit(solution)/shard_map/all_gather | solution.py:854
  22.1 186.6 %all-gather.3.cloned.1.call-start = ((), (), s32[]{:S(2)}) async-start(), calls=%async_computation.2 | async-start | bytes 4866048 | tf_op jit(solution)/shard_map/all_gather | solution.py:924
  22.1 7.1 %collective-permute-start.6 = (bf16[48,768]{1,0:T(8,128)(2,1)S(1)}, bf16[48,768]{1,0:T(8,128)(2,1)S(1)}, u32[]{:S(2)}, u32[]{:S(2)}) collective-permute-start(bf16[48,768]{1,0:T(8,128)(2,1)S(1)} %maximum_select_fusion), channel_id=1, source_target_pairs={{0,6},{1,7},{2,4},{3,5},{4,2},{5,3},{6,0},{7,1},{8,14},{9,15},{10,... | collective-permute-start | bytes 221192 | tf_op jit(solution)/shard_map/ppermute | solution.py:773
  31.8 34.0 %collective-permute-start.7 = (bf16[3,128,1024]{2,1,0:T(8,128)(2,1)S(1)}, bf16[3,128,1024]{2,1,0:T(8,128)(2,1)S(1)}, u32[]{:S(2)}, u32[]{:S(2)}) collective-permute-start(bf16[3,128,1024]{2,1,0:T(8,128)(2,1)S(1)} %fusion.refs_6_.refs_11_), channel_id=1, source_target_pairs={{0,2},{1,3},{2,4},{3,5},{4,6},{5,7},{6,0},{7,1},{8,10},{9,11},{10,... | collective-permute-start | bytes 2359304 | tf_op jit(solution)/shard_map/ppermute | solution.py:767
  32.8 10.9 %collective-permute-start.12 = (bf16[4,48,768]{2,1,0:T(8,128)(2,1)S(1)}, bf16[4,48,768]{2,1,0:T(8,128)(2,1)S(1)}, u32[]{:S(2)}, u32[]{:S(2)}) collective-permute-start(bf16[4,48,768]{2,1,0:T(8,128)(2,1)S(1)} %pad_maximum_fusion.3.refs_3_), channel_id=1, source_target_pairs={{0,24},{8,16},{16,8},{24,0},{1,25},{9,17},{17,9},{25,1},{2,26},{10... | collective-permute-start | bytes 884744 | tf_op jit(solution)/shard_map/ppermute | solution.py:770
  35.3 13.6 %collective-permute-start.11 = (bf16[4,48,768]{2,1,0:T(8,128)(2,1)S(1)}, bf16[4,48,768]{2,1,0:T(8,128)(2,1)S(1)}, u32[]{:S(2)}, u32[]{:S(2)}) collective-permute-start(bf16[4,48,768]{2,1,0:T(8,128)(2,1)S(1)} %pad_maximum_fusion.3.refs_3_), channel_id=1, source_target_pairs={{0,16},{8,24},{16,0},{24,8},{1,17},{9,25},{17,1},{25,9},{2,18},{10... | collective-permute-start | bytes 884744 | tf_op jit(solution)/shard_map/ppermute | solution.py:770
  35.8 13.1 %collective-permute-start.10 = (bf16[4,48,768]{2,1,0:T(8,128)(2,1)S(1)}, bf16[4,48,768]{2,1,0:T(8,128)(2,1)S(1)}, u32[]{:S(2)}, u32[]{:S(2)}) collective-permute-start(bf16[4,48,768]{2,1,0:T(8,128)(2,1)S(1)} %pad_maximum_fusion.3.refs_3_), channel_id=1, source_target_pairs={{0,8},{8,0},{16,24},{24,16},{1,9},{9,1},{17,25},{25,17},{2,10},{10... | collective-permute-start | bytes 884744 | tf_op jit(solution)/shard_map/ppermute | solution.py:770
  59.1 25.9 %collective-permute-start.13 = (bf16[2,192,1024]{2,1,0:T(8,128)(2,1)}, bf16[2,192,1024]{2,1,0:T(8,128)(2,1)S(1)}, u32[]{:S(2)}, u32[]{:S(2)}) collective-permute-start(bf16[2,192,1024]{2,1,0:T(8,128)(2,1)} %get-tuple-element.235), channel_id=1, source_target_pairs={{0,8},{8,0},{16,24},{24,16},{1,9},{9,1},{17,25},{25,17},{2,10},{10... | collective-permute-start | bytes 2359304 | tf_op jit(solution)/shard_map/ppermute | solution.py:748
  59.8 25.3 %collective-permute-start.14 = (bf16[2,192,1024]{2,1,0:T(8,128)(2,1)}, bf16[2,192,1024]{2,1,0:T(8,128)(2,1)S(1)}, u32[]{:S(2)}, u32[]{:S(2)}) collective-permute-start(bf16[2,192,1024]{2,1,0:T(8,128)(2,1)} %get-tuple-element.236), channel_id=1, source_target_pairs={{0,16},{8,24},{16,0},{24,8},{1,17},{9,25},{17,1},{25,9},{2,18},{10... | collective-permute-start | bytes 2359304 | tf_op jit(solution)/shard_map/ppermute | solution.py:748
  60.8 40.8 %collective-permute-start.15 = (bf16[2,192,1024]{2,1,0:T(8,128)(2,1)}, bf16[2,192,1024]{2,1,0:T(8,128)(2,1)S(1)}, u32[]{:S(2)}, u32[]{:S(2)}) collective-permute-start(bf16[2,192,1024]{2,1,0:T(8,128)(2,1)} %get-tuple-element.237), channel_id=1, source_target_pairs={{0,24},{8,16},{16,8},{24,0},{1,25},{9,17},{17,9},{25,1},{2,26},{10... | collective-permute-start | bytes 2359304 | tf_op jit(solution)/shard_map/ppermute | solution.py:748
  62.7 39.0 %collective-permute-start.9 = (bf16[3,128,1024]{2,1,0:T(8,128)(2,1)S(1)}, bf16[3,128,1024]{2,1,0:T(8,128)(2,1)S(1)}, u32[]{:S(2)}, u32[]{:S(2)}) collective-permute-start(bf16[3,128,1024]{2,1,0:T(8,128)(2,1)S(1)} %fusion.refs_6_.refs_11_), channel_id=1, source_target_pairs={{0,6},{1,7},{2,0},{3,1},{4,2},{5,3},{6,4},{7,5},{8,14},{9,15},{10,... | collective-permute-start | bytes 2359304 | tf_op jit(solution)/shard_map/ppermute | solution.py:767
  65.8 46.8 %collective-permute-start.8 = (bf16[3,128,1024]{2,1,0:T(8,128)(2,1)S(1)}, bf16[3,128,1024]{2,1,0:T(8,128)(2,1)S(1)}, u32[]{:S(2)}, u32[]{:S(2)}) collective-permute-start(bf16[3,128,1024]{2,1,0:T(8,128)(2,1)S(1)} %collective-permute-done.7.refs_7_.refs_12_), channel_id=1, source_target_pairs={{0,2},{1,3},{2,4},{3,5},{4,6},{5,7},{6,0},{7,1},{8,10},{9,11},{10,... | collective-permute-start | bytes 2359304 | tf_op jit(solution)/shard_map/ppermute | solution.py:767
  85.1 28.7 %collective-permute-start.17 = (bf16[3,128,1024]{2,1,0:T(8,128)(2,1)S(1)}, bf16[3,128,1024]{2,1,0:T(8,128)(2,1)}, u32[]{:S(2)}, u32[]{:S(2)}) collective-permute-start(bf16[3,128,1024]{2,1,0:T(8,128)(2,1)S(1)} %collective-permute-done.7.refs_7_.refs_12_), channel_id=1, source_target_pairs={{0,1},{1,0},{2,3},{3,2},{4,5},{5,4},{6,7},{7,6},{8,9},{9,8},{10,11... | collective-permute-start | bytes 2359304 | tf_op jit(solution)/shard_map/ppermute | solution.py:763
  101.6 12.2 %collective-permute-start.16 = (bf16[3,128,1024]{2,1,0:T(8,128)(2,1)S(1)}, bf16[3,128,1024]{2,1,0:T(8,128)(2,1)}, u32[]{:S(2)}, u32[]{:S(2)}) collective-permute-start(bf16[3,128,1024]{2,1,0:T(8,128)(2,1)S(1)} %fusion.refs_6_.refs_11_), channel_id=1, source_target_pairs={{0,1},{1,0},{2,3},{3,2},{4,5},{5,4},{6,7},{7,6},{8,9},{9,8},{10,11... | collective-permute-start | bytes 2359304 | tf_op jit(solution)/shard_map/ppermute | solution.py:763
  123.8 301.7 %reduce-scatter.5.cloned.1.call-start = ((), (), s32[]{:S(2)}) async-start(), calls=%async_computation.5 | async-start | bytes 4866048 | tf_op jit(solution)/shard_map/reduce_scatter | solution.py:934
  124.4 12.2 %collective-permute-start.20 = (bf16[192,1024]{1,0:T(8,128)(2,1)}, bf16[192,1024]{1,0:T(8,128)(2,1)S(1)}, u32[]{:S(2)}, u32[]{:S(2)}) collective-permute-start(bf16[192,1024]{1,0:T(8,128)(2,1)} %get-tuple-element.262.refs_7_), channel_id=1, source_target_pairs={{0,8},{8,0},{16,24},{24,16},{1,9},{9,1},{17,25},{25,17},{2,10},{10... | collective-permute-start | bytes 1179656 | tf_op jit(solution)/shard_map/ppermute | solution.py:748
  125.8 15.4 %collective-permute-start.21 = (bf16[192,1024]{1,0:T(8,128)(2,1)}, bf16[192,1024]{1,0:T(8,128)(2,1)S(1)}, u32[]{:S(2)}, u32[]{:S(2)}) collective-permute-start(bf16[192,1024]{1,0:T(8,128)(2,1)} %get-tuple-element.263.refs_8_), channel_id=1, source_target_pairs={{0,16},{8,24},{16,0},{24,8},{1,17},{9,25},{17,1},{25,9},{2,18},{10... | collective-permute-start | bytes 1179656 | tf_op jit(solution)/shard_map/ppermute | solution.py:748
  125.9 20.2 %collective-permute-start.22 = (bf16[192,1024]{1,0:T(8,128)(2,1)}, bf16[192,1024]{1,0:T(8,128)(2,1)S(1)}, u32[]{:S(2)}, u32[]{:S(2)}) collective-permute-start(bf16[192,1024]{1,0:T(8,128)(2,1)} %get-tuple-element.264.refs_9_), channel_id=1, source_target_pairs={{0,24},{8,16},{16,8},{24,0},{1,25},{9,17},{17,9},{25,1},{2,26},{10... | collective-permute-start | bytes 1179656 | tf_op jit(solution)/shard_map/ppermute | solution.py:748
  146.1 31.5 %collective-permute-start.23 = (bf16[192,1024]{1,0:T(8,128)(2,1)}, bf16[192,1024]{1,0:T(8,128)(2,1)S(1)}, u32[]{:S(2)}, u32[]{:S(2)}) collective-permute-start(bf16[192,1024]{1,0:T(8,128)(2,1)} %get-tuple-element.277.refs_7_), channel_id=1, source_target_pairs={{0,8},{8,0},{16,24},{24,16},{1,9},{9,1},{17,25},{25,17},{2,10},{10... | collective-permute-start | bytes 1179656 | tf_op jit(solution)/shard_map/ppermute | solution.py:748
  147.1 30.5 %collective-permute-start.24 = (bf16[192,1024]{1,0:T(8,128)(2,1)}, bf16[192,1024]{1,0:T(8,128)(2,1)S(1)}, u32[]{:S(2)}, u32[]{:S(2)}) collective-permute-start(bf16[192,1024]{1,0:T(8,128)(2,1)} %get-tuple-element.278.refs_8_), channel_id=1, source_target_pairs={{0,16},{8,24},{16,0},{24,8},{1,17},{9,25},{17,1},{25,9},{2,18},{10... | collective-permute-start | bytes 1179656 | tf_op jit(solution)/shard_map/ppermute | solution.py:748
  148.1 29.5 %collective-permute-start.25 = (bf16[192,1024]{1,0:T(8,128)(2,1)}, bf16[192,1024]{1,0:T(8,128)(2,1)S(1)}, u32[]{:S(2)}, u32[]{:S(2)}) collective-permute-start(bf16[192,1024]{1,0:T(8,128)(2,1)} %get-tuple-element.279.refs_9_), channel_id=1, source_target_pairs={{0,24},{8,16},{16,8},{24,0},{1,25},{9,17},{17,9},{25,1},{2,26},{10... | collective-permute-start | bytes 1179656 | tf_op jit(solution)/shard_map/ppermute | solution.py:748
  208.6 223.4 %reduce-scatter.3.cloned.1.call-start = ((), (), s32[]{:S(2)}) async-start(), calls=%async_computation.4 | async-start | bytes 7077888 | tf_op jit(solution)/shard_map/reduce_scatter | solution.py:957
  239.1 38.6 %collective-permute-start.26 = (bf16[192,1024]{1,0:T(8,128)(2,1)}, bf16[192,1024]{1,0:T(8,128)(2,1)S(1)}, u32[]{:S(2)}, u32[]{:S(2)}) collective-permute-start(bf16[192,1024]{1,0:T(8,128)(2,1)} %get-tuple-element.307), channel_id=1, source_target_pairs={{0,8},{8,0},{16,24},{24,16},{1,9},{9,1},{17,25},{25,17},{2,10},{10... | collective-permute-start | bytes 1179656 | tf_op jit(solution)/shard_map/ppermute | solution.py:748
  239.9 37.9 %collective-permute-start.27 = (bf16[192,1024]{1,0:T(8,128)(2,1)}, bf16[192,1024]{1,0:T(8,128)(2,1)S(1)}, u32[]{:S(2)}, u32[]{:S(2)}) collective-permute-start(bf16[192,1024]{1,0:T(8,128)(2,1)} %get-tuple-element.308), channel_id=1, source_target_pairs={{0,16},{8,24},{16,0},{24,8},{1,17},{9,25},{17,1},{25,9},{2,18},{10... | collective-permute-start | bytes 1179656 | tf_op jit(solution)/shard_map/ppermute | solution.py:748
  240.9 36.8 %collective-permute-start.28 = (bf16[192,1024]{1,0:T(8,128)(2,1)}, bf16[192,1024]{1,0:T(8,128)(2,1)S(1)}, u32[]{:S(2)}, u32[]{:S(2)}) collective-permute-start(bf16[192,1024]{1,0:T(8,128)(2,1)} %get-tuple-element.309), channel_id=1, source_target_pairs={{0,24},{8,16},{16,8},{24,0},{1,25},{9,17},{17,9},{25,1},{2,26},{10... | collective-permute-start | bytes 1179656 | tf_op jit(solution)/shard_map/ppermute | solution.py:748
  277.8 13.2 %collective-permute-start.29 = (bf16[192,1024]{1,0:T(8,128)(2,1)}, bf16[192,1024]{1,0:T(8,128)(2,1)S(1)}, u32[]{:S(2)}, u32[]{:S(2)}) collective-permute-start(bf16[192,1024]{1,0:T(8,128)(2,1)} %get-tuple-element.346), channel_id=1, source_target_pairs={{0,8},{8,0},{16,24},{24,16},{1,9},{9,1},{17,25},{25,17},{2,10},{10... | collective-permute-start | bytes 1179656 | tf_op jit(solution)/shard_map/ppermute | solution.py:748
  278.5 16.5 %collective-permute-start.30 = (bf16[192,1024]{1,0:T(8,128)(2,1)}, bf16[192,1024]{1,0:T(8,128)(2,1)S(1)}, u32[]{:S(2)}, u32[]{:S(2)}) collective-permute-start(bf16[192,1024]{1,0:T(8,128)(2,1)} %get-tuple-element.347), channel_id=1, source_target_pairs={{0,16},{8,24},{16,0},{24,8},{1,17},{9,25},{17,1},{25,9},{2,18},{10... | collective-permute-start | bytes 1179656 | tf_op jit(solution)/shard_map/ppermute | solution.py:748
  279.6 20.8 %collective-permute-start.31 = (bf16[192,1024]{1,0:T(8,128)(2,1)}, bf16[192,1024]{1,0:T(8,128)(2,1)S(1)}, u32[]{:S(2)}, u32[]{:S(2)}) collective-permute-start(bf16[192,1024]{1,0:T(8,128)(2,1)} %get-tuple-element.348), channel_id=1, source_target_pairs={{0,24},{8,16},{16,8},{24,0},{1,25},{9,17},{17,9},{25,1},{2,26},{10... | collective-permute-start | bytes 1179656 | tf_op jit(solution)/shard_map/ppermute | solution.py:748
  289.2 30.1 %collective-permute-start.32 = (bf16[192,1024]{1,0:T(8,128)(2,1)}, bf16[192,1024]{1,0:T(8,128)(2,1)S(1)}, u32[]{:S(2)}, u32[]{:S(2)}) collective-permute-start(bf16[192,1024]{1,0:T(8,128)(2,1)} %get-tuple-element.367), channel_id=1, source_target_pairs={{0,8},{8,0},{16,24},{24,16},{1,9},{9,1},{17,25},{25,17},{2,10},{10... | collective-permute-start | bytes 1179656 | tf_op jit(solution)/shard_map/ppermute | solution.py:748
  289.9 29.4 %collective-permute-start.33 = (bf16[192,1024]{1,0:T(8,128)(2,1)}, bf16[192,1024]{1,0:T(8,128)(2,1)S(1)}, u32[]{:S(2)}, u32[]{:S(2)}) collective-permute-start(bf16[192,1024]{1,0:T(8,128)(2,1)} %get-tuple-element.368), channel_id=1, source_target_pairs={{0,16},{8,24},{16,0},{24,8},{1,17},{9,25},{17,1},{25,9},{2,18},{10... | collective-permute-start | bytes 1179656 | tf_op jit(solution)/shard_map/ppermute | solution.py:748
  291.0 28.3 %collective-permute-start.34 = (bf16[192,1024]{1,0:T(8,128)(2,1)}, bf16[192,1024]{1,0:T(8,128)(2,1)S(1)}, u32[]{:S(2)}, u32[]{:S(2)}) collective-permute-start(bf16[192,1024]{1,0:T(8,128)(2,1)} %get-tuple-element.369), channel_id=1, source_target_pairs={{0,24},{8,16},{16,8},{24,0},{1,25},{9,17},{17,9},{25,1},{2,26},{10... | collective-permute-start | bytes 1179656 | tf_op jit(solution)/shard_map/ppermute | solution.py:748
  320.3 21.3 %collective-permute-start.38 = (bf16[16,48,1536]{2,1,0:T(8,128)(2,1)}, bf16[16,48,1536]{2,1,0:T(8,128)(2,1)S(1)}, u32[]{:S(2)}, u32[]{:S(2)}) collective-permute-start(bf16[16,48,1536]{2,1,0:T(8,128)(2,1)} %get-tuple-element.391), channel_id=1, source_target_pairs={{0,1},{1,0},{2,3},{3,2},{4,5},{5,4},{6,7},{7,6},{8,9},{9,8},{10,11... | collective-permute-start | bytes 7077896 | tf_op jit(solution)/shard_map/ppermute | solution.py:763
  320.3 21.3 %collective-permute-start.39 = (bf16[16,48,512]{2,1,0:T(8,128)(2,1)}, bf16[16,48,512]{2,1,0:T(8,128)(2,1)S(1)}, u32[]{:S(2)}, u32[]{:S(2)}) collective-permute-start(bf16[16,48,512]{2,1,0:T(8,128)(2,1)} %get-tuple-element.392), channel_id=1, source_target_pairs={{0,1},{1,0},{2,3},{3,2},{4,5},{5,4},{6,7},{7,6},{8,9},{9,8},{10,11... | collective-permute-start | bytes 2359304 | tf_op jit(solution)/shard_map/ppermute | solution.py:763
  320.8 12.8 %collective-permute-start.35 = (bf16[192,1024]{1,0:T(8,128)(2,1)}, bf16[192,1024]{1,0:T(8,128)(2,1)S(1)}, u32[]{:S(2)}, u32[]{:S(2)}) collective-permute-start(bf16[192,1024]{1,0:T(8,128)(2,1)} %get-tuple-element.387), channel_id=1, source_target_pairs={{0,8},{8,0},{16,24},{24,16},{1,9},{9,1},{17,25},{25,17},{2,10},{10... | collective-permute-start | bytes 1179656 | tf_op jit(solution)/shard_map/ppermute | solution.py:748
  322.2 18.0 %collective-permute-start.36 = (bf16[192,1024]{1,0:T(8,128)(2,1)}, bf16[192,1024]{1,0:T(8,128)(2,1)S(1)}, u32[]{:S(2)}, u32[]{:S(2)}) collective-permute-start(bf16[192,1024]{1,0:T(8,128)(2,1)} %get-tuple-element.388), channel_id=1, source_target_pairs={{0,16},{8,24},{16,0},{24,8},{1,17},{9,25},{17,1},{25,9},{2,18},{10... | collective-permute-start | bytes 1179656 | tf_op jit(solution)/shard_map/ppermute | solution.py:748
  323.2 18.4 %collective-permute-start.37 = (bf16[192,1024]{1,0:T(8,128)(2,1)}, bf16[192,1024]{1,0:T(8,128)(2,1)S(1)}, u32[]{:S(2)}, u32[]{:S(2)}) collective-permute-start(bf16[192,1024]{1,0:T(8,128)(2,1)} %get-tuple-element.389), channel_id=1, source_target_pairs={{0,24},{8,16},{16,8},{24,0},{1,25},{9,17},{17,9},{25,1},{2,26},{10... | collective-permute-start | bytes 1179656 | tf_op jit(solution)/shard_map/ppermute | solution.py:748
  345.0 18.7 %collective-permute-start.40 = (bf16[4,48,2048]{2,1,0:T(8,128)(2,1)S(1)}, bf16[4,48,2048]{2,1,0:T(8,128)(2,1)S(1)}, u32[]{:S(2)}, u32[]{:S(2)}) collective-permute-start(bf16[4,48,2048]{2,1,0:T(8,128)(2,1)S(1)} %pad_maximum_fusion), channel_id=1, source_target_pairs={{0,8},{8,0},{16,24},{24,16},{1,9},{9,1},{17,25},{25,17},{2,10},{10... | collective-permute-start | bytes 2359304 | tf_op jit(solution)/shard_map/ppermute | solution.py:770
  345.8 18.4 %collective-permute-start.41 = (bf16[4,48,2048]{2,1,0:T(8,128)(2,1)S(1)}, bf16[4,48,2048]{2,1,0:T(8,128)(2,1)S(1)}, u32[]{:S(2)}, u32[]{:S(2)}) collective-permute-start(bf16[4,48,2048]{2,1,0:T(8,128)(2,1)S(1)} %pad_maximum_fusion.1), channel_id=1, source_target_pairs={{0,16},{8,24},{16,0},{24,8},{1,17},{9,25},{17,1},{25,9},{2,18},{10... | collective-permute-start | bytes 2359304 | tf_op jit(solution)/shard_map/ppermute | solution.py:770
  365.0 20.2 %collective-permute-start.43 = (bf16[4,48,2048]{2,1,0:T(8,128)(2,1)S(1)}, bf16[4,48,2048]{2,1,0:T(8,128)(2,1)}, u32[]{:S(2)}, u32[]{:S(2)}) collective-permute-start(bf16[4,48,2048]{2,1,0:T(8,128)(2,1)S(1)} %pad_maximum_fusion.2), channel_id=1, source_target_pairs={{0,24},{8,16},{16,8},{24,0},{1,25},{9,17},{17,9},{25,1},{2,26},{10... | collective-permute-start | bytes 2359304 | tf_op jit(solution)/shard_map/ppermute | solution.py:770
  385.3 14.9 %collective-permute-start.44 = (bf16[4,48,512]{2,1,0:T(8,128)(2,1)S(1)}, bf16[4,48,512]{2,1,0:T(8,128)(2,1)S(1)}, u32[]{:S(2)}, u32[]{:S(2)}) collective-permute-start(bf16[4,48,512]{2,1,0:T(8,128)(2,1)S(1)} %get-tuple-element.420), channel_id=1, source_target_pairs={{0,8},{8,0},{16,24},{24,16},{1,9},{9,1},{17,25},{25,17},{2,10},{10... | collective-permute-start | bytes 589832 | tf_op jit(solution)/shard_map/ppermute | solution.py:770
  386.6 14.3 %collective-permute-start.45 = (bf16[4,48,512]{2,1,0:T(8,128)(2,1)S(1)}, bf16[4,48,512]{2,1,0:T(8,128)(2,1)S(1)}, u32[]{:S(2)}, u32[]{:S(2)}) collective-permute-start(bf16[4,48,512]{2,1,0:T(8,128)(2,1)S(1)} %get-tuple-element.421), channel_id=1, source_target_pairs={{0,16},{8,24},{16,0},{24,8},{1,17},{9,25},{17,1},{25,9},{2,18},{10... | collective-permute-start | bytes 589832 | tf_op jit(solution)/shard_map/ppermute | solution.py:770
  387.0 13.9 %collective-permute-start.46 = (bf16[4,48,512]{2,1,0:T(8,128)(2,1)S(1)}, bf16[4,48,512]{2,1,0:T(8,128)(2,1)S(1)}, u32[]{:S(2)}, u32[]{:S(2)}) collective-permute-start(bf16[4,48,512]{2,1,0:T(8,128)(2,1)S(1)} %get-tuple-element.422), channel_id=1, source_target_pairs={{0,24},{8,16},{16,8},{24,0},{1,25},{9,17},{17,9},{25,1},{2,26},{10... | collective-permute-start | bytes 589832 | tf_op jit(solution)/shard_map/ppermute | solution.py:770
  390.2 16.8 %collective-permute-start.49 = (bf16[48,2048]{1,0:T(8,128)(2,1)S(1)}, bf16[48,2048]{1,0:T(8,128)(2,1)S(1)}, u32[]{:S(2)}, u32[]{:S(2)}) collective-permute-start(bf16[48,2048]{1,0:T(8,128)(2,1)S(1)} %get-tuple-element.445), channel_id=1, source_target_pairs={{0,6},{1,7},{2,4},{3,5},{4,2},{5,3},{6,0},{7,1},{8,14},{9,15},{10,... | collective-permute-start | bytes 589832 | tf_op jit(solution)/shard_map/ppermute | solution.py:773
  400.2 9.3 %collective-permute-start.47 = (bf16[48,2048]{1,0:T(8,128)(2,1)S(1)}, bf16[48,2048]{1,0:T(8,128)(2,1)S(1)}, u32[]{:S(2)}, u32[]{:S(2)}) collective-permute-start(bf16[48,2048]{1,0:T(8,128)(2,1)S(1)} %get-tuple-element.446), channel_id=1, source_target_pairs={{0,2},{1,3},{2,0},{3,1},{4,6},{5,7},{6,4},{7,5},{8,10},{9,11},{10,... | collective-permute-start | bytes 589832 | tf_op jit(solution)/shard_map/ppermute | solution.py:773
  400.2 18.0 %collective-permute-start.48 = (bf16[48,2048]{1,0:T(8,128)(2,1)S(1)}, bf16[48,2048]{1,0:T(8,128)(2,1)S(1)}, u32[]{:S(2)}, u32[]{:S(2)}) collective-permute-start(bf16[48,2048]{1,0:T(8,128)(2,1)S(1)} %get-tuple-element.447), channel_id=1, source_target_pairs={{0,4},{1,5},{2,6},{3,7},{4,0},{5,1},{6,2},{7,3},{8,12},{9,13},{10,... | collective-permute-start | bytes 589832 | tf_op jit(solution)/shard_map/ppermute | solution.py:773
  419.5 15.2 %collective-permute-start.50 = (bf16[48,512]{1,0:T(8,128)(2,1)S(1)}, bf16[48,512]{1,0:T(8,128)(2,1)S(1)}, u32[]{:S(2)}, u32[]{:S(2)}) collective-permute-start(bf16[48,512]{1,0:T(8,128)(2,1)S(1)} %get-tuple-element.428), channel_id=1, source_target_pairs={{0,2},{1,3},{2,0},{3,1},{4,6},{5,7},{6,4},{7,5},{8,10},{9,11},{10,... | collective-permute-start | bytes 147464 | tf_op jit(solution)/shard_map/ppermute | solution.py:773
  419.6 15.1 %collective-permute-start.51 = (bf16[48,512]{1,0:T(8,128)(2,1)S(1)}, bf16[48,512]{1,0:T(8,128)(2,1)S(1)}, u32[]{:S(2)}, u32[]{:S(2)}) collective-permute-start(bf16[48,512]{1,0:T(8,128)(2,1)S(1)} %get-tuple-element.429), channel_id=1, source_target_pairs={{0,4},{1,5},{2,6},{3,7},{4,0},{5,1},{6,2},{7,3},{8,12},{9,13},{10,... | collective-permute-start | bytes 147464 | tf_op jit(solution)/shard_map/ppermute | solution.py:773
  421.1 13.5 %collective-permute-start.52 = (bf16[48,512]{1,0:T(8,128)(2,1)S(1)}, bf16[48,512]{1,0:T(8,128)(2,1)S(1)}, u32[]{:S(2)}, u32[]{:S(2)}) collective-permute-start(bf16[48,512]{1,0:T(8,128)(2,1)S(1)} %get-tuple-element.430), channel_id=1, source_target_pairs={{0,6},{1,7},{2,4},{3,5},{4,2},{5,3},{6,0},{7,1},{8,14},{9,15},{10,... | collective-permute-start | bytes 147464 | tf_op jit(solution)/shard_map/ppermute | solution.py:773
  (57 other events, 508.4 us)
Sparse Core Ops, SparseCore 0:
  22.2 102.2 all-gather.4
  127.6 75.6 all-gather.2
  208.8 122.9 reduce-scatter.4
  334.0 70.3 reduce-scatter.2
